TPU v7x, 32 devices: a whole 2x2x4 slice. The times are simulated.
32 devices in a mesh: gx: 16 (over z, y, core), gy: 2 (over x).
Axes of the slice: x: 2, y: 2, z: 4, core: 2. Of those that a mesh axis runs over, the one named last changes fastest.
Arguments:
- pressure_prev: float32 [128, 64, 256], P('gx', 'gy'), may hold values from -6 to 6
- pressure_now: float32 [128, 64, 256], P('gx', 'gy'), may hold values from -6 to 6
- courant: float32 [128, 64, 256], P('gx', 'gy'), may hold values from 0.05 to 0.18
- perturbation: float32 [128, 64, 256], P('gx', 'gy'), may hold values from 0.005 to 0.04
- source_pos: int32 [3], replicated, may hold values from 0 to 63
- wavelet: float32 [8], replicated, may hold values from -8 to 8
- rec_cells: int32 [16, 2, 128], P('gx', 'gy'), may hold values from 0 to 65535
- observed: float32 [16, 2, 8, 128], P('gx', 'gy'), may hold values from -20 to 20
Outputs:
- pressure: float32 [128, 64, 256], P('gx', 'gy')
- tangent: float32 [128, 64, 256], P('gx', 'gy')
- predicted: float32 [16, 2, 8, 128], P('gx', 'gy')
- updated_model: float32 [128, 64, 256], P('gx', 'gy')
Inputs may be any that keep to these rules, and one draw needn't show every extreme that they name: `rec_cells`: indices of cells inside the device's own block. `source_pos`: A cell inside the grid.
All inputs are finite; a program needn't handle non-finite values.
Results may differ from a plain program's by a relative error of at most 0.00002.
Values sent between devices are 32-bit elements; how exact they have to be, the bound alone decides.
No kernel may reach another device: no remote copies, remote signals or barrier semaphores. Data moves between devices by JAX's collectives and lax.ppermute only.
A program may use at most 64 MiB of HBM per device.

v0:
```python
import jax
import jax.numpy as jnp
from jax import lax
from jax.sharding import PartitionSpec as P

COEF = (-205.0 / 72.0, 8.0 / 5.0, -1.0 / 5.0, 8.0 / 315.0, -1.0 / 560.0)


def padded_2(value, sides, width):
    for axis, dim in sides:
        count, length = (lax.axis_size(axis), value.shape[dim])
        up = [(i, (i + 1) % count) for i in range(count - 1)]
        down = [(j, i) for i, j in up]
        last = lax.slice_in_dim(value, length - width, length, axis=dim)
        initial = lax.slice_in_dim(value, 0, width, axis=dim)
        before = lax.ppermute(last, axis, up)
        after = lax.ppermute(initial, axis, down)
        value = jnp.concatenate([before, value, after], axis=dim)
    return value


def laplace(padded):
    size_x = padded.shape[-3] - 8
    size_y = padded.shape[-2] - 8
    size_z = padded.shape[-1] - 8

    def part(off_x, off_y, off_z):
        return padded[..., off_x : off_x + size_x, off_y : off_y + size_y, off_z : off_z + size_z]

    total = 3.0 * COEF[0] * part(4, 4, 4)
    for k in range(1, 5):
        total = total + COEF[k] * (
            part(4 + k, 4, 4)
            + part(4 - k, 4, 4)
            + part(4, 4 + k, 4)
            + part(4, 4 - k, 4)
            + part(4, 4, 4 + k)
            + part(4, 4, 4 - k)
        )
    return total


def blur(field, axis):
    count = field.shape[axis] - 2
    return (
        0.25 * lax.slice_in_dim(field, 0, count, axis=axis)
        + 0.5 * lax.slice_in_dim(field, 1, 1 + count, axis=axis)
        + 0.25 * lax.slice_in_dim(field, 2, 2 + count, axis=axis)
    )


def pad_depth(field, width):
    spec = [(0, 0)] * (field.ndim - 1) + [(width, width)]
    return jnp.pad(field, spec)


def source_mask(size_x, size_y, size_z, start_x, start_y, source_pos):
    cells_x = start_x + jnp.arange(size_x, dtype=jnp.int32)
    cells_y = start_y + jnp.arange(size_y, dtype=jnp.int32)
    cells_z = jnp.arange(size_z, dtype=jnp.int32)
    hit = (
        (cells_x == source_pos[0])[:, None, None]
        & (cells_y == source_pos[1])[None, :, None]
        & (cells_z == source_pos[2])[None, None, :]
    )
    return hit.astype(jnp.float32)


def on_device(
    pressure_prev, pressure_now, courant, perturbation, source_pos, wavelet, rec_cells, observed
):
    size_x, size_y, size_z = pressure_now.shape
    steps = wavelet.shape[0]
    start_x = lax.axis_index("gx") * size_x
    start_y = lax.axis_index("gy") * size_y
    indices = rec_cells.reshape(-1)
    p_old, p_cur = (pressure_prev, pressure_now)
    q_old = jnp.zeros_like(p_cur)
    q_cur = jnp.zeros_like(p_cur)
    synth_list = []
    born_list = []
    mask = source_mask(size_x, size_y, size_z, start_x, start_y, source_pos)
    for step in range(steps):
        lap_p = laplace(pad_depth(padded_2(p_cur, (("gx", 0), ("gy", 1)), 4), 4))
        lap_q = laplace(pad_depth(padded_2(q_cur, (("gx", 0), ("gy", 1)), 4), 4))
        p_new = 2.0 * p_cur - p_old + courant * lap_p + wavelet[step] * mask
        q_new = 2.0 * q_cur - q_old + courant * lap_q + perturbation * lap_p
        synth_list.append(jnp.take(p_new.reshape(-1), indices))
        born_list.append(jnp.take(q_new.reshape(-1), indices))
        p_old, p_cur, q_old, q_cur = (p_cur, p_new, q_cur, q_new)
    rim = padded_2(perturbation, (("gx", 0), ("gy", 1)), 1)
    synthetic = jnp.stack(synth_list, axis=0).reshape(observed.shape)
    born = jnp.stack(born_list, axis=0).reshape(observed.shape)
    residual = observed - synthetic
    numer, denom = lax.psum((jnp.sum(residual * born), jnp.sum(born * born)), ("gx", "gy"))
    step_len = numer / (denom + 1e-06)
    predicted = residual - step_len * born
    smooth = pad_depth(rim, 1)
    for axis in range(3):
        smooth = blur(smooth, axis)
    updated_model = courant + step_len * smooth
    return (p_cur, q_cur, predicted, updated_model)


def solution(mesh):
    placed = (
        P("gx", "gy", None),
        P("gx", "gy", None),
        P("gx", "gy", None),
        P("gx", "gy", None),
        P(),
        P(),
        P("gx", "gy", None),
        P("gx", "gy", None, None),
    )
    return jax.shard_map(
        on_device,
        mesh=mesh,
        in_specs=placed,
        out_specs=(
            P("gx", "gy", None),
            P("gx", "gy", None),
            P("gx", "gy", None, None),
            P("gx", "gy", None),
        ),
        check_vma=False,
    )
```

profile of v0, /device:TPU:0, one launch (start us, length us, event | category | flops | bytes accessed | tf_op | source)
XLA Modules:
  0.0 326.7 jit_solution(2136785582295416012)
XLA Ops:
  0.7 2.5 collective-permute-start.33
  6.5 5.8 %collective-permute-start.64 = (f32[1,32,256]{2,1,0:T(8,128)S(1)}, f32[1,32,256]{2,1,0:T(8,128)S(1)}, u32[]{:S(2)}, u32[]{:S(2)}) collective-permute-start(f32[1,32,256]{2,1,0:T(8,128)S(1)} %get-tuple-element.90), channel_id=1, source_target_pairs={{0,2},{2,4},{4,6},{6,8},{8,10},{10,12},{12,14},{14,16},{16,18},{18... | collective-permute-start | bytes 98312 | tf_op jit(solution)/shard_map/ppermute | solution.py:16
  12.4 3.6 %collective-permute-start.1 = (f32[4,32,256]{2,1,0:T(8,128)S(1)}, f32[4,32,256]{2,1,0:T(8,128)S(1)}, u32[]{:S(2)}, u32[]{:S(2)}) collective-permute-start(f32[4,32,256]{2,1,0:T(8,128)S(1)} %get-tuple-element.123), channel_id=1, source_target_pairs={{0,2},{2,4},{4,6},{6,8},{8,10},{10,12},{12,14},{14,16},{16,18},{18... | collective-permute-start | bytes 393224 | tf_op jit(solution)/shard_map/ppermute | solution.py:16
  22.0 3.4 %collective-permute-start.35 = (f32[16,4,256]{2,1,0:T(4,128)S(1)}, f32[16,4,256]{2,1,0:T(4,128)S(1)}, u32[]{:S(2)}, u32[]{:S(2)}) collective-permute-start(f32[16,4,256]{2,1,0:T(4,128)S(1)} %get-tuple-element.85), channel_id=1, source_target_pairs={{0,1},{2,3},{4,5},{6,7},{8,9},{10,11},{12,13},{14,15},{16,17},{18,... | collective-permute-start | bytes 196616 | tf_op jit(solution)/shard_map/ppermute | solution.py:16
  26.9 4.5 %collective-permute-start.3 = (f32[16,4,256]{2,1,0:T(4,128)S(1)}, f32[16,4,256]{2,1,0:T(4,128)S(1)}, u32[]{:S(2)}, u32[]{:S(2)}) collective-permute-start(f32[16,4,256]{2,1,0:T(4,128)S(1)} %get-tuple-element.81), channel_id=1, source_target_pairs={{0,1},{2,3},{4,5},{6,7},{8,9},{10,11},{12,13},{14,15},{16,17},{18,... | collective-permute-start | bytes 196616 | tf_op jit(solution)/shard_map/ppermute | solution.py:16
  33.5 4.1 %collective-permute-done.2 = f32[16,4,256]{2,1,0:T(4,128)S(1)} collective-permute-done((f32[16,4,256]{2,1,0:T(4,128)S(1)}, f32[16,4,256]{2,1,0:T(4,128)S(1)}, u32[]{:S(2)}, u32[]{:S(2)}) %collective-permute-start.2) | collective-permute-done | bytes 65568 | tf_op jit(solution)/shard_map/ppermute | solution.py:17
  44.2 6.8 %collective-permute-start.37 = (f32[4,32,256]{2,1,0:T(8,128)S(1)}, f32[4,32,256]{2,1,0:T(8,128)S(1)}, u32[]{:S(2)}, u32[]{:S(2)}) collective-permute-start(f32[4,32,256]{2,1,0:T(8,128)S(1)} %get-tuple-element.118), channel_id=1, source_target_pairs={{0,2},{2,4},{4,6},{6,8},{8,10},{10,12},{12,14},{14,16},{16,18},{18... | collective-permute-start | bytes 393224 | tf_op jit(solution)/shard_map/ppermute | solution.py:16
  54.0 4.5 %collective-permute-start.39 = (f32[16,4,256]{2,1,0:T(4,128)S(1)}, f32[16,4,256]{2,1,0:T(4,128)S(1)}, u32[]{:S(2)}, u32[]{:S(2)}) collective-permute-start(f32[16,4,256]{2,1,0:T(4,128)S(1)} %get-tuple-element.79), channel_id=1, source_target_pairs={{0,1},{2,3},{4,5},{6,7},{8,9},{10,11},{12,13},{14,15},{16,17},{18,... | collective-permute-start | bytes 196616 | tf_op jit(solution)/shard_map/ppermute | solution.py:16
  60.8 4.5 %collective-permute-done.38 = f32[16,4,256]{2,1,0:T(4,128)S(1)} collective-permute-done((f32[16,4,256]{2,1,0:T(4,128)S(1)}, f32[16,4,256]{2,1,0:T(4,128)S(1)}, u32[]{:S(2)}, u32[]{:S(2)}) %collective-permute-start.38) | collective-permute-done | bytes 65568 | tf_op jit(solution)/shard_map/ppermute | solution.py:17
  72.5 5.6 %collective-permute-start.41 = (f32[4,32,256]{2,1,0:T(8,128)S(1)}, f32[4,32,256]{2,1,0:T(8,128)S(1)}, u32[]{:S(2)}, u32[]{:S(2)}) collective-permute-start(f32[4,32,256]{2,1,0:T(8,128)S(1)} %get-tuple-element.114), channel_id=1, source_target_pairs={{0,2},{2,4},{4,6},{6,8},{8,10},{10,12},{12,14},{14,16},{16,18},{18... | collective-permute-start | bytes 393224 | tf_op jit(solution)/shard_map/ppermute | solution.py:16
  81.2 4.5 %collective-permute-start.43 = (f32[16,4,256]{2,1,0:T(4,128)S(1)}, f32[16,4,256]{2,1,0:T(4,128)S(1)}, u32[]{:S(2)}, u32[]{:S(2)}) collective-permute-start(f32[16,4,256]{2,1,0:T(4,128)S(1)} %get-tuple-element.71), channel_id=1, source_target_pairs={{0,1},{2,3},{4,5},{6,7},{8,9},{10,11},{12,13},{14,15},{16,17},{18,... | collective-permute-start | bytes 196616 | tf_op jit(solution)/shard_map/ppermute | solution.py:16
  88.0 4.5 %collective-permute-done.42 = f32[16,4,256]{2,1,0:T(4,128)S(1)} collective-permute-done((f32[16,4,256]{2,1,0:T(4,128)S(1)}, f32[16,4,256]{2,1,0:T(4,128)S(1)}, u32[]{:S(2)}, u32[]{:S(2)}) %collective-permute-start.42) | collective-permute-done | bytes 65568 | tf_op jit(solution)/shard_map/ppermute | solution.py:17
  99.6 5.6 %collective-permute-start.45 = (f32[4,32,256]{2,1,0:T(8,128)S(1)}, f32[4,32,256]{2,1,0:T(8,128)S(1)}, u32[]{:S(2)}, u32[]{:S(2)}) collective-permute-start(f32[4,32,256]{2,1,0:T(8,128)S(1)} %get-tuple-element.110), channel_id=1, source_target_pairs={{0,2},{2,4},{4,6},{6,8},{8,10},{10,12},{12,14},{14,16},{16,18},{18... | collective-permute-start | bytes 393224 | tf_op jit(solution)/shard_map/ppermute | solution.py:16
  108.3 4.5 %collective-permute-start.47 = (f32[16,4,256]{2,1,0:T(4,128)S(1)}, f32[16,4,256]{2,1,0:T(4,128)S(1)}, u32[]{:S(2)}, u32[]{:S(2)}) collective-permute-start(f32[16,4,256]{2,1,0:T(4,128)S(1)} %get-tuple-element.63), channel_id=1, source_target_pairs={{0,1},{2,3},{4,5},{6,7},{8,9},{10,11},{12,13},{14,15},{16,17},{18,... | collective-permute-start | bytes 196616 | tf_op jit(solution)/shard_map/ppermute | solution.py:16
  115.1 4.5 %collective-permute-done.46 = f32[16,4,256]{2,1,0:T(4,128)S(1)} collective-permute-done((f32[16,4,256]{2,1,0:T(4,128)S(1)}, f32[16,4,256]{2,1,0:T(4,128)S(1)}, u32[]{:S(2)}, u32[]{:S(2)}) %collective-permute-start.46) | collective-permute-done | bytes 65568 | tf_op jit(solution)/shard_map/ppermute | solution.py:17
  126.7 5.6 %collective-permute-start.49 = (f32[4,32,256]{2,1,0:T(8,128)S(1)}, f32[4,32,256]{2,1,0:T(8,128)S(1)}, u32[]{:S(2)}, u32[]{:S(2)}) collective-permute-start(f32[4,32,256]{2,1,0:T(8,128)S(1)} %get-tuple-element.106), channel_id=1, source_target_pairs={{0,2},{2,4},{4,6},{6,8},{8,10},{10,12},{12,14},{14,16},{16,18},{18... | collective-permute-start | bytes 393224 | tf_op jit(solution)/shard_map/ppermute | solution.py:16
  135.3 4.5 %collective-permute-start.19 = (f32[16,4,256]{2,1,0:T(4,128)S(1)}, f32[16,4,256]{2,1,0:T(4,128)S(1)}, u32[]{:S(2)}, u32[]{:S(2)}) collective-permute-start(f32[16,4,256]{2,1,0:T(4,128)S(1)} %get-tuple-element.51), channel_id=1, source_target_pairs={{0,1},{2,3},{4,5},{6,7},{8,9},{10,11},{12,13},{14,15},{16,17},{18,... | collective-permute-start | bytes 196616 | tf_op jit(solution)/shard_map/ppermute | solution.py:16
  141.2 4.5 %collective-permute-start.51 = (f32[16,4,256]{2,1,0:T(4,128)S(1)}, f32[16,4,256]{2,1,0:T(4,128)S(1)}, u32[]{:S(2)}, u32[]{:S(2)}) collective-permute-start(f32[16,4,256]{2,1,0:T(4,128)S(1)} %get-tuple-element.55), channel_id=1, source_target_pairs={{0,1},{2,3},{4,5},{6,7},{8,9},{10,11},{12,13},{14,15},{16,17},{18,... | collective-permute-start | bytes 196616 | tf_op jit(solution)/shard_map/ppermute | solution.py:16
  147.9 4.1 %collective-permute-done.50 = f32[16,4,256]{2,1,0:T(4,128)S(1)} collective-permute-done((f32[16,4,256]{2,1,0:T(4,128)S(1)}, f32[16,4,256]{2,1,0:T(4,128)S(1)}, u32[]{:S(2)}, u32[]{:S(2)}) %collective-permute-start.50) | collective-permute-done | bytes 65568 | tf_op jit(solution)/shard_map/ppermute | solution.py:17
  158.6 7.1 %collective-permute-start.53 = (f32[4,32,256]{2,1,0:T(8,128)S(1)}, f32[4,32,256]{2,1,0:T(8,128)S(1)}, u32[]{:S(2)}, u32[]{:S(2)}) collective-permute-start(f32[4,32,256]{2,1,0:T(8,128)S(1)} %get-tuple-element.102), channel_id=1, source_target_pairs={{0,2},{2,4},{4,6},{6,8},{8,10},{10,12},{12,14},{14,16},{16,18},{18... | collective-permute-start | bytes 393224 | tf_op jit(solution)/shard_map/ppermute | solution.py:16
  168.9 4.5 %collective-permute-start.55 = (f32[16,4,256]{2,1,0:T(4,128)S(1)}, f32[16,4,256]{2,1,0:T(4,128)S(1)}, u32[]{:S(2)}, u32[]{:S(2)}) collective-permute-start(f32[16,4,256]{2,1,0:T(4,128)S(1)} %get-tuple-element.47), channel_id=1, source_target_pairs={{0,1},{2,3},{4,5},{6,7},{8,9},{10,11},{12,13},{14,15},{16,17},{18,... | collective-permute-start | bytes 196616 | tf_op jit(solution)/shard_map/ppermute | solution.py:16
  175.6 4.7 %collective-permute-done.54 = f32[16,4,256]{2,1,0:T(4,128)S(1)} collective-permute-done((f32[16,4,256]{2,1,0:T(4,128)S(1)}, f32[16,4,256]{2,1,0:T(4,128)S(1)}, u32[]{:S(2)}, u32[]{:S(2)}) %collective-permute-start.54) | collective-permute-done | bytes 65568 | tf_op jit(solution)/shard_map/ppermute | solution.py:17
  182.9 2.0 collective-permute-start.25
  187.6 5.2 %collective-permute-start.57 = (f32[4,32,256]{2,1,0:T(8,128)S(1)}, f32[4,32,256]{2,1,0:T(8,128)S(1)}, u32[]{:S(2)}, u32[]{:S(2)}) collective-permute-start(f32[4,32,256]{2,1,0:T(8,128)S(1)} %get-tuple-element.98), channel_id=1, source_target_pairs={{0,2},{2,4},{4,6},{6,8},{8,10},{10,12},{12,14},{14,16},{16,18},{18... | collective-permute-start | bytes 393224 | tf_op jit(solution)/shard_map/ppermute | solution.py:16
  195.9 4.5 %collective-permute-start.59 = (f32[16,4,256]{2,1,0:T(4,128)S(1)}, f32[16,4,256]{2,1,0:T(4,128)S(1)}, u32[]{:S(2)}, u32[]{:S(2)}) collective-permute-start(f32[16,4,256]{2,1,0:T(4,128)S(1)} %get-tuple-element.39), channel_id=1, source_target_pairs={{0,1},{2,3},{4,5},{6,7},{8,9},{10,11},{12,13},{14,15},{16,17},{18,... | collective-permute-start | bytes 196616 | tf_op jit(solution)/shard_map/ppermute | solution.py:16
  202.7 4.5 %collective-permute-done.58 = f32[16,4,256]{2,1,0:T(4,128)S(1)} collective-permute-done((f32[16,4,256]{2,1,0:T(4,128)S(1)}, f32[16,4,256]{2,1,0:T(4,128)S(1)}, u32[]{:S(2)}, u32[]{:S(2)}) %collective-permute-start.58) | collective-permute-done | bytes 65568 | tf_op jit(solution)/shard_map/ppermute | solution.py:17
  215.8 6.3 %collective-permute-start.61 = (f32[4,32,256]{2,1,0:T(8,128)}, f32[4,32,256]{2,1,0:T(8,128)}, u32[]{:S(2)}, u32[]{:S(2)}) collective-permute-start(f32[4,32,256]{2,1,0:T(8,128)} %get-tuple-element.94), channel_id=1, source_target_pairs={{0,2},{2,4},{4,6},{6,8},{8,10},{10,12},{12,14},{14,16},{16,18},{18... | collective-permute-start | bytes 393224 | tf_op jit(solution)/shard_map/ppermute | solution.py:16
  229.4 2.5 gather_fusion.9
  258.2 4.5 %collective-permute-start.63 = (f32[16,4,256]{2,1,0:T(4,128)S(1)}, f32[16,4,256]{2,1,0:T(4,128)S(1)}, u32[]{:S(2)}, u32[]{:S(2)}) collective-permute-start(f32[16,4,256]{2,1,0:T(4,128)S(1)} %get-tuple-element.31), channel_id=1, source_target_pairs={{0,1},{2,3},{4,5},{6,7},{8,9},{10,11},{12,13},{14,15},{16,17},{18,... | collective-permute-start | bytes 196616 | tf_op jit(solution)/shard_map/ppermute | solution.py:16
  266.8 2.1 collective-permute-done.62
  271.6 3.1 fusion.17
  281.8 42.1 %all-reduce.19 = (f32[]{:T(128)}, f32[]{:T(128)}) all-reduce(f32[]{:T(128)} %get-tuple-element.176, f32[]{:T(128)} %get-tuple-element.177), channel_id=1, replica_groups=mesh['gx'=16,'gy'=2] {'gx','gy'}, use_global_device_ids=true, to_apply=%region_1.3 | all-reduce | flops 2 | bytes 16 | tf_op jit(solution)/shard_map/psum | solution.py:95
  (300 shorter events, 141.4 us)
Async XLA Ops:
  0.7 19.9 %collective-permute-start.33 = (f32[4,32,256]{2,1,0:T(8,128)S(1)}, f32[4,32,256]{2,1,0:T(8,128)S(1)}, u32[]{:S(2)}, u32[]{:S(2)}) collective-permute-start(f32[4,32,256]{2,1,0:T(8,128)S(1)} %broadcast.143), channel_id=1, source_target_pairs={{0,2},{2,4},{4,6},{6,8},{8,10},{10,12},{12,14},{14,16},{16,18},{18... | collective-permute-start | bytes 393224 | tf_op jit(solution)/shard_map/ppermute | solution.py:16
  3.2 18.8 %collective-permute-start.32 = (f32[4,32,256]{2,1,0:T(8,128)S(1)}, f32[4,32,256]{2,1,0:T(8,128)S(1)}, u32[]{:S(2)}, u32[]{:S(2)}) collective-permute-start(f32[4,32,256]{2,1,0:T(8,128)S(1)} %broadcast.143), channel_id=1, source_target_pairs={{2,0},{4,2},{6,4},{8,6},{10,8},{12,10},{14,12},{16,14},{18,16},{20... | collective-permute-start | bytes 393224 | tf_op jit(solution)/shard_map/ppermute | solution.py:17
  5.2 100.0 %collective-permute-start.65 = (f32[1,32,256]{2,1,0:T(8,128)S(1)}, f32[1,32,256]{2,1,0:T(8,128)S(1)}, u32[]{:S(2)}, u32[]{:S(2)}) collective-permute-start(f32[1,32,256]{2,1,0:T(8,128)S(1)} %get-tuple-element.89), channel_id=1, source_target_pairs={{2,0},{4,2},{6,4},{8,6},{10,8},{12,10},{14,12},{16,14},{18,16},{20... | collective-permute-start | bytes 98312 | tf_op jit(solution)/shard_map/ppermute | solution.py:17
  6.5 37.6 %collective-permute-start.64 = (f32[1,32,256]{2,1,0:T(8,128)S(1)}, f32[1,32,256]{2,1,0:T(8,128)S(1)}, u32[]{:S(2)}, u32[]{:S(2)}) collective-permute-start(f32[1,32,256]{2,1,0:T(8,128)S(1)} %get-tuple-element.90), channel_id=1, source_target_pairs={{0,2},{2,4},{4,6},{6,8},{8,10},{10,12},{12,14},{14,16},{16,18},{18... | collective-permute-start | bytes 98312 | tf_op jit(solution)/shard_map/ppermute | solution.py:16
  12.4 13.0 %collective-permute-start.1 = (f32[4,32,256]{2,1,0:T(8,128)S(1)}, f32[4,32,256]{2,1,0:T(8,128)S(1)}, u32[]{:S(2)}, u32[]{:S(2)}) collective-permute-start(f32[4,32,256]{2,1,0:T(8,128)S(1)} %get-tuple-element.123), channel_id=1, source_target_pairs={{0,2},{2,4},{4,6},{6,8},{8,10},{10,12},{12,14},{14,16},{16,18},{18... | collective-permute-start | bytes 393224 | tf_op jit(solution)/shard_map/ppermute | solution.py:16
  22.0 9.5 %collective-permute-start.35 = (f32[16,4,256]{2,1,0:T(4,128)S(1)}, f32[16,4,256]{2,1,0:T(4,128)S(1)}, u32[]{:S(2)}, u32[]{:S(2)}) collective-permute-start(f32[16,4,256]{2,1,0:T(4,128)S(1)} %get-tuple-element.85), channel_id=1, source_target_pairs={{0,1},{2,3},{4,5},{6,7},{8,9},{10,11},{12,13},{14,15},{16,17},{18,... | collective-permute-start | bytes 196616 | tf_op jit(solution)/shard_map/ppermute | solution.py:16
  40.2 10.9 %collective-permute-start.5 = (f32[4,32,256]{2,1,0:T(8,128)S(1)}, f32[4,32,256]{2,1,0:T(8,128)S(1)}, u32[]{:S(2)}, u32[]{:S(2)}) collective-permute-start(f32[4,32,256]{2,1,0:T(8,128)S(1)} %get-tuple-element.115), channel_id=1, source_target_pairs={{0,2},{2,4},{4,6},{6,8},{8,10},{10,12},{12,14},{14,16},{16,18},{18... | collective-permute-start | bytes 393224 | tf_op jit(solution)/shard_map/ppermute | solution.py:16
  41.5 9.5 %collective-permute-start.4 = (f32[4,32,256]{2,1,0:T(8,128)S(1)}, f32[4,32,256]{2,1,0:T(8,128)S(1)}, u32[]{:S(2)}, u32[]{:S(2)}) collective-permute-start(f32[4,32,256]{2,1,0:T(8,128)S(1)} %get-tuple-element.116), channel_id=1, source_target_pairs={{2,0},{4,2},{6,4},{8,6},{10,8},{12,10},{14,12},{16,14},{18,16},{20... | collective-permute-start | bytes 393224 | tf_op jit(solution)/shard_map/ppermute | solution.py:17
  42.9 11.1 %collective-permute-start.36 = (f32[4,32,256]{2,1,0:T(8,128)S(1)}, f32[4,32,256]{2,1,0:T(8,128)S(1)}, u32[]{:S(2)}, u32[]{:S(2)}) collective-permute-start(f32[4,32,256]{2,1,0:T(8,128)S(1)} %get-tuple-element.117), channel_id=1, source_target_pairs={{2,0},{4,2},{6,4},{8,6},{10,8},{12,10},{14,12},{16,14},{18,16},{20... | collective-permute-start | bytes 393224 | tf_op jit(solution)/shard_map/ppermute | solution.py:17
  44.2 9.8 %collective-permute-start.37 = (f32[4,32,256]{2,1,0:T(8,128)S(1)}, f32[4,32,256]{2,1,0:T(8,128)S(1)}, u32[]{:S(2)}, u32[]{:S(2)}) collective-permute-start(f32[4,32,256]{2,1,0:T(8,128)S(1)} %get-tuple-element.118), channel_id=1, source_target_pairs={{0,2},{2,4},{4,6},{6,8},{8,10},{10,12},{12,14},{14,16},{16,18},{18... | collective-permute-start | bytes 393224 | tf_op jit(solution)/shard_map/ppermute | solution.py:16
  67.9 10.3 %collective-permute-start.9 = (f32[4,32,256]{2,1,0:T(8,128)S(1)}, f32[4,32,256]{2,1,0:T(8,128)S(1)}, u32[]{:S(2)}, u32[]{:S(2)}) collective-permute-start(f32[4,32,256]{2,1,0:T(8,128)S(1)} %get-tuple-element.111), channel_id=1, source_target_pairs={{0,2},{2,4},{4,6},{6,8},{8,10},{10,12},{12,14},{14,16},{16,18},{18... | collective-permute-start | bytes 393224 | tf_op jit(solution)/shard_map/ppermute | solution.py:16
  71.2 9.9 %collective-permute-start.40 = (f32[4,32,256]{2,1,0:T(8,128)S(1)}, f32[4,32,256]{2,1,0:T(8,128)S(1)}, u32[]{:S(2)}, u32[]{:S(2)}) collective-permute-start(f32[4,32,256]{2,1,0:T(8,128)S(1)} %get-tuple-element.113), channel_id=1, source_target_pairs={{2,0},{4,2},{6,4},{8,6},{10,8},{12,10},{14,12},{16,14},{18,16},{20... | collective-permute-start | bytes 393224 | tf_op jit(solution)/shard_map/ppermute | solution.py:17
  95.0 10.3 %collective-permute-start.13 = (f32[4,32,256]{2,1,0:T(8,128)S(1)}, f32[4,32,256]{2,1,0:T(8,128)S(1)}, u32[]{:S(2)}, u32[]{:S(2)}) collective-permute-start(f32[4,32,256]{2,1,0:T(8,128)S(1)} %get-tuple-element.107), channel_id=1, source_target_pairs={{0,2},{2,4},{4,6},{6,8},{8,10},{10,12},{12,14},{14,16},{16,18},{18... | collective-permute-start | bytes 393224 | tf_op jit(solution)/shard_map/ppermute | solution.py:16
  98.3 9.9 %collective-permute-start.44 = (f32[4,32,256]{2,1,0:T(8,128)S(1)}, f32[4,32,256]{2,1,0:T(8,128)S(1)}, u32[]{:S(2)}, u32[]{:S(2)}) collective-permute-start(f32[4,32,256]{2,1,0:T(8,128)S(1)} %get-tuple-element.109), channel_id=1, source_target_pairs={{2,0},{4,2},{6,4},{8,6},{10,8},{12,10},{14,12},{16,14},{18,16},{20... | collective-permute-start | bytes 393224 | tf_op jit(solution)/shard_map/ppermute | solution.py:17
  122.1 11.8 %collective-permute-start.17 = (f32[4,32,256]{2,1,0:T(8,128)S(1)}, f32[4,32,256]{2,1,0:T(8,128)S(1)}, u32[]{:S(2)}, u32[]{:S(2)}) collective-permute-start(f32[4,32,256]{2,1,0:T(8,128)S(1)} %get-tuple-element.103), channel_id=1, source_target_pairs={{0,2},{2,4},{4,6},{6,8},{8,10},{10,12},{12,14},{14,16},{16,18},{18... | collective-permute-start | bytes 393224 | tf_op jit(solution)/shard_map/ppermute | solution.py:16
  124.1 11.2 %collective-permute-start.16 = (f32[4,32,256]{2,1,0:T(8,128)S(1)}, f32[4,32,256]{2,1,0:T(8,128)S(1)}, u32[]{:S(2)}, u32[]{:S(2)}) collective-permute-start(f32[4,32,256]{2,1,0:T(8,128)S(1)} %get-tuple-element.104), channel_id=1, source_target_pairs={{2,0},{4,2},{6,4},{8,6},{10,8},{12,10},{14,12},{16,14},{18,16},{20... | collective-permute-start | bytes 393224 | tf_op jit(solution)/shard_map/ppermute | solution.py:17
  125.4 14.5 %collective-permute-start.48 = (f32[4,32,256]{2,1,0:T(8,128)S(1)}, f32[4,32,256]{2,1,0:T(8,128)S(1)}, u32[]{:S(2)}, u32[]{:S(2)}) collective-permute-start(f32[4,32,256]{2,1,0:T(8,128)S(1)} %get-tuple-element.105), channel_id=1, source_target_pairs={{2,0},{4,2},{6,4},{8,6},{10,8},{12,10},{14,12},{16,14},{18,16},{20... | collective-permute-start | bytes 393224 | tf_op jit(solution)/shard_map/ppermute | solution.py:17
  126.7 14.5 %collective-permute-start.49 = (f32[4,32,256]{2,1,0:T(8,128)S(1)}, f32[4,32,256]{2,1,0:T(8,128)S(1)}, u32[]{:S(2)}, u32[]{:S(2)}) collective-permute-start(f32[4,32,256]{2,1,0:T(8,128)S(1)} %get-tuple-element.106), channel_id=1, source_target_pairs={{0,2},{2,4},{4,6},{6,8},{8,10},{10,12},{12,14},{14,16},{16,18},{18... | collective-permute-start | bytes 393224 | tf_op jit(solution)/shard_map/ppermute | solution.py:16
  132.4 26.2 %collective-permute-start.66 = (f32[10,1,256]{2,1,0:T(1,128)S(1)}, f32[10,1,256]{2,1,0:T(1,128)S(1)}, u32[]{:S(2)}, u32[]{:S(2)}) collective-permute-start(f32[10,1,256]{2,1,0:T(1,128)S(1)} %get-tuple-element.87), channel_id=1, source_target_pairs={{0,1},{2,3},{4,5},{6,7},{8,9},{10,11},{12,13},{14,15},{16,17},{18,... | collective-permute-start | bytes 30728 | tf_op jit(solution)/shard_map/ppermute | solution.py:16
  134.0 31.8 %collective-permute-start.67 = (f32[10,1,256]{2,1,0:T(1,128)S(1)}, f32[10,1,256]{2,1,0:T(1,128)S(1)}, u32[]{:S(2)}, u32[]{:S(2)}) collective-permute-start(f32[10,1,256]{2,1,0:T(1,128)S(1)} %get-tuple-element.88), channel_id=1, source_target_pairs={{1,0},{3,2},{5,4},{7,6},{9,8},{11,10},{13,12},{15,14},{17,16},{19,... | collective-permute-start | bytes 30728 | tf_op jit(solution)/shard_map/ppermute | solution.py:17
  135.3 10.5 %collective-permute-start.19 = (f32[16,4,256]{2,1,0:T(4,128)S(1)}, f32[16,4,256]{2,1,0:T(4,128)S(1)}, u32[]{:S(2)}, u32[]{:S(2)}) collective-permute-start(f32[16,4,256]{2,1,0:T(4,128)S(1)} %get-tuple-element.51), channel_id=1, source_target_pairs={{0,1},{2,3},{4,5},{6,7},{8,9},{10,11},{12,13},{14,15},{16,17},{18,... | collective-permute-start | bytes 196616 | tf_op jit(solution)/shard_map/ppermute | solution.py:16
  154.5 11.6 %collective-permute-start.21 = (f32[4,32,256]{2,1,0:T(8,128)S(1)}, f32[4,32,256]{2,1,0:T(8,128)S(1)}, u32[]{:S(2)}, u32[]{:S(2)}) collective-permute-start(f32[4,32,256]{2,1,0:T(8,128)S(1)} %get-tuple-element.99), channel_id=1, source_target_pairs={{0,2},{2,4},{4,6},{6,8},{8,10},{10,12},{12,14},{14,16},{16,18},{18... | collective-permute-start | bytes 393224 | tf_op jit(solution)/shard_map/ppermute | solution.py:16
  156.0 10.1 %collective-permute-start.20 = (f32[4,32,256]{2,1,0:T(8,128)S(1)}, f32[4,32,256]{2,1,0:T(8,128)S(1)}, u32[]{:S(2)}, u32[]{:S(2)}) collective-permute-start(f32[4,32,256]{2,1,0:T(8,128)S(1)} %get-tuple-element.100), channel_id=1, source_target_pairs={{2,0},{4,2},{6,4},{8,6},{10,8},{12,10},{14,12},{16,14},{18,16},{20... | collective-permute-start | bytes 393224 | tf_op jit(solution)/shard_map/ppermute | solution.py:17
  157.3 11.6 %collective-permute-start.52 = (f32[4,32,256]{2,1,0:T(8,128)S(1)}, f32[4,32,256]{2,1,0:T(8,128)S(1)}, u32[]{:S(2)}, u32[]{:S(2)}) collective-permute-start(f32[4,32,256]{2,1,0:T(8,128)S(1)} %get-tuple-element.101), channel_id=1, source_target_pairs={{2,0},{4,2},{6,4},{8,6},{10,8},{12,10},{14,12},{16,14},{18,16},{20... | collective-permute-start | bytes 393224 | tf_op jit(solution)/shard_map/ppermute | solution.py:17
  158.6 10.3 %collective-permute-start.53 = (f32[4,32,256]{2,1,0:T(8,128)S(1)}, f32[4,32,256]{2,1,0:T(8,128)S(1)}, u32[]{:S(2)}, u32[]{:S(2)}) collective-permute-start(f32[4,32,256]{2,1,0:T(8,128)S(1)} %get-tuple-element.102), channel_id=1, source_target_pairs={{0,2},{2,4},{4,6},{6,8},{8,10},{10,12},{12,14},{14,16},{16,18},{18... | collective-permute-start | bytes 393224 | tf_op jit(solution)/shard_map/ppermute | solution.py:16
  182.9 10.0 %collective-permute-start.25 = (f32[4,32,256]{2,1,0:T(8,128)S(1)}, f32[4,32,256]{2,1,0:T(8,128)S(1)}, u32[]{:S(2)}, u32[]{:S(2)}) collective-permute-start(f32[4,32,256]{2,1,0:T(8,128)S(1)} %get-tuple-element.95), channel_id=1, source_target_pairs={{0,2},{2,4},{4,6},{6,8},{8,10},{10,12},{12,14},{14,16},{16,18},{18... | collective-permute-start | bytes 393224 | tf_op jit(solution)/shard_map/ppermute | solution.py:16
  186.3 9.5 %collective-permute-start.56 = (f32[4,32,256]{2,1,0:T(8,128)S(1)}, f32[4,32,256]{2,1,0:T(8,128)S(1)}, u32[]{:S(2)}, u32[]{:S(2)}) collective-permute-start(f32[4,32,256]{2,1,0:T(8,128)S(1)} %get-tuple-element.97), channel_id=1, source_target_pairs={{2,0},{4,2},{6,4},{8,6},{10,8},{12,10},{14,12},{16,14},{18,16},{20... | collective-permute-start | bytes 393224 | tf_op jit(solution)/shard_map/ppermute | solution.py:17
  210.5 43.2 %collective-permute-start.29 = (f32[4,32,256]{2,1,0:T(8,128)}, f32[4,32,256]{2,1,0:T(8,128)S(1)}, u32[]{:S(2)}, u32[]{:S(2)}) collective-permute-start(f32[4,32,256]{2,1,0:T(8,128)} %get-tuple-element.91), channel_id=1, source_target_pairs={{0,2},{2,4},{4,6},{6,8},{8,10},{10,12},{12,14},{14,16},{16,18},{18... | collective-permute-start | bytes 393224 | tf_op jit(solution)/shard_map/ppermute | solution.py:16
  212.5 41.2 %collective-permute-start.28 = (f32[4,32,256]{2,1,0:T(8,128)}, f32[4,32,256]{2,1,0:T(8,128)}, u32[]{:S(2)}, u32[]{:S(2)}) collective-permute-start(f32[4,32,256]{2,1,0:T(8,128)} %get-tuple-element.92), channel_id=1, source_target_pairs={{2,0},{4,2},{6,4},{8,6},{10,8},{12,10},{14,12},{16,14},{18,16},{20... | collective-permute-start | bytes 393224 | tf_op jit(solution)/shard_map/ppermute | solution.py:17
  214.5 42.9 %collective-permute-start.60 = (f32[4,32,256]{2,1,0:T(8,128)}, f32[4,32,256]{2,1,0:T(8,128)}, u32[]{:S(2)}, u32[]{:S(2)}) collective-permute-start(f32[4,32,256]{2,1,0:T(8,128)} %get-tuple-element.93), channel_id=1, source_target_pairs={{2,0},{4,2},{6,4},{8,6},{10,8},{12,10},{14,12},{16,14},{18,16},{20... | collective-permute-start | bytes 393224 | tf_op jit(solution)/shard_map/ppermute | solution.py:17
  215.8 41.6 %collective-permute-start.61 = (f32[4,32,256]{2,1,0:T(8,128)}, f32[4,32,256]{2,1,0:T(8,128)}, u32[]{:S(2)}, u32[]{:S(2)}) collective-permute-start(f32[4,32,256]{2,1,0:T(8,128)} %get-tuple-element.94), channel_id=1, source_target_pairs={{0,2},{2,4},{4,6},{6,8},{8,10},{10,12},{12,14},{14,16},{16,18},{18... | collective-permute-start | bytes 393224 | tf_op jit(solution)/shard_map/ppermute | solution.py:16
  254.5 9.9 %collective-permute-start.31 = (f32[16,4,256]{2,1,0:T(4,128)S(1)}, f32[16,4,256]{2,1,0:T(4,128)S(1)}, u32[]{:S(2)}, u32[]{:S(2)}) collective-permute-start(f32[16,4,256]{2,1,0:T(4,128)S(1)} %get-tuple-element.27), channel_id=1, source_target_pairs={{0,1},{2,3},{4,5},{6,7},{8,9},{10,11},{12,13},{14,15},{16,17},{18,... | collective-permute-start | bytes 196616 | tf_op jit(solution)/shard_map/ppermute | solution.py:16
  (64 other events, 573.9 us)
where the time goes:
time: 329 us; the launch traced here: 327 us
  starting transfers between devices  167 us (51%)
  blocking collectives  42.1 us (13%)
  local copies, waits for them, and re-layouts  41.5 us (13%)
  other arithmetic  37.6 us (11%)
  waiting for transfers between devices  34.9 us (11%)
  between operations  3.84 us (1%)
    ppermute x34, starting transfers between devices, padded_2(): before = lax.ppermute(last, axis, up)  122 us
    ppermute x34, starting transfers between devices, padded_2(): after = lax.ppermute(initial, axis, down)  44.6 us
    psum x1, blocking collectives, on_device(): lax.psum((jnp.sum(residual * born), jnp.sum(born * born)), ('gx', 'gy'))  42.1 us
    ppermute x34, waiting for transfers between devices, padded_2(): after = lax.ppermute(initial, axis, down)  33.2 us
    concatenate x47, other arithmetic, padded_2(): value = jnp.concatenate([before, value, after], axis=dim)  15.1 us
    gather x8, local copies, waits for them, and re-layouts, on_device(): born_list.append(jnp.take(q_new.reshape(-1), indices))  14.9 us
    gather x8, local copies, waits for them, and re-layouts, on_device(): synth_list.append(jnp.take(p_new.reshape(-1), indices))  14.5 us
    add x8, other arithmetic, on_device(): q_new = 2.0 * q_cur - q_old + courant * lap_q + perturbation * lap_p  11.5 us
  transfers between devices with their start and end apart: 68, of which 15 were waited for; matrix products, arithmetic and copies ran while one was open for 17% of the time, Pallas kernels for 0%

commit v1 on v0

v1 whole, which is shorter than its diff:
```python
import functools

import jax
import jax.numpy as jnp
from jax import lax
from jax.experimental import pallas as pl
from jax.experimental.pallas import tpu as pltpu
from jax.sharding import PartitionSpec as P

COEF = (-205.0 / 72.0, 8.0 / 5.0, -1.0 / 5.0, 8.0 / 315.0, -1.0 / 560.0)
AXES = ("gx", "gy")
LANES = 128
F32 = jnp.float32

VMEM = pl.BlockSpec(memory_space=pltpu.VMEM)
SMEM = pl.BlockSpec(memory_space=pltpu.SMEM)


def struct(*shape):
    return jax.ShapeDtypeStruct(shape, F32)


def params():
    return pltpu.CompilerParams(vmem_limit_bytes=24 * 1024 * 1024)


def cost(flops, moved):
    return pl.CostEstimate(flops=flops, bytes_accessed=moved, transcendentals=0)


def near_pairs(count):
    return [(i, i ^ 1) for i in range(count)]


def far_pairs(count):
    pairs = []
    for i in range(1, count - 1, 2):
        pairs += [(i, i + 1), (i + 1, i)]
    return pairs


def diagonal(pairs_x, pairs_y, count_y):
    return [(a * count_y + b, c * count_y + d) for a, c in pairs_x for b, d in pairs_y]


def laplace(field, layer, row, rows, lane):
    centre = [field[layer, half, row : row + rows, :] for half in range(2)]
    totals = [(3.0 * COEF[0]) * value for value in centre]
    for k in range(1, 5):
        keep_up = lane < LANES - k
        keep_down = lane >= k
        up = [pltpu.roll(value, LANES - k, 1) for value in centre]
        down = [pltpu.roll(value, k, 1) for value in centre]
        depth = [
            jnp.where(keep_up, up[0], up[1]) + jnp.where(keep_down, down[0], 0.0),
            jnp.where(keep_up, up[1], 0.0) + jnp.where(keep_down, down[1], down[0]),
        ]
        for half in range(2):
            pair = (
                field[layer + k, half, row : row + rows, :]
                + field[layer - k, half, row : row + rows, :]
            )
            pair = pair + (
                field[layer, half, row + k : row + k + rows, :]
                + field[layer, half, row - k : row - k + rows, :]
            )
            totals[half] = totals[half] + COEF[k] * (pair + depth[half])
    return totals


def halves(value):
    return (value[..., :LANES], value[..., LANES:])


def put(target, layers, rows, value):
    for half, part in enumerate(halves(value)):
        target[layers, half, rows, :] = part


def place_wide(wide, scalars, own, near, far, strips, near_strips, corners, first):
    size_x, size_y, _ = own.shape
    par_x = scalars[0]
    par_y = scalars[1]
    inner = slice(16, 16 + size_y)
    put(wide, slice(8, 8 + size_x), inner, own[...])
    near_at = (size_x + 8) * (1 - par_x)
    far_at = (size_x + 8) * par_x
    put(wide, pl.ds(near_at, 8), inner, near[0:8])
    put(wide, pl.ds(far_at, 8), inner, far[0:8])
    for side in range(2):
        rows = slice(8, 16) if side == 0 else slice(16 + size_y, 24 + size_y)

        def fill(which, rows=rows):
            if which < len(strips):
                put(wide, slice(8, 8 + size_x), rows, strips[which][8 * first : 8 * first + 8])
                put(wide, pl.ds(near_at, 8), rows, near_strips[which][8 * first : 8 * first + 8])
                corner_at = 4 + (size_x + 4) * par_x
                put(wide, pl.ds(corner_at, 4), rows, corners[which][4 * first : 4 * first + 4])
            else:
                zero = jnp.zeros((size_x + 8, 8, 2 * LANES), F32)
                put(wide, slice(4, 12 + size_x), rows, zero)

        pl.when(par_y == 1 - side)(functools.partial(fill, 0))
        pl.when(par_y == side)(functools.partial(fill, 1))


def each_side(scalars, count, size_y, present, absent):
    par_y = scalars[1]
    for side in range(2):
        start = 0 if side == 0 else 8 + size_y
        for which in range(2):
            action = present if which < count else absent
            at = 1 - side if which == 0 else side
            pl.when(par_y == at)(functools.partial(action, start))


def send_strips(scalars, value, size_x, size_y):
    even = scalars[1] == 0
    low = value[:, 0:8, :]
    high = value[:, size_y - 8 : size_y, :]
    return [jnp.where(even, high, low), jnp.where(even, low, high)]


def step_pair_kernel(count, tangent, blank, *refs):
    refs = list(refs)
    scalars = refs.pop(0)
    if not tangent:
        wave = refs.pop(0)
    if not blank:
        own, near, far = refs[:3]
        refs = refs[3:]
        strips, refs = refs[:count], refs[count:]
        near_strips, refs = refs[:count], refs[count:]
        corners, refs = refs[:count], refs[count:]
        prev = refs.pop(0)
    speed = refs.pop(0)
    if tangent:
        drive1, drive2 = refs[:2]
        refs = refs[2:]
        partner_strips, refs = refs[:count], refs[count:]
    else:
        perturb = refs.pop(0)
    next1, next2 = refs[:2]
    refs = refs[2:]
    if not tangent:
        drive1, drive2 = refs[:2]
        refs = refs[2:]
    strip_out, refs = refs[:count], refs[count:]
    if tangent:
        corner_out, refs = refs[:count], refs[count:]
    size_x, size_y, _ = next2.shape
    par_x = scalars[0]
    inner = slice(8, 8 + size_y)

    def lanes(rows):
        return lax.broadcasted_iota(jnp.int32, (rows, LANES), 1)

    if not blank:
        wide = refs.pop(0)
        place_wide(
            wide, scalars, own, near, far, strips, near_strips, corners, 1 if tangent else 0
        )

        def advance(layer, start, rows):
            laps = laplace(wide, layer + 4, start + 8, rows, lanes(rows))
            span = slice(start, start + rows)
            for half in range(2):
                value = wide[layer + 4, half, start + 8 : start + 8 + rows, :]
                fresh = (
                    2.0 * value
                    - prev[layer, half, span, :]
                    + speed[layer, half, span, :] * laps[half]
                )
                if tangent:
                    fresh = fresh + drive1[layer, half, span, :]
                else:
                    drive1[layer, half, span, :] = perturb[layer, half, span, :] * laps[half]
                next1[layer, half, span, :] = fresh

        def main(layer, carry):
            advance(layer, 8, size_y)
            return carry

        lax.fori_loop(0, size_x + 8, main, 0)

        def present(start):
            def body(layer, carry):
                advance(layer, start, 8)
                return carry

            lax.fori_loop(4, 4 + size_x, body, 0)

        def absent(start):
            zero = jnp.zeros((size_x, 2, 8, LANES), F32)
            next1[4 : 4 + size_x, :, start : start + 8, :] = zero
            if not tangent:
                drive1[4 : 4 + size_x, :, start : start + 8, :] = zero

        each_side(scalars, count, size_y, present, absent)
    else:
        next1[...] = drive1[...]

    if not tangent:
        src_x, src_y, src_z = scalars[2], scalars[3], scalars[4]

        @pl.when((src_x >= -4) & (src_x < size_x + 4) & (src_y >= -8) & (src_y < size_y + 8))
        def _():
            half = lax.shift_right_logical(src_z, 7)
            hit = lax.broadcasted_iota(jnp.int32, (1, LANES), 1) == src_z - half * LANES
            row = next1[src_x + 4, half, pl.ds(src_y + 8, 1), :]
            next1[src_x + 4, half, pl.ds(src_y + 8, 1), :] = row + jnp.where(hit, wave[0], 0.0)

    def second(layer, carry):
        laps = laplace(next1, layer + 4, 8, size_y, lanes(size_y))
        for half in range(2):
            fresh = 2.0 * next1[layer + 4, half, inner, :]
            if not blank:
                fresh = fresh - wide[layer + 8, half, 16 : 16 + size_y, :]
            fresh = fresh + speed[layer + 4, half, inner, :] * laps[half]
            if tangent:
                fresh = fresh + drive2[layer, half]
            else:
                drive2[layer, half] = perturb[layer + 4, half, inner, :] * laps[half]
            next2[layer, :, half * LANES : (half + 1) * LANES] = fresh
        return carry

    lax.fori_loop(0, size_x, second, 0)

    if not tangent:

        @pl.when((src_x >= 0) & (src_x < size_x) & (src_y >= 0) & (src_y < size_y))
        def _():
            hit = lax.broadcasted_iota(jnp.int32, (1, 2 * LANES), 1) == src_z
            row = next2[src_x, pl.ds(src_y, 1), :]
            next2[src_x, pl.ds(src_y, 1), :] = row + jnp.where(hit, wave[1], 0.0)

    made = send_strips(scalars, next2[...], size_x, size_y)
    for which in range(count):
        if not tangent:
            strip_out[which][...] = made[which]
        else:
            strip_out[which][0:size_x] = partner_strips[which][...]
            strip_out[which][size_x : 2 * size_x] = made[which]
            facing = pl.ds((size_x - 4) * par_x, 4)
            corner_out[which][0:4] = partner_strips[which][facing]
            strip = strip_out[which][pl.ds(size_x + (size_x - 4) * par_x, 4)]
            corner_out[which][4:8] = strip


def wide_shape(shape):
    return pltpu.VMEM((shape[0] + 16, 2, shape[1] + 32, LANES), F32)


def ring_struct(shape):
    return struct(shape[0] + 8, 2, shape[1] + 16, LANES)


def pressure_steps(shape, count, scalars, wave, pieces, prev, speed, perturb):
    own, near, far, strips, near_strips, corners = pieces
    outs = [ring_struct(shape), struct(*shape), ring_struct(shape)]
    outs += [struct(shape[0], 2, shape[1], LANES)]
    outs += [struct(shape[0], 8, shape[2])] * count
    args = [own, near, far, *strips, *near_strips, *corners, prev, speed, perturb]
    out = pl.pallas_call(
        functools.partial(step_pair_kernel, count, False, False),
        out_shape=outs,
        in_specs=[SMEM, SMEM] + [VMEM] * len(args),
        out_specs=[VMEM] * len(outs),
        scratch_shapes=[wide_shape(shape)],
        compiler_params=params(),
        cost_estimate=cost(9_000_000, 4_000_000),
        name="pressure_steps",
    )(scalars, wave, *args)
    return out[0], out[1], out[2], out[3], list(out[4:])


def tangent_steps(shape, count, scalars, pieces, prev, speed, drive1, drive2, partner_strips):
    blank = pieces is None
    outs = [ring_struct(shape), struct(*shape)]
    outs += [struct(2 * shape[0], 8, shape[2])] * count
    outs += [struct(8, 8, shape[2])] * count
    args = []
    if not blank:
        own, near, far, strips, near_strips, corners = pieces
        args = [own, near, far, *strips, *near_strips, *corners, prev]
    args += [speed, drive1, drive2, *partner_strips]
    out = pl.pallas_call(
        functools.partial(step_pair_kernel, count, True, blank),
        out_shape=outs,
        in_specs=[SMEM] + [VMEM] * len(args),
        out_specs=[VMEM] * len(outs),
        scratch_shapes=[] if blank else [wide_shape(shape)],
        compiler_params=params(),
        cost_estimate=cost(9_000_000, 4_000_000),
        name="tangent_steps",
    )(scalars, *args)
    return out[0], out[1], list(out[2 : 2 + count]), list(out[2 + count :])


def pack_kernel(count, scalars, p_now, p_prev, speed, perturb, far, near, *outs):
    size_x, size_y, _ = p_now.shape
    par_x = scalars[0]
    far_face = pl.ds((size_x - 4) * par_x, 4)
    near_face = pl.ds((size_x - 4) * (1 - par_x), 4)
    for target, face in ((far, far_face), (near, near_face)):
        target[0:size_x] = p_now[...]
        for k, field in enumerate((p_prev, speed, perturb)):
            target[size_x + 4 * k : size_x + 4 * k + 4] = field[face]
    strips, corners = outs[:count], outs[count:]
    for k, field in enumerate((p_now, perturb, p_prev, speed)):
        made = send_strips(scalars, field[...], size_x, size_y)
        for which in range(count):
            strips[which][k * size_x : (k + 1) * size_x] = made[which]
    for which in range(count):
        for k in range(2):
            start = k * size_x + (size_x - 4) * par_x
            corners[which][4 * k : 4 * k + 4] = strips[which][pl.ds(start, 4)]


def pack(shape, count, scalars, p_now, p_prev, speed, perturb):
    outs = [struct(shape[0] + 12, shape[1], shape[2])] * 2
    outs += [struct(4 * shape[0], 8, shape[2])] * count
    outs += [struct(8, 8, shape[2])] * count
    out = pl.pallas_call(
        functools.partial(pack_kernel, count),
        out_shape=outs,
        in_specs=[SMEM] + [VMEM] * 4,
        out_specs=[VMEM] * len(outs),
        compiler_params=params(),
        cost_estimate=cost(10_000, 3_000_000),
        name="pack",
    )(scalars, p_now, p_prev, speed, perturb)
    return out[0], out[1], list(out[2 : 2 + count]), list(out[2 + count :])


def gather_ring_kernel(count, scalars, p_prev, speed, perturb, near, far, *refs):
    strips, refs = refs[:count], refs[count:]
    near_strips, refs = refs[:count], refs[count:]
    corners, targets = refs[:count], refs[count:]
    size_x, size_y, _ = p_prev.shape
    par_x, par_y = scalars[0], scalars[1]
    inner = slice(8, 8 + size_y)
    near_at = (size_x + 4) * (1 - par_x)
    far_at = (size_x + 4) * par_x
    for k, (own, target) in enumerate(zip((p_prev, speed, perturb), targets)):
        put(target, slice(4, 4 + size_x), inner, own[...])
        face = slice(size_x + 4 * k, size_x + 4 * k + 4)
        put(target, pl.ds(near_at, 4), inner, near[face])
        put(target, pl.ds(far_at, 4), inner, far[face])
        part = (2, 3, 1)[k]
        for side in range(2):
            rows = slice(0, 8) if side == 0 else slice(8 + size_y, 16 + size_y)

            def fill(which, k=k, rows=rows, target=target, part=part):
                if which < count:
                    base = part * size_x
                    put(target, slice(4, 4 + size_x), rows, strips[which][base : base + size_x])
                    if k == 2:
                        face = pl.ds(base + (size_x - 4) * par_x, 4)
                        put(target, pl.ds(near_at, 4), rows, near_strips[which][face])
                        put(target, pl.ds(far_at, 4), rows, corners[which][4:8])
                else:
                    zero = jnp.zeros((size_x + 8, 8, 2 * LANES), F32)
                    put(target, slice(0, 8 + size_x), rows, zero)

            pl.when(par_y == 1 - side)(functools.partial(fill, 0))
            pl.when(par_y == side)(functools.partial(fill, 1))


def gather_ring(shape, count, scalars, fields, near, far, strips, near_strips, corners):
    args = [*fields, near, far, *strips, *near_strips, *corners]
    return pl.pallas_call(
        functools.partial(gather_ring_kernel, count),
        out_shape=[ring_struct(shape)] * 3,
        in_specs=[SMEM] + [VMEM] * len(args),
        out_specs=[VMEM] * 3,
        compiler_params=params(),
        cost_estimate=cost(10_000, 4_000_000),
        name="gather_ring",
    )(scalars, *args)


def receive_kernel(cells, p1, p2, q1, q2, synth, born):
    size_x, size_y, size_z = p2.shape
    rows, count = size_x * size_y, cells.shape[1]
    flat = cells[...]
    shift = size_z.bit_length() - 1
    row_of = lax.shift_right_logical(flat, shift)
    depth_of = flat - lax.shift_left(row_of, shift)
    pick = lax.broadcasted_iota(jnp.int32, (rows, count), 0) == row_of
    pick = pick.astype(F32).astype(jnp.bfloat16)
    depth = lax.broadcasted_iota(jnp.int32, (LANES, count), 0)
    hits = [depth == depth_of, depth + LANES == depth_of]

    def at(parts):
        total = jnp.zeros((1, count), F32)
        for part, hit in zip(parts, hits):
            rest = part
            picked = None
            for _ in range(3):
                piece = rest.astype(jnp.bfloat16)
                rest = rest - piece.astype(F32)
                got = lax.dot_general(
                    piece, pick, (((0,), (0,)), ((), ())), preferred_element_type=F32
                )
                picked = got if picked is None else picked + got
            total = total + jnp.sum(jnp.where(hit, picked, 0.0), axis=0, keepdims=True)
        return total

    for one, two, target in ((p1, p2, synth), (q1, q2, born)):
        first = [
            one[4 : 4 + size_x, half, 8 : 8 + size_y, :].reshape(rows, LANES) for half in range(2)
        ]
        target[0:1, :] = at(first)
        second = [part.reshape(rows, LANES) for part in halves(two[...])]
        target[1:2, :] = at(second)


def receive(cells, p1, p2, q1, q2):
    count = cells.shape[1]
    return pl.pallas_call(
        receive_kernel,
        out_shape=[struct(2, count)] * 2,
        in_specs=[VMEM] * 5,
        out_specs=[VMEM] * 2,
        compiler_params=params(),
        cost_estimate=cost(20_000_000, 2_500_000),
        name="receive",
    )(cells, p1, p2, q1, q2)


def smooth_kernel(perturb, smooth):
    size_x, size_y, _ = smooth.shape
    lane = lax.broadcasted_iota(jnp.int32, (size_y, LANES), 1)

    def layer_step(layer, carry):
        parts = []
        for half in range(2):

            def along_x(start, half=half):
                span = slice(start, start + size_y)
                return (
                    0.25 * perturb[layer + 3, half, span, :]
                    + 0.5 * perturb[layer + 4, half, span, :]
                    + 0.25 * perturb[layer + 5, half, span, :]
                )

            parts.append(0.25 * along_x(7) + 0.5 * along_x(8) + 0.25 * along_x(9))
        up = [pltpu.roll(value, LANES - 1, 1) for value in parts]
        down = [pltpu.roll(value, 1, 1) for value in parts]
        keep_up, keep_down = lane < LANES - 1, lane >= 1
        above = [jnp.where(keep_up, up[0], up[1]), jnp.where(keep_up, up[1], 0.0)]
        below = [jnp.where(keep_down, down[0], 0.0), jnp.where(keep_down, down[1], down[0])]
        for half in range(2):
            value = 0.25 * below[half] + 0.5 * parts[half] + 0.25 * above[half]
            smooth[layer, :, half * LANES : (half + 1) * LANES] = value
        return carry

    lax.fori_loop(0, size_x, layer_step, 0)


def smoothed(shape, perturb):
    return pl.pallas_call(
        smooth_kernel,
        out_shape=struct(*shape),
        in_specs=[VMEM],
        out_specs=VMEM,
        compiler_params=params(),
        cost_estimate=cost(1_000_000, 1_200_000),
        name="smooth",
    )(perturb)


def on_device(
    pressure_prev, pressure_now, courant, perturbation, source_pos, wavelet, rec_cells, observed
):
    shape = pressure_now.shape
    size_x, size_y, size_z = shape
    count_x, count_y = lax.axis_size("gx"), lax.axis_size("gy")
    place_x, place_y = lax.axis_index("gx"), lax.axis_index("gy")
    steps = wavelet.shape[0]
    scalars = jnp.stack(
        [
            place_x % 2,
            place_y % 2,
            source_pos[0] - place_x * size_x,
            source_pos[1] - place_y * size_y,
            source_pos[2],
        ]
    ).astype(jnp.int32)
    near_x, far_x = near_pairs(count_x), far_pairs(count_x)
    pairs_y = [near_pairs(count_y)]
    if count_y > 2:
        pairs_y.append(far_pairs(count_y))
    count = len(pairs_y)
    far_diagonal = [diagonal(far_x, pairs, count_y) for pairs in pairs_y]

    def swap_near(value):
        return lax.ppermute(value, "gx", near_x)

    def swap_far(value):
        return lax.ppermute(value, "gx", far_x)

    def swap_strips(strips, corners):
        got = [lax.ppermute(value, "gy", pairs) for value, pairs in zip(strips, pairs_y)]
        got_corners = [
            lax.ppermute(value, AXES, pairs) for value, pairs in zip(corners, far_diagonal)
        ]
        return got, [swap_near(value) for value in got], got_corners

    far_send, near_send, strips, corners = pack(
        shape, count, scalars, pressure_now, pressure_prev, courant, perturbation
    )
    far, near = swap_far(far_send), swap_near(near_send)
    strips, near_strips, corners = swap_strips(strips, corners)
    p_prev, speed, perturb = gather_ring(
        shape,
        count,
        scalars,
        (pressure_prev, courant, perturbation),
        near,
        far,
        strips,
        near_strips,
        corners,
    )
    smooth = smoothed(shape, perturb)
    cells = rec_cells.reshape(1, -1)
    p_cur, q_cur, q_prev = pressure_now, None, None
    p_far, p_near = far, near
    q_far = q_near = None
    synth_list, born_list = [], []
    for step in range(0, steps, 2):
        wave = lax.slice_in_dim(wavelet, step, step + 2)
        around = (strips, near_strips, corners)
        p_pieces = (p_cur, p_near, p_far) + around
        q_pieces = None if q_cur is None else (q_cur, q_near, q_far) + around
        p_prev, p_cur, drive1, drive2, p_strips = pressure_steps(
            shape, count, scalars, wave, p_pieces, p_prev, speed, perturb
        )
        last = step + 2 >= steps
        if not last:
            p_far, p_near = swap_far(p_cur), swap_near(p_cur)
        q_prev, q_cur, strips, corners = tangent_steps(
            shape, count, scalars, q_pieces, q_prev, speed, drive1, drive2, p_strips
        )
        if not last:
            strips, near_strips, corners = swap_strips(strips, corners)
            q_far, q_near = swap_far(q_cur), swap_near(q_cur)
        synth, born = receive(cells, p_prev, p_cur, q_prev, q_cur)
        synth_list.append(synth)
        born_list.append(born)
    synthetic = jnp.concatenate(synth_list, axis=0)
    born = jnp.concatenate(born_list, axis=0)
    residual = observed.reshape(born.shape) - synthetic
    sums = jnp.stack([jnp.sum(residual * born), jnp.sum(born * born)])
    total = count_x * count_y
    spread = jnp.broadcast_to(sums.reshape(1, 1, 2), (total, 1, 2))
    sums = jnp.sum(lax.all_to_all(spread, AXES, 0, 0), axis=(0, 1))
    step_len = sums[0] / (sums[1] + 1e-6)
    predicted = (residual - step_len * born).reshape(observed.shape)
    updated_model = courant + step_len * smooth
    return (p_cur, q_cur, predicted, updated_model)


def solution(mesh):
    field = P("gx", "gy", None)
    traces = P("gx", "gy", None, None)
    return jax.shard_map(
        on_device,
        mesh=mesh,
        in_specs=(field, field, field, field, P(), P(), field, traces),
        out_specs=(field, field, traces, field),
        check_vma=False,
    )
```

time: 329 us -> 142 us (0.43)
  starting transfers between devices: 167 us -> 69.5 us
  Pallas kernels: 0 us -> 42.6 us
  blocking collectives: 42.1 us -> 0 us
  other arithmetic: 37.6 us -> 3.37 us
  local copies, waits for them, and re-layouts: 41.5 us -> 8.69 us
  waiting for transfers between devices: 34.9 us -> 13.5 us
    ppermute x68 -> x26, starting transfers between devices: 167 us -> 61.4 us  [the longest x11 46.4 us: swap_near(): return lax.ppermute(value, 'gx', near_x)]
    pallas_call x0 -> x15, Pallas kernels: none -> 42.6 us  [the longest x4 20.5 us: pressure_steps(): pl.pallas_call(functools.partial(step_pair_kernel, count, False, False),...]
    psum x1 -> x0, blocking collectives: 42.1 us -> none  [on_device(): lax.psum((jnp.sum(residual * born), jnp.sum(born * born)), ('gx', 'gy'))]
    gather x16 -> x0, local copies, waits for them, and re-layouts: 29.4 us -> none  [the longest x8 14.9 us: on_device(): born_list.append(jnp.take(q_new.reshape(-1), indices))]
    ppermute x68 -> x26, waiting for transfers between devices: 34.9 us -> 7.21 us  [the longest x4 4.77 us: swap_strips(): lax.ppermute(value, 'gy', pairs)]
    add x18 -> x0, other arithmetic: 18.4 us -> none  [the longest x8 11.5 us: on_device(): q_new = 2.0 * q_cur - q_old + courant * lap_q + perturbation * lap_p]
    concatenate x47 -> x0, other arithmetic: 15.1 us -> none  [padded_2(): value = jnp.concatenate([before, value, after], axis=dim)]
    all_to_all x0 -> x1, starting transfers between devices: none -> 8.09 us  [on_device(): sums = jnp.sum(lax.all_to_all(spread, AXES, 0, 0), axis=(0, 1))]
  transfers between devices with their start and end apart: 68 -> 27, of which waited for: 15 -> 5; matrix products, arithmetic and copies ran while one was open for 17% -> 0% of each run, Pallas kernels for 0% -> 13%
where the time goes in v1:
time: 142 us; the launch traced here: 141 us
  starting transfers between devices  69.5 us (49%)
  Pallas kernels  42.6 us (30%)
  waiting for transfers between devices  13.5 us (10%)
  local copies, waits for them, and re-layouts  8.69 us (6%)
  between operations  3.49 us (2%)
  other arithmetic  3.37 us (2%)
    ppermute x11, starting transfers between devices, swap_near(): return lax.ppermute(value, 'gx', near_x)  46.4 us
    pallas_call x4, Pallas kernels, pressure_steps(): pl.pallas_call(functools.partial(step_pair_kernel, count, False, False),...  20.5 us
    pallas_call x4, Pallas kernels, tangent_steps(): pl.pallas_call(functools.partial(step_pair_kernel, count, True, blank), o...  17.2 us
    all_to_all x1, starting transfers between devices, on_device(): sums = jnp.sum(lax.all_to_all(spread, AXES, 0, 0), axis=(0, 1))  8.09 us
    ppermute x4, starting transfers between devices, swap_strips(): lax.ppermute(value, 'gy', pairs)  7.75 us
    all_to_all x1, waiting for transfers between devices, on_device(): sums = jnp.sum(lax.all_to_all(spread, AXES, 0, 0), axis=(0, 1))  6.28 us
    unnamed x22, local copies, waits for them, and re-layouts  6.1 us
    ppermute x4, waiting for transfers between devices, swap_strips(): lax.ppermute(value, 'gy', pairs)  4.77 us
  transfers between devices with their start and end apart: 27, of which 5 were waited for; matrix products, arithmetic and copies ran while one was open for 0% of the time, Pallas kernels for 13%

profile of v1, /device:TPU:0, one launch (start us, length us, event | category | flops | bytes accessed | tf_op | source)
XLA Modules:
  0.0 141.1 jit_solution(10717163752298756327)
XLA Ops:
  3.8 0.9 copy-done
  5.7 0.9 copy-done.3
  6.7 0.9 copy-done.4
  9.5 2.6 %collective-permute-start.2 = (f32[32,8,256]{2,1,0:T(8,128)S(1)}, f32[32,8,256]{2,1,0:T(8,128)S(1)}, u32[]{:S(2)}, u32[]{:S(2)}) collective-permute-start(f32[32,8,256]{2,1,0:T(8,128)S(1)} %get-tuple-element.55), channel_id=1, source_target_pairs={{0,1},{1,0},{2,3},{3,2},{4,5},{5,4},{6,7},{7,6},{8,9},{9,8},{10,11... | collective-permute-start | bytes 786440 | tf_op jit(solution)/shard_map/ppermute | solution.py:505
  12.1 4.8 %collective-permute-done.2.refs_0_.refs_5_ = f32[32,8,256]{2,1,0:T(8,128)S(1)} collective-permute-done((f32[32,8,256]{2,1,0:T(8,128)S(1)}, f32[32,8,256]{2,1,0:T(8,128)S(1)}, u32[]{:S(2)}, u32[]{:S(2)}) %collective-permute-start.2) | collective-permute-done | bytes 262176 | tf_op jit(solution)/shard_map/ppermute | solution.py:505
  16.8 2.2 %collective-permute-start.3 = (f32[32,8,256]{2,1,0:T(8,128)S(1)}, f32[32,8,256]{2,1,0:T(8,128)S(1)}, u32[]{:S(2)}, u32[]{:S(2)}) collective-permute-start(f32[32,8,256]{2,1,0:T(8,128)S(1)} %collective-permute-done.2.refs_0_.refs_5_), channel_id=1, source_target_pairs={{0,2},{2,0},{4,6},{6,4},{8,10},{10,8},{12,14},{14,12},{16,18},{18,... | collective-permute-start | bytes 786440 | tf_op jit(solution)/shard_map/ppermute | solution.py:499
  21.0 5.0 %pressure_steps.4 = (f32[16,2,48,128]{3,2,1,0:T(8,128)S(1)}, f32[8,32,256]{2,1,0:T(8,128)S(1)}, f32[16,2,48,128]{3,2,1,0:T(8,128)S(1)}, f32[8,2,32,128]{3,2,1,0:T(8,128)S(1)}, f32[8,8,256]{2,1,0:T(8,128)S(1)}) custom-call(s32[5]{0:T(128)S(1)} %stack.28.scalars.refs_0_, f32[2]{0:T(128)S(1)} %get-tuple-element.106.refs_1_, f32[8,32,256]{2,1,0:T(8,128)S(1)} %copy-done.4, ...), custom_call_target="tpu_custom_call" | custom-call | flops 9000000 | bytes 4000000 | tf_op jit(solution)/shard_map/pressure_steps/pallas_call | solution.py:264
  25.9 1.8 %tangent_steps.4 = (f32[16,2,48,128]{3,2,1,0:T(8,128)S(1)}, f32[8,32,256]{2,1,0:T(8,128)S(1)}, f32[16,8,256]{2,1,0:T(8,128)S(1)}, f32[8,8,256]{2,1,0:T(8,128)S(1)}) custom-call(s32[5]{0:T(128)S(1)} %stack.28.scalars.refs_0_, f32[16,2,48,128]{3,2,1,0:T(8,128)S(1)} %get-tuple-element.58.refs_9_.refs_1_.refs_8_, ...), custom_call_target="tpu_custom_call" | custom-call | flops 9000000 | bytes 4000000 | tf_op jit(solution)/shard_map/tangent_steps/pallas_call | solution.py:287
  28.4 2.1 %collective-permute-start.7 = (f32[16,8,256]{2,1,0:T(8,128)S(1)}, f32[16,8,256]{2,1,0:T(8,128)S(1)}, u32[]{:S(2)}, u32[]{:S(2)}) collective-permute-start(f32[16,8,256]{2,1,0:T(8,128)S(1)} %get-tuple-element.64), channel_id=1, source_target_pairs={{0,1},{1,0},{2,3},{3,2},{4,5},{5,4},{6,7},{7,6},{8,9},{9,8},{10,11... | collective-permute-start | bytes 393224 | tf_op jit(solution)/shard_map/ppermute | solution.py:505
  30.5 11.9 %collective-permute-start.5 = (f32[8,32,256]{2,1,0:T(8,128)S(1)}, f32[8,32,256]{2,1,0:T(8,128)S(1)}, u32[]{:S(2)}, u32[]{:S(2)}) collective-permute-start(f32[8,32,256]{2,1,0:T(8,128)S(1)} %get-tuple-element.60.refs_2_.p2), channel_id=1, source_target_pairs={{0,2},{2,0},{4,6},{6,4},{8,10},{10,8},{12,14},{14,12},{16,18},{18,... | collective-permute-start | bytes 786440 | tf_op jit(solution)/shard_map/ppermute | solution.py:499
  43.1 2.0 %collective-permute-start.12 = (f32[8,32,256]{2,1,0:T(8,128)S(1)}, f32[8,32,256]{2,1,0:T(8,128)S(1)}, u32[]{:S(2)}, u32[]{:S(2)}) collective-permute-start(f32[8,32,256]{2,1,0:T(8,128)S(1)} %get-tuple-element.68.refs_1_.q2), channel_id=1, source_target_pairs={{0,2},{2,0},{4,6},{6,4},{8,10},{10,8},{12,14},{14,12},{16,18},{18,... | collective-permute-start | bytes 786440 | tf_op jit(solution)/shard_map/ppermute | solution.py:499
  45.8 3.8 %collective-permute-start.8 = (f32[16,8,256]{2,1,0:T(8,128)S(1)}, f32[16,8,256]{2,1,0:T(8,128)S(1)}, u32[]{:S(2)}, u32[]{:S(2)}) collective-permute-start(f32[16,8,256]{2,1,0:T(8,128)S(1)} %collective-permute-done.7.refs_5_.refs_4_), channel_id=1, source_target_pairs={{0,2},{2,0},{4,6},{6,4},{8,10},{10,8},{12,14},{14,12},{16,18},{18,... | collective-permute-start | bytes 393224 | tf_op jit(solution)/shard_map/ppermute | solution.py:499
  49.7 1.0 collective-permute-done.8.refs_6_.refs_5_
  50.7 5.0 %pressure_steps.5 = (f32[16,2,48,128]{3,2,1,0:T(8,128)S(1)}, f32[8,32,256]{2,1,0:T(8,128)S(1)}, f32[16,2,48,128]{3,2,1,0:T(8,128)S(1)}, f32[8,2,32,128]{3,2,1,0:T(8,128)S(1)}, f32[8,8,256]{2,1,0:T(8,128)S(1)}) custom-call(s32[5]{0:T(128)S(1)} %stack.28.scalars.refs_0_, f32[2]{0:T(128)S(1)} %get-tuple-element.109.refs_1_, ...), custom_call_target="tpu_custom_call" | custom-call | flops 9000000 | bytes 4000000 | tf_op jit(solution)/shard_map/pressure_steps/pallas_call | solution.py:264
  55.6 4.9 %tangent_steps.5 = (f32[16,2,48,128]{3,2,1,0:T(8,128)S(1)}, f32[8,32,256]{2,1,0:T(8,128)S(1)}, f32[16,8,256]{2,1,0:T(8,128)S(1)}, f32[8,8,256]{2,1,0:T(8,128)S(1)}) custom-call(s32[5]{0:T(128)S(1)} %stack.28.scalars.refs_0_, f32[8,32,256]{2,1,0:T(8,128)S(1)} %get-tuple-element.68.refs_1_.q2, f32[8,32,256]{2,1,0:T(8,128)S(1)} %collective-permute-done.12.refs_2_, ...), custom_call_target="tpu_custom_call" | custom-call | flops 9000000 | bytes 4000000 | tf_op jit(solution)/shard_map/tangent_steps/pallas_call | solution.py:287
  61.2 1.6 %collective-permute-start.14 = (f32[16,8,256]{2,1,0:T(8,128)S(1)}, f32[16,8,256]{2,1,0:T(8,128)S(1)}, u32[]{:S(2)}, u32[]{:S(2)}) collective-permute-start(f32[16,8,256]{2,1,0:T(8,128)S(1)} %get-tuple-element.73), channel_id=1, source_target_pairs={{0,1},{1,0},{2,3},{3,2},{4,5},{5,4},{6,7},{7,6},{8,9},{9,8},{10,11... | collective-permute-start | bytes 393224 | tf_op jit(solution)/shard_map/ppermute | solution.py:505
  62.8 4.6 %collective-permute-start.10 = (f32[8,32,256]{2,1,0:T(8,128)S(1)}, f32[8,32,256]{2,1,0:T(8,128)S(1)}, u32[]{:S(2)}, u32[]{:S(2)}) collective-permute-start(f32[8,32,256]{2,1,0:T(8,128)S(1)} %get-tuple-element.67.refs_2_.p2), channel_id=1, source_target_pairs={{0,2},{2,0},{4,6},{6,4},{8,10},{10,8},{12,14},{14,12},{16,18},{18,... | collective-permute-start | bytes 786440 | tf_op jit(solution)/shard_map/ppermute | solution.py:499
  68.0 1.6 %collective-permute-start.19 = (f32[8,32,256]{2,1,0:T(8,128)S(1)}, f32[8,32,256]{2,1,0:T(8,128)S(1)}, u32[]{:S(2)}, u32[]{:S(2)}) collective-permute-start(f32[8,32,256]{2,1,0:T(8,128)S(1)} %get-tuple-element.77.refs_1_.q2), channel_id=1, source_target_pairs={{0,2},{2,0},{4,6},{6,4},{8,10},{10,8},{12,14},{14,12},{16,18},{18,... | collective-permute-start | bytes 786440 | tf_op jit(solution)/shard_map/ppermute | solution.py:499
  70.3 6.6 %collective-permute-start.15 = (f32[16,8,256]{2,1,0:T(8,128)S(1)}, f32[16,8,256]{2,1,0:T(8,128)S(1)}, u32[]{:S(2)}, u32[]{:S(2)}) collective-permute-start(f32[16,8,256]{2,1,0:T(8,128)S(1)} %collective-permute-done.14.refs_5_.refs_4_), channel_id=1, source_target_pairs={{0,2},{2,0},{4,6},{6,4},{8,10},{10,8},{12,14},{14,12},{16,18},{18,... | collective-permute-start | bytes 393224 | tf_op jit(solution)/shard_map/ppermute | solution.py:499
  76.9 1.0 collective-permute-done.15.refs_6_.refs_5_
  77.9 5.0 %pressure_steps.6 = (f32[16,2,48,128]{3,2,1,0:T(8,128)S(1)}, f32[8,32,256]{2,1,0:T(8,128)S(1)}, f32[16,2,48,128]{3,2,1,0:T(8,128)S(1)}, f32[8,2,32,128]{3,2,1,0:T(8,128)S(1)}, f32[8,8,256]{2,1,0:T(8,128)S(1)}) custom-call(s32[5]{0:T(128)S(1)} %stack.28.scalars.refs_0_, f32[2]{0:T(128)S(1)} %get-tuple-element.107.refs_1_, ...), custom_call_target="tpu_custom_call" | custom-call | flops 9000000 | bytes 4000000 | tf_op jit(solution)/shard_map/pressure_steps/pallas_call | solution.py:264
  82.9 4.9 %tangent_steps.6 = (f32[16,2,48,128]{3,2,1,0:T(8,128)S(1)}, f32[8,32,256]{2,1,0:T(8,128)S(1)}, f32[16,8,256]{2,1,0:T(8,128)S(1)}, f32[8,8,256]{2,1,0:T(8,128)S(1)}) custom-call(s32[5]{0:T(128)S(1)} %stack.28.scalars.refs_0_, f32[8,32,256]{2,1,0:T(8,128)S(1)} %get-tuple-element.77.refs_1_.q2, f32[8,32,256]{2,1,0:T(8,128)S(1)} %collective-permute-done.19.refs_2_, ...), custom_call_target="tpu_custom_call" | custom-call | flops 9000000 | bytes 4000000 | tf_op jit(solution)/shard_map/tangent_steps/pallas_call | solution.py:287
  88.4 1.5 %collective-permute-start.21 = (f32[16,8,256]{2,1,0:T(8,128)S(1)}, f32[16,8,256]{2,1,0:T(8,128)S(1)}, u32[]{:S(2)}, u32[]{:S(2)}) collective-permute-start(f32[16,8,256]{2,1,0:T(8,128)S(1)} %get-tuple-element.82), channel_id=1, source_target_pairs={{0,1},{1,0},{2,3},{3,2},{4,5},{5,4},{6,7},{7,6},{8,9},{9,8},{10,11... | collective-permute-start | bytes 393224 | tf_op jit(solution)/shard_map/ppermute | solution.py:505
  90.0 3.5 %collective-permute-start.17 = (f32[8,32,256]{2,1,0:T(8,128)S(1)}, f32[8,32,256]{2,1,0:T(8,128)S(1)}, u32[]{:S(2)}, u32[]{:S(2)}) collective-permute-start(f32[8,32,256]{2,1,0:T(8,128)S(1)} %get-tuple-element.76.refs_2_.p2), channel_id=1, source_target_pairs={{0,2},{2,0},{4,6},{6,4},{8,10},{10,8},{12,14},{14,12},{16,18},{18,... | collective-permute-start | bytes 786440 | tf_op jit(solution)/shard_map/ppermute | solution.py:499
  94.1 2.5 %collective-permute-start.24 = (f32[8,32,256]{2,1,0:T(8,128)S(1)}, f32[8,32,256]{2,1,0:T(8,128)S(1)}, u32[]{:S(2)}, u32[]{:S(2)}) collective-permute-start(f32[8,32,256]{2,1,0:T(8,128)S(1)} %get-tuple-element.86.refs_1_.q2), channel_id=1, source_target_pairs={{0,2},{2,0},{4,6},{6,4},{8,10},{10,8},{12,14},{14,12},{16,18},{18,... | collective-permute-start | bytes 786440 | tf_op jit(solution)/shard_map/ppermute | solution.py:499
  97.3 7.1 %collective-permute-start.22 = (f32[16,8,256]{2,1,0:T(8,128)S(1)}, f32[16,8,256]{2,1,0:T(8,128)S(1)}, u32[]{:S(2)}, u32[]{:S(2)}) collective-permute-start(f32[16,8,256]{2,1,0:T(8,128)S(1)} %collective-permute-done.21.refs_5_.refs_4_), channel_id=1, source_target_pairs={{0,2},{2,0},{4,6},{6,4},{8,10},{10,8},{12,14},{14,12},{16,18},{18,... | collective-permute-start | bytes 393224 | tf_op jit(solution)/shard_map/ppermute | solution.py:499
  106.4 5.6 %pressure_steps.7 = (f32[16,2,48,128]{3,2,1,0:T(8,128)S(1)}, f32[8,32,256]{2,1,0:T(8,128)}, f32[16,2,48,128]{3,2,1,0:T(8,128)S(1)}, f32[8,2,32,128]{3,2,1,0:T(8,128)S(1)}, f32[8,8,256]{2,1,0:T(8,128)S(1)}) custom-call(s32[5]{0:T(128)S(1)} %stack.28.scalars.refs_0_, f32[2]{0:T(128)S(1)} %get-tuple-element.108.refs_1_, ...), custom_call_target="tpu_custom_call" | custom-call | flops 9000000 | bytes 4000000 | tf_op jit(solution)/shard_map/pressure_steps/pallas_call | solution.py:264
  112.1 5.6 %tangent_steps.7 = (f32[16,2,48,128]{3,2,1,0:T(8,128)S(1)}, f32[8,32,256]{2,1,0:T(8,128)}, f32[16,8,256]{2,1,0:T(8,128)}, f32[8,8,256]{2,1,0:T(8,128)}) custom-call(s32[5]{0:T(128)S(1)} %stack.28.scalars.refs_0_, f32[8,32,256]{2,1,0:T(8,128)S(1)} %get-tuple-element.86.refs_1_.q2, f32[8,32,256]{2,1,0:T(8,128)S(1)} %collective-permute-done.24.refs_2_, ...), custom_call_target="tpu_custom_call" | custom-call | flops 9000000 | bytes 4000000 | tf_op jit(solution)/shard_map/tangent_steps/pallas_call | solution.py:287
  117.7 0.9 copy-done.6
  120.6 1.4 pad_maximum_fusion.1
  122.6 8.1 %all-to-all-start = ((f32[32,1,2]{2,1,0:T(1,128)}), f32[32,1,2]{2,1,0:T(1,128)S(1)}, u32[]{:S(2)}, u32[]{:S(2)}) async-start(f32[32,1,2]{2,1,0:T(1,128)} %broadcast_in_dim.2), calls=%async_computation | async-start | bytes 32768 | tf_op jit(solution)/shard_map/all_to_all | solution.py:559
  131.6 6.3 %all-to-all-done = f32[32,1,2]{2,1,0:T(1,128)S(1)} async-done(((f32[32,1,2]{2,1,0:T(1,128)}), f32[32,1,2]{2,1,0:T(1,128)S(1)}, u32[]{:S(2)}, u32[]{:S(2)}) %all-to-all-start) | async-done | bytes 288 | tf_op jit(solution)/shard_map/all_to_all | solution.py:559
  (69 shorter events, 20.1 us)
Async XLA Ops:
  3.8 1.0 copy-start
  7.6 12.6 %copy-start.1 = (f32[8,32,256]{2,1,0:T(8,128)S(1)}, f32[8,32,256]{2,1,0:T(8,128)}, u32[]{:S(2)}) copy-start(f32[8,32,256]{2,1,0:T(8,128)} %speed.3) | copy-start | bytes 786436
  8.3 12.0 %collective-permute-start = (f32[20,32,256]{2,1,0:T(8,128)S(1)}, f32[20,32,256]{2,1,0:T(8,128)S(1)}, u32[]{:S(2)}, u32[]{:S(2)}) collective-permute-start(f32[20,32,256]{2,1,0:T(8,128)S(1)} %get-tuple-element.53), channel_id=1, source_target_pairs={{0,2},{2,0},{4,6},{6,4},{8,10},{10,8},{12,14},{14,12},{16,18},{18,... | collective-permute-start | bytes 1966088 | tf_op jit(solution)/shard_map/ppermute | solution.py:499
  8.8 11.4 %collective-permute-start.1 = (f32[20,32,256]{2,1,0:T(8,128)S(1)}, f32[20,32,256]{2,1,0:T(8,128)S(1)}, u32[]{:S(2)}, u32[]{:S(2)}) collective-permute-start(f32[20,32,256]{2,1,0:T(8,128)S(1)} %get-tuple-element.54), channel_id=1, source_target_pairs={{2,4},{4,2},{6,8},{8,6},{10,12},{12,10},{14,16},{16,14},{18,20},{2... | collective-permute-start | bytes 1966088 | tf_op jit(solution)/shard_map/ppermute | solution.py:502
  9.5 10.2 %copy-start.9 = (f32[8]{0:T(128)S(1)}, f32[8]{0:T(128)}, u32[]{:S(2)}) copy-start(f32[8]{0:T(128)} %param.13) | copy-start | bytes 100
  9.5 7.3 %collective-permute-start.2 = (f32[32,8,256]{2,1,0:T(8,128)S(1)}, f32[32,8,256]{2,1,0:T(8,128)S(1)}, u32[]{:S(2)}, u32[]{:S(2)}) collective-permute-start(f32[32,8,256]{2,1,0:T(8,128)S(1)} %get-tuple-element.55), channel_id=1, source_target_pairs={{0,1},{1,0},{2,3},{3,2},{4,5},{5,4},{6,7},{7,6},{8,9},{9,8},{10,11... | collective-permute-start | bytes 786440 | tf_op jit(solution)/shard_map/ppermute | solution.py:505
  16.8 3.4 %collective-permute-start.3 = (f32[32,8,256]{2,1,0:T(8,128)S(1)}, f32[32,8,256]{2,1,0:T(8,128)S(1)}, u32[]{:S(2)}, u32[]{:S(2)}) collective-permute-start(f32[32,8,256]{2,1,0:T(8,128)S(1)} %collective-permute-done.2.refs_0_.refs_5_), channel_id=1, source_target_pairs={{0,2},{2,0},{4,6},{6,4},{8,10},{10,8},{12,14},{14,12},{16,18},{18,... | collective-permute-start | bytes 786440 | tf_op jit(solution)/shard_map/ppermute | solution.py:499
  19.1 0.7 collective-permute-start.4
  27.7 17.4 %collective-permute-start.9 = (f32[8,8,256]{2,1,0:T(8,128)S(1)}, f32[8,8,256]{2,1,0:T(8,128)S(1)}, u32[]{:S(2)}, u32[]{:S(2)}) collective-permute-start(f32[8,8,256]{2,1,0:T(8,128)S(1)} %get-tuple-element.65), channel_id=1, source_target_pairs={{2,5},{3,4},{4,3},{5,2},{6,9},{7,8},{8,7},{9,6},{10,13},{11,12},{1... | collective-permute-start | bytes 196616 | tf_op jit(solution)/shard_map/ppermute | solution.py:507
  28.4 17.4 %collective-permute-start.7 = (f32[16,8,256]{2,1,0:T(8,128)S(1)}, f32[16,8,256]{2,1,0:T(8,128)S(1)}, u32[]{:S(2)}, u32[]{:S(2)}) collective-permute-start(f32[16,8,256]{2,1,0:T(8,128)S(1)} %get-tuple-element.64), channel_id=1, source_target_pairs={{0,1},{1,0},{2,3},{3,2},{4,5},{5,4},{6,7},{7,6},{8,9},{9,8},{10,11... | collective-permute-start | bytes 393224 | tf_op jit(solution)/shard_map/ppermute | solution.py:505
  30.5 20.2 %collective-permute-start.5 = (f32[8,32,256]{2,1,0:T(8,128)S(1)}, f32[8,32,256]{2,1,0:T(8,128)S(1)}, u32[]{:S(2)}, u32[]{:S(2)}) collective-permute-start(f32[8,32,256]{2,1,0:T(8,128)S(1)} %get-tuple-element.60.refs_2_.p2), channel_id=1, source_target_pairs={{0,2},{2,0},{4,6},{6,4},{8,10},{10,8},{12,14},{14,12},{16,18},{18,... | collective-permute-start | bytes 786440 | tf_op jit(solution)/shard_map/ppermute | solution.py:499
  42.4 8.2 %collective-permute-start.6 = (f32[8,32,256]{2,1,0:T(8,128)S(1)}, f32[8,32,256]{2,1,0:T(8,128)S(1)}, u32[]{:S(2)}, u32[]{:S(2)}) collective-permute-start(f32[8,32,256]{2,1,0:T(8,128)S(1)} %get-tuple-element.60.refs_2_.p2), channel_id=1, source_target_pairs={{2,4},{4,2},{6,8},{8,6},{10,12},{12,10},{14,16},{16,14},{18,20},{2... | collective-permute-start | bytes 786440 | tf_op jit(solution)/shard_map/ppermute | solution.py:502
  43.1 12.5 %collective-permute-start.12 = (f32[8,32,256]{2,1,0:T(8,128)S(1)}, f32[8,32,256]{2,1,0:T(8,128)S(1)}, u32[]{:S(2)}, u32[]{:S(2)}) collective-permute-start(f32[8,32,256]{2,1,0:T(8,128)S(1)} %get-tuple-element.68.refs_1_.q2), channel_id=1, source_target_pairs={{0,2},{2,0},{4,6},{6,4},{8,10},{10,8},{12,14},{14,12},{16,18},{18,... | collective-permute-start | bytes 786440 | tf_op jit(solution)/shard_map/ppermute | solution.py:499
  45.1 10.5 %collective-permute-start.13 = (f32[8,32,256]{2,1,0:T(8,128)S(1)}, f32[8,32,256]{2,1,0:T(8,128)S(1)}, u32[]{:S(2)}, u32[]{:S(2)}) collective-permute-start(f32[8,32,256]{2,1,0:T(8,128)S(1)} %get-tuple-element.68.refs_1_.q2), channel_id=1, source_target_pairs={{2,4},{4,2},{6,8},{8,6},{10,12},{12,10},{14,16},{16,14},{18,20},{2... | collective-permute-start | bytes 786440 | tf_op jit(solution)/shard_map/ppermute | solution.py:502
  45.8 4.8 %collective-permute-start.8 = (f32[16,8,256]{2,1,0:T(8,128)S(1)}, f32[16,8,256]{2,1,0:T(8,128)S(1)}, u32[]{:S(2)}, u32[]{:S(2)}) collective-permute-start(f32[16,8,256]{2,1,0:T(8,128)S(1)} %collective-permute-done.7.refs_5_.refs_4_), channel_id=1, source_target_pairs={{0,2},{2,0},{4,6},{6,4},{8,10},{10,8},{12,14},{14,12},{16,18},{18,... | collective-permute-start | bytes 393224 | tf_op jit(solution)/shard_map/ppermute | solution.py:499
  60.5 9.1 %collective-permute-start.16 = (f32[8,8,256]{2,1,0:T(8,128)S(1)}, f32[8,8,256]{2,1,0:T(8,128)S(1)}, u32[]{:S(2)}, u32[]{:S(2)}) collective-permute-start(f32[8,8,256]{2,1,0:T(8,128)S(1)} %get-tuple-element.74), channel_id=1, source_target_pairs={{2,5},{3,4},{4,3},{5,2},{6,9},{7,8},{8,7},{9,6},{10,13},{11,12},{1... | collective-permute-start | bytes 196616 | tf_op jit(solution)/shard_map/ppermute | solution.py:507
  61.2 9.1 %collective-permute-start.14 = (f32[16,8,256]{2,1,0:T(8,128)S(1)}, f32[16,8,256]{2,1,0:T(8,128)S(1)}, u32[]{:S(2)}, u32[]{:S(2)}) collective-permute-start(f32[16,8,256]{2,1,0:T(8,128)S(1)} %get-tuple-element.73), channel_id=1, source_target_pairs={{0,1},{1,0},{2,3},{3,2},{4,5},{5,4},{6,7},{7,6},{8,9},{9,8},{10,11... | collective-permute-start | bytes 393224 | tf_op jit(solution)/shard_map/ppermute | solution.py:505
  62.8 15.1 %collective-permute-start.10 = (f32[8,32,256]{2,1,0:T(8,128)S(1)}, f32[8,32,256]{2,1,0:T(8,128)S(1)}, u32[]{:S(2)}, u32[]{:S(2)}) collective-permute-start(f32[8,32,256]{2,1,0:T(8,128)S(1)} %get-tuple-element.67.refs_2_.p2), channel_id=1, source_target_pairs={{0,2},{2,0},{4,6},{6,4},{8,10},{10,8},{12,14},{14,12},{16,18},{18,... | collective-permute-start | bytes 786440 | tf_op jit(solution)/shard_map/ppermute | solution.py:499
  67.3 10.5 %collective-permute-start.11 = (f32[8,32,256]{2,1,0:T(8,128)S(1)}, f32[8,32,256]{2,1,0:T(8,128)S(1)}, u32[]{:S(2)}, u32[]{:S(2)}) collective-permute-start(f32[8,32,256]{2,1,0:T(8,128)S(1)} %get-tuple-element.67.refs_2_.p2), channel_id=1, source_target_pairs={{2,4},{4,2},{6,8},{8,6},{10,12},{12,10},{14,16},{16,14},{18,20},{2... | collective-permute-start | bytes 786440 | tf_op jit(solution)/shard_map/ppermute | solution.py:502
  68.0 14.8 %collective-permute-start.19 = (f32[8,32,256]{2,1,0:T(8,128)S(1)}, f32[8,32,256]{2,1,0:T(8,128)S(1)}, u32[]{:S(2)}, u32[]{:S(2)}) collective-permute-start(f32[8,32,256]{2,1,0:T(8,128)S(1)} %get-tuple-element.77.refs_1_.q2), channel_id=1, source_target_pairs={{0,2},{2,0},{4,6},{6,4},{8,10},{10,8},{12,14},{14,12},{16,18},{18,... | collective-permute-start | bytes 786440 | tf_op jit(solution)/shard_map/ppermute | solution.py:499
  69.6 13.2 %collective-permute-start.20 = (f32[8,32,256]{2,1,0:T(8,128)S(1)}, f32[8,32,256]{2,1,0:T(8,128)S(1)}, u32[]{:S(2)}, u32[]{:S(2)}) collective-permute-start(f32[8,32,256]{2,1,0:T(8,128)S(1)} %get-tuple-element.77.refs_1_.q2), channel_id=1, source_target_pairs={{2,4},{4,2},{6,8},{8,6},{10,12},{12,10},{14,16},{16,14},{18,20},{2... | collective-permute-start | bytes 786440 | tf_op jit(solution)/shard_map/ppermute | solution.py:502
  70.3 7.6 %collective-permute-start.15 = (f32[16,8,256]{2,1,0:T(8,128)S(1)}, f32[16,8,256]{2,1,0:T(8,128)S(1)}, u32[]{:S(2)}, u32[]{:S(2)}) collective-permute-start(f32[16,8,256]{2,1,0:T(8,128)S(1)} %collective-permute-done.14.refs_5_.refs_4_), channel_id=1, source_target_pairs={{0,2},{2,0},{4,6},{6,4},{8,10},{10,8},{12,14},{14,12},{16,18},{18,... | collective-permute-start | bytes 393224 | tf_op jit(solution)/shard_map/ppermute | solution.py:499
  87.8 8.9 %collective-permute-start.23 = (f32[8,8,256]{2,1,0:T(8,128)S(1)}, f32[8,8,256]{2,1,0:T(8,128)S(1)}, u32[]{:S(2)}, u32[]{:S(2)}) collective-permute-start(f32[8,8,256]{2,1,0:T(8,128)S(1)} %get-tuple-element.83), channel_id=1, source_target_pairs={{2,5},{3,4},{4,3},{5,2},{6,9},{7,8},{8,7},{9,6},{10,13},{11,12},{1... | collective-permute-start | bytes 196616 | tf_op jit(solution)/shard_map/ppermute | solution.py:507
  88.4 8.9 %collective-permute-start.21 = (f32[16,8,256]{2,1,0:T(8,128)S(1)}, f32[16,8,256]{2,1,0:T(8,128)S(1)}, u32[]{:S(2)}, u32[]{:S(2)}) collective-permute-start(f32[16,8,256]{2,1,0:T(8,128)S(1)} %get-tuple-element.82), channel_id=1, source_target_pairs={{0,1},{1,0},{2,3},{3,2},{4,5},{5,4},{6,7},{7,6},{8,9},{9,8},{10,11... | collective-permute-start | bytes 393224 | tf_op jit(solution)/shard_map/ppermute | solution.py:505
  90.0 16.4 %collective-permute-start.17 = (f32[8,32,256]{2,1,0:T(8,128)S(1)}, f32[8,32,256]{2,1,0:T(8,128)S(1)}, u32[]{:S(2)}, u32[]{:S(2)}) collective-permute-start(f32[8,32,256]{2,1,0:T(8,128)S(1)} %get-tuple-element.76.refs_2_.p2), channel_id=1, source_target_pairs={{0,2},{2,0},{4,6},{6,4},{8,10},{10,8},{12,14},{14,12},{16,18},{18,... | collective-permute-start | bytes 786440 | tf_op jit(solution)/shard_map/ppermute | solution.py:499
  93.5 13.0 %collective-permute-start.18 = (f32[8,32,256]{2,1,0:T(8,128)S(1)}, f32[8,32,256]{2,1,0:T(8,128)S(1)}, u32[]{:S(2)}, u32[]{:S(2)}) collective-permute-start(f32[8,32,256]{2,1,0:T(8,128)S(1)} %get-tuple-element.76.refs_2_.p2), channel_id=1, source_target_pairs={{2,4},{4,2},{6,8},{8,6},{10,12},{12,10},{14,16},{16,14},{18,20},{2... | collective-permute-start | bytes 786440 | tf_op jit(solution)/shard_map/ppermute | solution.py:502
  94.1 10.3 %copy-start.7 = (s32[1,1,128]{2,1,0:T(1,128)S(1)}, s32[1,1,128]{2,1,0:T(1,128)}, u32[]{:S(2)}) copy-start(s32[1,1,128]{2,1,0:T(1,128)} %param.14) | copy-start | bytes 1540
  94.1 17.9 %collective-permute-start.24 = (f32[8,32,256]{2,1,0:T(8,128)S(1)}, f32[8,32,256]{2,1,0:T(8,128)S(1)}, u32[]{:S(2)}, u32[]{:S(2)}) collective-permute-start(f32[8,32,256]{2,1,0:T(8,128)S(1)} %get-tuple-element.86.refs_1_.q2), channel_id=1, source_target_pairs={{0,2},{2,0},{4,6},{6,4},{8,10},{10,8},{12,14},{14,12},{16,18},{18,... | collective-permute-start | bytes 786440 | tf_op jit(solution)/shard_map/ppermute | solution.py:499
  96.7 15.4 %collective-permute-start.25 = (f32[8,32,256]{2,1,0:T(8,128)S(1)}, f32[8,32,256]{2,1,0:T(8,128)S(1)}, u32[]{:S(2)}, u32[]{:S(2)}) collective-permute-start(f32[8,32,256]{2,1,0:T(8,128)S(1)} %get-tuple-element.86.refs_1_.q2), channel_id=1, source_target_pairs={{2,4},{4,2},{6,8},{8,6},{10,12},{12,10},{14,16},{16,14},{18,20},{2... | collective-permute-start | bytes 786440 | tf_op jit(solution)/shard_map/ppermute | solution.py:502
  97.3 9.1 %collective-permute-start.22 = (f32[16,8,256]{2,1,0:T(8,128)S(1)}, f32[16,8,256]{2,1,0:T(8,128)S(1)}, u32[]{:S(2)}, u32[]{:S(2)}) collective-permute-start(f32[16,8,256]{2,1,0:T(8,128)S(1)} %collective-permute-done.21.refs_5_.refs_4_), channel_id=1, source_target_pairs={{0,2},{2,0},{4,6},{6,4},{8,10},{10,8},{12,14},{14,12},{16,18},{18,... | collective-permute-start | bytes 393224 | tf_op jit(solution)/shard_map/ppermute | solution.py:499
  112.1 5.6 %copy-start.5 = (f32[8,32,256]{2,1,0:T(8,128)S(1)}, f32[8,32,256]{2,1,0:T(8,128)}, u32[]{:S(2)}) copy-start(f32[8,32,256]{2,1,0:T(8,128)} %get-tuple-element.49.p2) | copy-start | bytes 786436
  122.6 15.2 %all-to-all-start = ((f32[32,1,2]{2,1,0:T(1,128)}), f32[32,1,2]{2,1,0:T(1,128)S(1)}, u32[]{:S(2)}, u32[]{:S(2)}) async-start(f32[32,1,2]{2,1,0:T(1,128)} %broadcast_in_dim.2), calls=%async_computation | async-start | bytes 32768 | tf_op jit(solution)/shard_map/all_to_all | solution.py:559
  (6 other events, 5.1 us)

commit v2 on v1

--- a/solution.py
+++ b/solution.py
@@ -41,6 +41,10 @@
 
 def diagonal(pairs_x, pairs_y, count_y):
     return [(a * count_y + b, c * count_y + d) for a, c in pairs_x for b, d in pairs_y]
+
+
+def parity():
+    return lax.rem(lax.axis_index("gx"), 2), lax.rem(lax.axis_index("gy"), 2)
 
 
 def laplace(field, layer, row, rows, lane):
@@ -121,11 +125,12 @@
     return [jnp.where(even, high, low), jnp.where(even, low, high)]
 
 
-def step_pair_kernel(count, tangent, blank, *refs):
+def step_pair_kernel(count, tangent, blank, at, *refs):
     refs = list(refs)
-    scalars = refs.pop(0)
+    scalars = parity()
     if not tangent:
-        wave = refs.pop(0)
+        source, wave = refs[:2]
+        refs = refs[2:]
     if not blank:
         own, near, far = refs[:3]
         refs = refs[3:]
@@ -177,18 +182,12 @@
                     drive1[layer, half, span, :] = perturb[layer, half, span, :] * laps[half]
                 next1[layer, half, span, :] = fresh
 
-        def main(layer, carry):
+        for layer in range(size_x + 8):
             advance(layer, 8, size_y)
-            return carry
-
-        lax.fori_loop(0, size_x + 8, main, 0)
 
         def present(start):
-            def body(layer, carry):
+            for layer in range(4, 4 + size_x):
                 advance(layer, start, 8)
-                return carry
-
-            lax.fori_loop(4, 4 + size_x, body, 0)
 
         def absent(start):
             zero = jnp.zeros((size_x, 2, 8, LANES), F32)
@@ -201,16 +200,18 @@
         next1[...] = drive1[...]
 
     if not tangent:
-        src_x, src_y, src_z = scalars[2], scalars[3], scalars[4]
+        src_x = source[0] - lax.axis_index("gx") * size_x
+        src_y = source[1] - lax.axis_index("gy") * size_y
+        src_z = source[2]
 
         @pl.when((src_x >= -4) & (src_x < size_x + 4) & (src_y >= -8) & (src_y < size_y + 8))
         def _():
             half = lax.shift_right_logical(src_z, 7)
             hit = lax.broadcasted_iota(jnp.int32, (1, LANES), 1) == src_z - half * LANES
             row = next1[src_x + 4, half, pl.ds(src_y + 8, 1), :]
-            next1[src_x + 4, half, pl.ds(src_y + 8, 1), :] = row + jnp.where(hit, wave[0], 0.0)
-
-    def second(layer, carry):
+            next1[src_x + 4, half, pl.ds(src_y + 8, 1), :] = row + jnp.where(hit, wave[at], 0.0)
+
+    for layer in range(size_x):
         laps = laplace(next1, layer + 4, 8, size_y, lanes(size_y))
         for half in range(2):
             fresh = 2.0 * next1[layer + 4, half, inner, :]
@@ -222,9 +223,6 @@
             else:
                 drive2[layer, half] = perturb[layer + 4, half, inner, :] * laps[half]
             next2[layer, :, half * LANES : (half + 1) * LANES] = fresh
-        return carry
-
-    lax.fori_loop(0, size_x, second, 0)
 
     if not tangent:
 
@@ -232,7 +230,7 @@
         def _():
             hit = lax.broadcasted_iota(jnp.int32, (1, 2 * LANES), 1) == src_z
             row = next2[src_x, pl.ds(src_y, 1), :]
-            next2[src_x, pl.ds(src_y, 1), :] = row + jnp.where(hit, wave[1], 0.0)
+            next2[src_x, pl.ds(src_y, 1), :] = row + jnp.where(hit, wave[at + 1], 0.0)
 
     made = send_strips(scalars, next2[...], size_x, size_y)
     for which in range(count):
@@ -255,14 +253,14 @@
     return struct(shape[0] + 8, 2, shape[1] + 16, LANES)
 
 
-def pressure_steps(shape, count, scalars, wave, pieces, prev, speed, perturb):
+def pressure_steps(shape, count, at, source, wave, pieces, prev, speed, perturb):
     own, near, far, strips, near_strips, corners = pieces
     outs = [ring_struct(shape), struct(*shape), ring_struct(shape)]
     outs += [struct(shape[0], 2, shape[1], LANES)]
     outs += [struct(shape[0], 8, shape[2])] * count
     args = [own, near, far, *strips, *near_strips, *corners, prev, speed, perturb]
     out = pl.pallas_call(
-        functools.partial(step_pair_kernel, count, False, False),
+        functools.partial(step_pair_kernel, count, False, False, at),
         out_shape=outs,
         in_specs=[SMEM, SMEM] + [VMEM] * len(args),
         out_specs=[VMEM] * len(outs),
@@ -270,11 +268,11 @@
         compiler_params=params(),
         cost_estimate=cost(9_000_000, 4_000_000),
         name="pressure_steps",
-    )(scalars, wave, *args)
+    )(source, wave, *args)
     return out[0], out[1], out[2], out[3], list(out[4:])
 
 
-def tangent_steps(shape, count, scalars, pieces, prev, speed, drive1, drive2, partner_strips):
+def tangent_steps(shape, count, pieces, prev, speed, drive1, drive2, partner_strips):
     blank = pieces is None
     outs = [ring_struct(shape), struct(*shape)]
     outs += [struct(2 * shape[0], 8, shape[2])] * count
@@ -285,60 +283,69 @@
         args = [own, near, far, *strips, *near_strips, *corners, prev]
     args += [speed, drive1, drive2, *partner_strips]
     out = pl.pallas_call(
-        functools.partial(step_pair_kernel, count, True, blank),
+        functools.partial(step_pair_kernel, count, True, blank, 0),
         out_shape=outs,
-        in_specs=[SMEM] + [VMEM] * len(args),
+        in_specs=[VMEM] * len(args),
         out_specs=[VMEM] * len(outs),
         scratch_shapes=[] if blank else [wide_shape(shape)],
         compiler_params=params(),
         cost_estimate=cost(9_000_000, 4_000_000),
         name="tangent_steps",
-    )(scalars, *args)
+    )(*args)
     return out[0], out[1], list(out[2 : 2 + count]), list(out[2 + count :])
 
 
-def pack_kernel(count, scalars, p_now, p_prev, speed, perturb, far, near, *outs):
+def pack_kernel(count, p_now, p_prev, speed, perturb, far, near, *rest):
     size_x, size_y, _ = p_now.shape
-    par_x = scalars[0]
+    strips, corners, sems = rest[:count], rest[count : 2 * count], rest[2 * count]
+    par_x, par_y = parity()
     far_face = pl.ds((size_x - 4) * par_x, 4)
     near_face = pl.ds((size_x - 4) * (1 - par_x), 4)
+    moves = []
     for target, face in ((far, far_face), (near, near_face)):
-        target[0:size_x] = p_now[...]
+        moves.append((p_now, target.at[0:size_x]))
         for k, field in enumerate((p_prev, speed, perturb)):
-            target[size_x + 4 * k : size_x + 4 * k + 4] = field[face]
-    strips, corners = outs[:count], outs[count:]
-    for k, field in enumerate((p_now, perturb, p_prev, speed)):
-        made = send_strips(scalars, field[...], size_x, size_y)
-        for which in range(count):
-            strips[which][k * size_x : (k + 1) * size_x] = made[which]
+            start = size_x + 4 * k
+            moves.append((field.at[face], target.at[start : start + 4]))
     for which in range(count):
-        for k in range(2):
-            start = k * size_x + (size_x - 4) * par_x
-            corners[which][4 * k : 4 * k + 4] = strips[which][pl.ds(start, 4)]
-
-
-def pack(shape, count, scalars, p_now, p_prev, speed, perturb):
+        high = 1 - par_y if which == 0 else par_y
+        rows = pl.ds(pl.multiple_of(high * (size_y - 8), 8), 8)
+        for k, field in enumerate((p_now, perturb, p_prev, speed)):
+            moves.append((field.at[:, rows], strips[which].at[k * size_x : (k + 1) * size_x]))
+            if k < 2:
+                moves.append((field.at[far_face, rows], corners[which].at[4 * k : 4 * k + 4]))
+    copies = [
+        pltpu.make_async_copy(source, target, sems.at[k]) for k, (source, target) in enumerate(moves)
+    ]
+    for copy in copies:
+        copy.start()
+    for copy in copies:
+        copy.wait()
+
+
+def pack(shape, count, p_now, p_prev, speed, perturb):
     outs = [struct(shape[0] + 12, shape[1], shape[2])] * 2
     outs += [struct(4 * shape[0], 8, shape[2])] * count
     outs += [struct(8, 8, shape[2])] * count
     out = pl.pallas_call(
         functools.partial(pack_kernel, count),
         out_shape=outs,
-        in_specs=[SMEM] + [VMEM] * 4,
+        in_specs=[pl.BlockSpec(memory_space=pl.ANY)] * 4,
         out_specs=[VMEM] * len(outs),
+        scratch_shapes=[pltpu.SemaphoreType.DMA((8 + 6 * count,))],
         compiler_params=params(),
         cost_estimate=cost(10_000, 3_000_000),
         name="pack",
-    )(scalars, p_now, p_prev, speed, perturb)
+    )(p_now, p_prev, speed, perturb)
     return out[0], out[1], list(out[2 : 2 + count]), list(out[2 + count :])
 
 
-def gather_ring_kernel(count, scalars, p_prev, speed, perturb, near, far, *refs):
+def gather_ring_kernel(count, p_prev, speed, perturb, near, far, *refs):
     strips, refs = refs[:count], refs[count:]
     near_strips, refs = refs[:count], refs[count:]
     corners, targets = refs[:count], refs[count:]
     size_x, size_y, _ = p_prev.shape
-    par_x, par_y = scalars[0], scalars[1]
+    par_x, par_y = parity()
     inner = slice(8, 8 + size_y)
     near_at = (size_x + 4) * (1 - par_x)
     far_at = (size_x + 4) * par_x
@@ -367,21 +374,27 @@
             pl.when(par_y == side)(functools.partial(fill, 1))
 
 
-def gather_ring(shape, count, scalars, fields, near, far, strips, near_strips, corners):
+def gather_ring(shape, count, fields, near, far, strips, near_strips, corners):
     args = [*fields, near, far, *strips, *near_strips, *corners]
     return pl.pallas_call(
         functools.partial(gather_ring_kernel, count),
         out_shape=[ring_struct(shape)] * 3,
-        in_specs=[SMEM] + [VMEM] * len(args),
+        in_specs=[VMEM] * len(args),
         out_specs=[VMEM] * 3,
         compiler_params=params(),
         cost_estimate=cost(10_000, 4_000_000),
         name="gather_ring",
-    )(scalars, *args)
-
-
-def receive_kernel(cells, p1, p2, q1, q2, synth, born):
+    )(*args)
+
+
+def receive_kernel(rounds, cells, p1, p2, q1, q2, *refs):
     size_x, size_y, size_z = p2.shape
+    if rounds:
+        earlier, observed = refs[: 2 * rounds], refs[2 * rounds]
+        synth, born, spread = refs[2 * rounds + 1 :]
+    else:
+        synth, born = refs
+    steps = synth.shape[0]
     rows, count = size_x * size_y, cells.shape[1]
     flat = cells[...]
     shift = size_z.bit_length() - 1
@@ -411,22 +424,75 @@
         first = [
             one[4 : 4 + size_x, half, 8 : 8 + size_y, :].reshape(rows, LANES) for half in range(2)
         ]
-        target[0:1, :] = at(first)
+        target[steps - 2 : steps - 1, :] = at(first)
         second = [part.reshape(rows, LANES) for part in halves(two[...])]
-        target[1:2, :] = at(second)
-
-
-def receive(cells, p1, p2, q1, q2):
+        target[steps - 1 : steps, :] = at(second)
+
+
+    if rounds:
+        for k in range(rounds):
+            synth[2 * k : 2 * k + 2, :] = earlier[2 * k][...]
+            born[2 * k : 2 * k + 2, :] = earlier[2 * k + 1][...]
+        residual = observed[...] - synth[...]
+        tangent = born[...]
+        synth[...] = residual
+        numer, denom = jnp.sum(residual * tangent), jnp.sum(tangent * tangent)
+        lane = lax.broadcasted_iota(jnp.int32, spread.shape, 2)
+        spread[...] = jnp.where(lane == 0, numer, jnp.where(lane == 1, denom, 0.0))
+
+
+def receive(cells, p1, p2, q1, q2, earlier=(), observed=None, total=0):
     count = cells.shape[1]
+    rounds = len(earlier) // 2
+    outs = [struct(2 * rounds + 2, count)] * 2
+    args = [cells, p1, p2, q1, q2]
+    if rounds:
+        outs.append(struct(total, 1, LANES))
+        args += [*earlier, observed]
     return pl.pallas_call(
-        receive_kernel,
-        out_shape=[struct(2, count)] * 2,
-        in_specs=[VMEM] * 5,
-        out_specs=[VMEM] * 2,
+        functools.partial(receive_kernel, rounds),
+        out_shape=outs,
+        in_specs=[VMEM] * len(args),
+        out_specs=[VMEM] * len(outs),
         compiler_params=params(),
         cost_estimate=cost(20_000_000, 2_500_000),
         name="receive",
-    )(cells, p1, p2, q1, q2)
+    )(*args)
+
+
+def finish_kernel(sums, residual, born, speed, smooth, predicted, model, traces, field, sems):
+    lane = lax.broadcasted_iota(jnp.int32, sums.shape, 2)
+    values = sums[...]
+    numer = jnp.sum(jnp.where(lane == 0, values, 0.0))
+    denom = jnp.sum(jnp.where(lane == 1, values, 0.0))
+    length = jnp.full((1, LANES), numer) / (jnp.full((1, LANES), denom) + 1e-6)
+    traces[...] = residual[...] - length * born[...]
+    first = pltpu.make_async_copy(traces, predicted, sems.at[0])
+    first.start()
+    both = jnp.concatenate([length, length], axis=1)
+    field[...] = speed[...] + both[None] * smooth[...]
+    second = pltpu.make_async_copy(field, model, sems.at[1])
+    second.start()
+    first.wait()
+    second.wait()
+
+
+def finish(sums, residual, born, speed, smooth):
+    outs = [struct(*born.shape), struct(*speed.shape)]
+    return pl.pallas_call(
+        finish_kernel,
+        out_shape=outs,
+        in_specs=[VMEM] * 5,
+        out_specs=[pl.BlockSpec(memory_space=pl.ANY)] * 2,
+        scratch_shapes=[
+            pltpu.VMEM(born.shape, F32),
+            pltpu.VMEM(speed.shape, F32),
+            pltpu.SemaphoreType.DMA((2,)),
+        ],
+        compiler_params=params(),
+        cost_estimate=cost(200_000, 800_000),
+        name="finish",
+    )(sums, residual, born, speed, smooth)
 
 
 def smooth_kernel(perturb, smooth):
@@ -477,17 +543,7 @@
     shape = pressure_now.shape
     size_x, size_y, size_z = shape
     count_x, count_y = lax.axis_size("gx"), lax.axis_size("gy")
-    place_x, place_y = lax.axis_index("gx"), lax.axis_index("gy")
     steps = wavelet.shape[0]
-    scalars = jnp.stack(
-        [
-            place_x % 2,
-            place_y % 2,
-            source_pos[0] - place_x * size_x,
-            source_pos[1] - place_y * size_y,
-            source_pos[2],
-        ]
-    ).astype(jnp.int32)
     near_x, far_x = near_pairs(count_x), far_pairs(count_x)
     pairs_y = [near_pairs(count_y)]
     if count_y > 2:
@@ -509,14 +565,13 @@
         return got, [swap_near(value) for value in got], got_corners
 
     far_send, near_send, strips, corners = pack(
-        shape, count, scalars, pressure_now, pressure_prev, courant, perturbation
+        shape, count, pressure_now, pressure_prev, courant, perturbation
     )
     far, near = swap_far(far_send), swap_near(near_send)
     strips, near_strips, corners = swap_strips(strips, corners)
     p_prev, speed, perturb = gather_ring(
         shape,
         count,
-        scalars,
         (pressure_prev, courant, perturbation),
         near,
         far,
@@ -529,37 +584,33 @@
     p_cur, q_cur, q_prev = pressure_now, None, None
     p_far, p_near = far, near
     q_far = q_near = None
-    synth_list, born_list = [], []
+    earlier = []
     for step in range(0, steps, 2):
-        wave = lax.slice_in_dim(wavelet, step, step + 2)
         around = (strips, near_strips, corners)
         p_pieces = (p_cur, p_near, p_far) + around
         q_pieces = None if q_cur is None else (q_cur, q_near, q_far) + around
         p_prev, p_cur, drive1, drive2, p_strips = pressure_steps(
-            shape, count, scalars, wave, p_pieces, p_prev, speed, perturb
+            shape, count, step, source_pos, wavelet, p_pieces, p_prev, speed, perturb
         )
         last = step + 2 >= steps
         if not last:
             p_far, p_near = swap_far(p_cur), swap_near(p_cur)
         q_prev, q_cur, strips, corners = tangent_steps(
-            shape, count, scalars, q_pieces, q_prev, speed, drive1, drive2, p_strips
+            shape, count, q_pieces, q_prev, speed, drive1, drive2, p_strips
         )
         if not last:
             strips, near_strips, corners = swap_strips(strips, corners)
             q_far, q_near = swap_far(q_cur), swap_near(q_cur)
-        synth, born = receive(cells, p_prev, p_cur, q_prev, q_cur)
-        synth_list.append(synth)
-        born_list.append(born)
-    synthetic = jnp.concatenate(synth_list, axis=0)
-    born = jnp.concatenate(born_list, axis=0)
-    residual = observed.reshape(born.shape) - synthetic
-    sums = jnp.stack([jnp.sum(residual * born), jnp.sum(born * born)])
+        if not last:
+            earlier += receive(cells, p_prev, p_cur, q_prev, q_cur)
     total = count_x * count_y
-    spread = jnp.broadcast_to(sums.reshape(1, 1, 2), (total, 1, 2))
-    sums = jnp.sum(lax.all_to_all(spread, AXES, 0, 0), axis=(0, 1))
-    step_len = sums[0] / (sums[1] + 1e-6)
-    predicted = (residual - step_len * born).reshape(observed.shape)
-    updated_model = courant + step_len * smooth
+    observed_traces = observed.reshape(steps, -1)
+    residual, born, spread = receive(
+        cells, p_prev, p_cur, q_prev, q_cur, earlier, observed_traces, total
+    )
+    sums = lax.all_to_all(spread, AXES, 0, 0)
+    predicted, updated_model = finish(sums, residual, born, courant, smooth)
+    predicted = predicted.reshape(observed.shape)
     return (p_cur, q_cur, predicted, updated_model)
 
 

time: 142 us -> 115 us (0.81)
  Pallas kernels: 42.6 us -> 26.7 us
  other arithmetic: 3.37 us -> 0 us
  starting transfers between devices: 69.5 us -> 66.2 us
  local copies, waits for them, and re-layouts: 8.69 us -> 6.09 us
  between operations: 3.49 us -> 1.12 us
    pallas_call x12 -> x13, Pallas kernels: 40.4 us -> 24.5 us  [the longest x4 12 us: pressure_steps(): pl.pallas_call(functools.partial(step_pair_kernel, count, False, False, a...]
    ppermute x11, starting transfers between devices: 46.4 us -> 41.6 us  [swap_near(): return lax.ppermute(value, 'gx', near_x)]
    unnamed x22 -> x26, local copies, waits for them, and re-layouts: 6.1 us -> 6.09 us
  transfers between devices with their start and end apart: 27 -> 27, of which waited for: 5 -> 5; matrix products, arithmetic and copies ran while one was open for 0% -> 0% of each run, Pallas kernels for 13% -> 11%
where the time goes in v2:
time: 115 us; the launch traced here: 114 us
  starting transfers between devices  66.2 us (58%)
  Pallas kernels  26.7 us (23%)
  waiting for transfers between devices  14 us (12%)
  local copies, waits for them, and re-layouts  6.09 us (5%)
    ppermute x11, starting transfers between devices, swap_near(): return lax.ppermute(value, 'gx', near_x)  41.6 us
    pallas_call x4, Pallas kernels, pressure_steps(): pl.pallas_call(functools.partial(step_pair_kernel, count, False, False, a...  12 us
    all_to_all x1, starting transfers between devices, on_device(): sums = lax.all_to_all(spread, AXES, 0, 0)  9.02 us
    pallas_call x4, Pallas kernels, tangent_steps(): pl.pallas_call(functools.partial(step_pair_kernel, count, True, blank, 0)...  8.16 us
    ppermute x4, starting transfers between devices, swap_strips(): lax.ppermute(value, 'gy', pairs)  7.99 us
    all_to_all x1, waiting for transfers between devices, on_device(): sums = lax.all_to_all(spread, AXES, 0, 0)  6.28 us
    unnamed x26, local copies, waits for them, and re-layouts  6.09 us
    ppermute x7, starting transfers between devices, swap_far(): return lax.ppermute(value, 'gx', far_x)  4.81 us
  transfers between devices with their start and end apart: 27, of which 5 were waited for; matrix products, arithmetic and copies ran while one was open for 0% of the time, Pallas kernels for 11%

profile of v2, /device:TPU:0, one launch (start us, length us, event | category | flops | bytes accessed | tf_op | source)
XLA Modules:
  0.0 114.1 jit_solution(15808190828730015707)
XLA Ops:
  0.6 0.9 copy-done
  1.6 0.9 copy-done.2
  2.5 0.9 copy-done.4
  3.5 0.9 copy-done.6
  4.4 1.3 %pack.1 = (f32[20,32,256]{2,1,0:T(8,128)S(1)}, f32[20,32,256]{2,1,0:T(8,128)S(1)}, f32[32,8,256]{2,1,0:T(8,128)S(1)}, f32[8,8,256]{2,1,0:T(8,128)S(1)}) custom-call(f32[8,32,256]{2,1,0:T(8,128)S(1)} %copy-done.2, f32[8,32,256]{2,1,0:T(8,128)S(1)} %copy-done.4, f32[8,32,256]{2,1,0:T(8,128)S(1)} %copy-done, f32[8,32,256]{2,1,0:T(8,128)S(1)} %copy-done.6), custom_call_target="tpu_custom_call" | custom-call | flops 10000 | bytes 3000000 | tf_op jit(solution)/shard_map/pack/pallas_call | solution.py:330
  6.9 2.6 %collective-permute-start.2 = (f32[32,8,256]{2,1,0:T(8,128)S(1)}, f32[32,8,256]{2,1,0:T(8,128)S(1)}, u32[]{:S(2)}, u32[]{:S(2)}) collective-permute-start(f32[32,8,256]{2,1,0:T(8,128)S(1)} %get-tuple-element.58), channel_id=1, source_target_pairs={{0,1},{1,0},{2,3},{3,2},{4,5},{5,4},{6,7},{7,6},{8,9},{9,8},{10,11... | collective-permute-start | bytes 786440 | tf_op jit(solution)/shard_map/ppermute | solution.py:561
  9.5 4.8 %collective-permute-done.2.refs_0_.refs_5_ = f32[32,8,256]{2,1,0:T(8,128)S(1)} collective-permute-done((f32[32,8,256]{2,1,0:T(8,128)S(1)}, f32[32,8,256]{2,1,0:T(8,128)S(1)}, u32[]{:S(2)}, u32[]{:S(2)}) %collective-permute-start.2) | collective-permute-done | bytes 262176 | tf_op jit(solution)/shard_map/ppermute | solution.py:561
  14.3 2.2 %collective-permute-start.3 = (f32[32,8,256]{2,1,0:T(8,128)S(1)}, f32[32,8,256]{2,1,0:T(8,128)S(1)}, u32[]{:S(2)}, u32[]{:S(2)}) collective-permute-start(f32[32,8,256]{2,1,0:T(8,128)S(1)} %collective-permute-done.2.refs_0_.refs_5_), channel_id=1, source_target_pairs={{0,2},{2,0},{4,6},{6,4},{8,10},{10,8},{12,14},{14,12},{16,18},{18,... | collective-permute-start | bytes 786440 | tf_op jit(solution)/shard_map/ppermute | solution.py:555
  18.5 2.8 %pressure_steps.4 = (f32[16,2,48,128]{3,2,1,0:T(8,128)S(1)}, f32[8,32,256]{2,1,0:T(8,128)S(1)}, f32[16,2,48,128]{3,2,1,0:T(8,128)S(1)}, f32[8,2,32,128]{3,2,1,0:T(8,128)S(1)}, f32[8,8,256]{2,1,0:T(8,128)S(1)}) custom-call(s32[3]{0:T(128)S(1)} %copy-done.9, f32[8]{0:T(128)S(1)} %copy-done.10, f32[8,32,256]{2,1,0:T(8,128)S(1)} %copy-done.3, ...), custom_call_target="tpu_custom_call" | custom-call | flops 9000000 | bytes 4000000 | tf_op jit(solution)/shard_map/pressure_steps/pallas_call | solution.py:262
  22.7 2.1 %collective-permute-start.7 = (f32[16,8,256]{2,1,0:T(8,128)S(1)}, f32[16,8,256]{2,1,0:T(8,128)S(1)}, u32[]{:S(2)}, u32[]{:S(2)}) collective-permute-start(f32[16,8,256]{2,1,0:T(8,128)S(1)} %get-tuple-element.67), channel_id=1, source_target_pairs={{0,1},{1,0},{2,3},{3,2},{4,5},{5,4},{6,7},{7,6},{8,9},{9,8},{10,11... | collective-permute-start | bytes 393224 | tf_op jit(solution)/shard_map/ppermute | solution.py:561
  25.4 13.6 %collective-permute-start.5 = (f32[8,32,256]{2,1,0:T(8,128)S(1)}, f32[8,32,256]{2,1,0:T(8,128)S(1)}, u32[]{:S(2)}, u32[]{:S(2)}) collective-permute-start(f32[8,32,256]{2,1,0:T(8,128)S(1)} %get-tuple-element.63.refs_2_.p2), channel_id=1, source_target_pairs={{0,2},{2,0},{4,6},{6,4},{8,10},{10,8},{12,14},{14,12},{16,18},{18,... | collective-permute-start | bytes 786440 | tf_op jit(solution)/shard_map/ppermute | solution.py:555
  39.7 2.9 %collective-permute-start.12 = (f32[8,32,256]{2,1,0:T(8,128)S(1)}, f32[8,32,256]{2,1,0:T(8,128)S(1)}, u32[]{:S(2)}, u32[]{:S(2)}) collective-permute-start(f32[8,32,256]{2,1,0:T(8,128)S(1)} %get-tuple-element.71.refs_0_.q2), channel_id=1, source_target_pairs={{0,2},{2,0},{4,6},{6,4},{8,10},{10,8},{12,14},{14,12},{16,18},{18,... | collective-permute-start | bytes 786440 | tf_op jit(solution)/shard_map/ppermute | solution.py:555
  42.7 1.3 %collective-permute-done.8.refs_6_.refs_4_ = f32[16,8,256]{2,1,0:T(8,128)S(1)} collective-permute-done((f32[16,8,256]{2,1,0:T(8,128)S(1)}, f32[16,8,256]{2,1,0:T(8,128)S(1)}, u32[]{:S(2)}, u32[]{:S(2)}) %collective-permute-start.8) | collective-permute-done | bytes 131104 | tf_op jit(solution)/shard_map/ppermute | solution.py:555
  43.9 2.8 %pressure_steps.5 = (f32[16,2,48,128]{3,2,1,0:T(8,128)S(1)}, f32[8,32,256]{2,1,0:T(8,128)S(1)}, f32[16,2,48,128]{3,2,1,0:T(8,128)S(1)}, f32[8,2,32,128]{3,2,1,0:T(8,128)S(1)}, f32[8,8,256]{2,1,0:T(8,128)S(1)}) custom-call(s32[3]{0:T(128)S(1)} %copy-done.9, f32[8]{0:T(128)S(1)} %copy-done.10, f32[8,32,256]{2,1,0:T(8,128)S(1)} %get-tuple-element.63.refs_2_.p2, ...), custom_call_target="tpu_custom_call" | custom-call | flops 9000000 | bytes 4000000 | tf_op jit(solution)/shard_map/pressure_steps/pallas_call | solution.py:262
  46.8 2.3 %tangent_steps.5 = (f32[16,2,48,128]{3,2,1,0:T(8,128)S(1)}, f32[8,32,256]{2,1,0:T(8,128)S(1)}, f32[16,8,256]{2,1,0:T(8,128)S(1)}, f32[8,8,256]{2,1,0:T(8,128)S(1)}) custom-call(f32[8,32,256]{2,1,0:T(8,128)S(1)} %get-tuple-element.71.refs_0_.q2, f32[8,32,256]{2,1,0:T(8,128)S(1)} %collective-permute-done.12.refs_1_, ...), custom_call_target="tpu_custom_call" | custom-call | flops 9000000 | bytes 4000000 | tf_op jit(solution)/shard_map/tangent_steps/pallas_call | solution.py:285
  49.7 2.1 %collective-permute-start.14 = (f32[16,8,256]{2,1,0:T(8,128)S(1)}, f32[16,8,256]{2,1,0:T(8,128)S(1)}, u32[]{:S(2)}, u32[]{:S(2)}) collective-permute-start(f32[16,8,256]{2,1,0:T(8,128)S(1)} %get-tuple-element.76), channel_id=1, source_target_pairs={{0,1},{1,0},{2,3},{3,2},{4,5},{5,4},{6,7},{7,6},{8,9},{9,8},{10,11... | collective-permute-start | bytes 393224 | tf_op jit(solution)/shard_map/ppermute | solution.py:561
  52.5 8.1 %collective-permute-start.10 = (f32[8,32,256]{2,1,0:T(8,128)S(1)}, f32[8,32,256]{2,1,0:T(8,128)S(1)}, u32[]{:S(2)}, u32[]{:S(2)}) collective-permute-start(f32[8,32,256]{2,1,0:T(8,128)S(1)} %get-tuple-element.70.refs_2_.p2), channel_id=1, source_target_pairs={{0,2},{2,0},{4,6},{6,4},{8,10},{10,8},{12,14},{14,12},{16,18},{18,... | collective-permute-start | bytes 786440 | tf_op jit(solution)/shard_map/ppermute | solution.py:555
  61.2 3.1 %collective-permute-start.19 = (f32[8,32,256]{2,1,0:T(8,128)S(1)}, f32[8,32,256]{2,1,0:T(8,128)S(1)}, u32[]{:S(2)}, u32[]{:S(2)}) collective-permute-start(f32[8,32,256]{2,1,0:T(8,128)S(1)} %get-tuple-element.80.refs_0_.q2), channel_id=1, source_target_pairs={{0,2},{2,0},{4,6},{6,4},{8,10},{10,8},{12,14},{14,12},{16,18},{18,... | collective-permute-start | bytes 786440 | tf_op jit(solution)/shard_map/ppermute | solution.py:555
  64.4 1.3 %collective-permute-done.15.refs_6_.refs_4_ = f32[16,8,256]{2,1,0:T(8,128)S(1)} collective-permute-done((f32[16,8,256]{2,1,0:T(8,128)S(1)}, f32[16,8,256]{2,1,0:T(8,128)S(1)}, u32[]{:S(2)}, u32[]{:S(2)}) %collective-permute-start.15) | collective-permute-done | bytes 131104 | tf_op jit(solution)/shard_map/ppermute | solution.py:555
  65.7 3.0 %pressure_steps.6 = (f32[16,2,48,128]{3,2,1,0:T(8,128)S(1)}, f32[8,32,256]{2,1,0:T(8,128)S(1)}, f32[16,2,48,128]{3,2,1,0:T(8,128)S(1)}, f32[8,2,32,128]{3,2,1,0:T(8,128)S(1)}, f32[8,8,256]{2,1,0:T(8,128)S(1)}) custom-call(s32[3]{0:T(128)S(1)} %copy-done.9, f32[8]{0:T(128)S(1)} %copy-done.10, f32[8,32,256]{2,1,0:T(8,128)S(1)} %get-tuple-element.70.refs_2_.p2, ...), custom_call_target="tpu_custom_call" | custom-call | flops 9000000 | bytes 4000000 | tf_op jit(solution)/shard_map/pressure_steps/pallas_call | solution.py:262
  68.6 2.3 %tangent_steps.6 = (f32[16,2,48,128]{3,2,1,0:T(8,128)S(1)}, f32[8,32,256]{2,1,0:T(8,128)S(1)}, f32[16,8,256]{2,1,0:T(8,128)S(1)}, f32[8,8,256]{2,1,0:T(8,128)S(1)}) custom-call(f32[8,32,256]{2,1,0:T(8,128)S(1)} %get-tuple-element.80.refs_0_.q2, f32[8,32,256]{2,1,0:T(8,128)S(1)} %collective-permute-done.19.refs_1_, ...), custom_call_target="tpu_custom_call" | custom-call | flops 9000000 | bytes 4000000 | tf_op jit(solution)/shard_map/tangent_steps/pallas_call | solution.py:285
  71.6 1.2 %collective-permute-start.21 = (f32[16,8,256]{2,1,0:T(8,128)S(1)}, f32[16,8,256]{2,1,0:T(8,128)S(1)}, u32[]{:S(2)}, u32[]{:S(2)}) collective-permute-start(f32[16,8,256]{2,1,0:T(8,128)S(1)} %get-tuple-element.85), channel_id=1, source_target_pairs={{0,1},{1,0},{2,3},{3,2},{4,5},{5,4},{6,7},{7,6},{8,9},{9,8},{10,11... | collective-permute-start | bytes 393224 | tf_op jit(solution)/shard_map/ppermute | solution.py:561
  73.5 8.3 %collective-permute-start.17 = (f32[8,32,256]{2,1,0:T(8,128)S(1)}, f32[8,32,256]{2,1,0:T(8,128)S(1)}, u32[]{:S(2)}, u32[]{:S(2)}) collective-permute-start(f32[8,32,256]{2,1,0:T(8,128)S(1)} %get-tuple-element.79.refs_2_.p2), channel_id=1, source_target_pairs={{0,2},{2,0},{4,6},{6,4},{8,10},{10,8},{12,14},{14,12},{16,18},{18,... | collective-permute-start | bytes 786440 | tf_op jit(solution)/shard_map/ppermute | solution.py:555
  82.6 2.6 %collective-permute-start.24 = (f32[8,32,256]{2,1,0:T(8,128)S(1)}, f32[8,32,256]{2,1,0:T(8,128)S(1)}, u32[]{:S(2)}, u32[]{:S(2)}) collective-permute-start(f32[8,32,256]{2,1,0:T(8,128)S(1)} %get-tuple-element.89.refs_0_.q2), channel_id=1, source_target_pairs={{0,2},{2,0},{4,6},{6,4},{8,10},{10,8},{12,14},{14,12},{16,18},{18,... | collective-permute-start | bytes 786440 | tf_op jit(solution)/shard_map/ppermute | solution.py:555
  87.4 3.5 %pressure_steps.7 = (f32[16,2,48,128]{3,2,1,0:T(8,128)S(1)}, f32[8,32,256]{2,1,0:T(8,128)}, f32[16,2,48,128]{3,2,1,0:T(8,128)S(1)}, f32[8,2,32,128]{3,2,1,0:T(8,128)S(1)}, f32[8,8,256]{2,1,0:T(8,128)S(1)}) custom-call(s32[3]{0:T(128)S(1)} %copy-done.9, f32[8]{0:T(128)S(1)} %copy-done.10, f32[8,32,256]{2,1,0:T(8,128)S(1)} %get-tuple-element.79.refs_2_.p2, ...), custom_call_target="tpu_custom_call" | custom-call | flops 9000000 | bytes 4000000 | tf_op jit(solution)/shard_map/pressure_steps/pallas_call | solution.py:262
  90.9 3.0 %tangent_steps.7 = (f32[16,2,48,128]{3,2,1,0:T(8,128)S(1)}, f32[8,32,256]{2,1,0:T(8,128)}, f32[16,8,256]{2,1,0:T(8,128)}, f32[8,8,256]{2,1,0:T(8,128)}) custom-call(f32[8,32,256]{2,1,0:T(8,128)S(1)} %get-tuple-element.89.refs_0_.q2, f32[8,32,256]{2,1,0:T(8,128)S(1)} %collective-permute-done.24.refs_1_, f32[8,32,256]{2,1,0:T(8,128)S(1)} %collective-permute-done.25.refs_2_, ...), custom_call_target="tpu_custom_call" | custom-call | flops 9000000 | bytes 4000000 | tf_op jit(solution)/shard_map/tangent_steps/pallas_call | solution.py:285
  94.5 0.9 copy-done.8
  95.5 1.4 %receive.7 = (f32[8,128]{1,0:T(8,128)S(1)}, f32[8,128]{1,0:T(8,128)S(1)}, f32[32,1,128]{2,1,0:T(1,128)}) custom-call(s32[1,128]{1,0:T(1,128)S(1)} %bitcast.6, f32[16,2,48,128]{3,2,1,0:T(8,128)S(1)} %get-tuple-element.95.p1, f32[8,32,256]{2,1,0:T(8,128)S(1)} %copy-done.7, f32[16,2,48,128]{3,2,1,0:T(8,128)S(1)} %get-tuple-element.96.q1, ...), custom_call_target="tpu_custom_call" | custom-call | flops 20000000 | bytes 2500000 | tf_op jit(solution)/shard_map/receive/pallas_call | solution.py:452
  96.9 9.0 %all-to-all-start = ((f32[32,1,128]{2,1,0:T(1,128)}), f32[32,1,128]{2,1,0:T(1,128)S(1)}, u32[]{:S(2)}, u32[]{:S(2)}) async-start(f32[32,1,128]{2,1,0:T(1,128)} %get-tuple-element.103), calls=%async_computation | async-start | bytes 32768 | tf_op jit(solution)/shard_map/all_to_all | solution.py:611
  105.9 0.8 smooth.1
  106.7 6.3 %all-to-all-done.sums = f32[32,1,128]{2,1,0:T(1,128)S(1)} async-done(((f32[32,1,128]{2,1,0:T(1,128)}), f32[32,1,128]{2,1,0:T(1,128)S(1)}, u32[]{:S(2)}, u32[]{:S(2)}) %all-to-all-start) | async-done | bytes 16416 | tf_op jit(solution)/shard_map/all_to_all | solution.py:611
  113.0 0.9 finish.1
  (64 shorter events, 12.9 us)
Async XLA Ops:
  4.4 13.2 %copy-start.1 = (f32[8,32,256]{2,1,0:T(8,128)S(1)}, f32[8,32,256]{2,1,0:T(8,128)}, u32[]{:S(2)}) copy-start(f32[8,32,256]{2,1,0:T(8,128)} %speed.5) | copy-start | bytes 786436
  4.4 13.2 %copy-start.5 = (f32[8,32,256]{2,1,0:T(8,128)S(1)}, f32[8,32,256]{2,1,0:T(8,128)}, u32[]{:S(2)}) copy-start(f32[8,32,256]{2,1,0:T(8,128)} %p_prev.3) | copy-start | bytes 786436
  5.7 11.9 %collective-permute-start = (f32[20,32,256]{2,1,0:T(8,128)S(1)}, f32[20,32,256]{2,1,0:T(8,128)S(1)}, u32[]{:S(2)}, u32[]{:S(2)}) collective-permute-start(f32[20,32,256]{2,1,0:T(8,128)S(1)} %get-tuple-element.56), channel_id=1, source_target_pairs={{0,2},{2,0},{4,6},{6,4},{8,10},{10,8},{12,14},{14,12},{16,18},{18,... | collective-permute-start | bytes 1966088 | tf_op jit(solution)/shard_map/ppermute | solution.py:555
  6.2 11.4 %collective-permute-start.1 = (f32[20,32,256]{2,1,0:T(8,128)S(1)}, f32[20,32,256]{2,1,0:T(8,128)S(1)}, u32[]{:S(2)}, u32[]{:S(2)}) collective-permute-start(f32[20,32,256]{2,1,0:T(8,128)S(1)} %get-tuple-element.57), channel_id=1, source_target_pairs={{2,4},{4,2},{6,8},{8,6},{10,12},{12,10},{14,16},{16,14},{18,20},{2... | collective-permute-start | bytes 1966088 | tf_op jit(solution)/shard_map/ppermute | solution.py:558
  6.9 7.3 %collective-permute-start.2 = (f32[32,8,256]{2,1,0:T(8,128)S(1)}, f32[32,8,256]{2,1,0:T(8,128)S(1)}, u32[]{:S(2)}, u32[]{:S(2)}) collective-permute-start(f32[32,8,256]{2,1,0:T(8,128)S(1)} %get-tuple-element.58), channel_id=1, source_target_pairs={{0,1},{1,0},{2,3},{3,2},{4,5},{5,4},{6,7},{7,6},{8,9},{9,8},{10,11... | collective-permute-start | bytes 786440 | tf_op jit(solution)/shard_map/ppermute | solution.py:561
  14.3 3.4 %collective-permute-start.3 = (f32[32,8,256]{2,1,0:T(8,128)S(1)}, f32[32,8,256]{2,1,0:T(8,128)S(1)}, u32[]{:S(2)}, u32[]{:S(2)}) collective-permute-start(f32[32,8,256]{2,1,0:T(8,128)S(1)} %collective-permute-done.2.refs_0_.refs_5_), channel_id=1, source_target_pairs={{0,2},{2,0},{4,6},{6,4},{8,10},{10,8},{12,14},{14,12},{16,18},{18,... | collective-permute-start | bytes 786440 | tf_op jit(solution)/shard_map/ppermute | solution.py:555
  16.5 1.4 %copy-start.3 = (f32[8,32,256]{2,1,0:T(8,128)S(1)}, f32[8,32,256]{2,1,0:T(8,128)}, u32[]{:S(2)}) copy-start(f32[8,32,256]{2,1,0:T(8,128)} %refs_2_.1) | copy-start | bytes 786436
  16.5 0.8 collective-permute-start.4
  22.0 17.7 %collective-permute-start.9 = (f32[8,8,256]{2,1,0:T(8,128)S(1)}, f32[8,8,256]{2,1,0:T(8,128)S(1)}, u32[]{:S(2)}, u32[]{:S(2)}) collective-permute-start(f32[8,8,256]{2,1,0:T(8,128)S(1)} %get-tuple-element.68), channel_id=1, source_target_pairs={{2,5},{3,4},{4,3},{5,2},{6,9},{7,8},{8,7},{9,6},{10,13},{11,12},{1... | collective-permute-start | bytes 196616 | tf_op jit(solution)/shard_map/ppermute | solution.py:563
  22.7 19.9 %collective-permute-start.7 = (f32[16,8,256]{2,1,0:T(8,128)S(1)}, f32[16,8,256]{2,1,0:T(8,128)S(1)}, u32[]{:S(2)}, u32[]{:S(2)}) collective-permute-start(f32[16,8,256]{2,1,0:T(8,128)S(1)} %get-tuple-element.67), channel_id=1, source_target_pairs={{0,1},{1,0},{2,3},{3,2},{4,5},{5,4},{6,7},{7,6},{8,9},{9,8},{10,11... | collective-permute-start | bytes 393224 | tf_op jit(solution)/shard_map/ppermute | solution.py:561
  24.7 19.2 %collective-permute-start.6 = (f32[8,32,256]{2,1,0:T(8,128)S(1)}, f32[8,32,256]{2,1,0:T(8,128)S(1)}, u32[]{:S(2)}, u32[]{:S(2)}) collective-permute-start(f32[8,32,256]{2,1,0:T(8,128)S(1)} %get-tuple-element.63.refs_2_.p2), channel_id=1, source_target_pairs={{2,4},{4,2},{6,8},{8,6},{10,12},{12,10},{14,16},{16,14},{18,20},{2... | collective-permute-start | bytes 786440 | tf_op jit(solution)/shard_map/ppermute | solution.py:558
  25.4 18.5 %collective-permute-start.5 = (f32[8,32,256]{2,1,0:T(8,128)S(1)}, f32[8,32,256]{2,1,0:T(8,128)S(1)}, u32[]{:S(2)}, u32[]{:S(2)}) collective-permute-start(f32[8,32,256]{2,1,0:T(8,128)S(1)} %get-tuple-element.63.refs_2_.p2), channel_id=1, source_target_pairs={{0,2},{2,0},{4,6},{6,4},{8,10},{10,8},{12,14},{14,12},{16,18},{18,... | collective-permute-start | bytes 786440 | tf_op jit(solution)/shard_map/ppermute | solution.py:555
  39.0 7.8 %collective-permute-start.13 = (f32[8,32,256]{2,1,0:T(8,128)S(1)}, f32[8,32,256]{2,1,0:T(8,128)S(1)}, u32[]{:S(2)}, u32[]{:S(2)}) collective-permute-start(f32[8,32,256]{2,1,0:T(8,128)S(1)} %get-tuple-element.71.refs_0_.q2), channel_id=1, source_target_pairs={{2,4},{4,2},{6,8},{8,6},{10,12},{12,10},{14,16},{16,14},{18,20},{2... | collective-permute-start | bytes 786440 | tf_op jit(solution)/shard_map/ppermute | solution.py:558
  39.7 7.1 %collective-permute-start.12 = (f32[8,32,256]{2,1,0:T(8,128)S(1)}, f32[8,32,256]{2,1,0:T(8,128)S(1)}, u32[]{:S(2)}, u32[]{:S(2)}) collective-permute-start(f32[8,32,256]{2,1,0:T(8,128)S(1)} %get-tuple-element.71.refs_0_.q2), channel_id=1, source_target_pairs={{0,2},{2,0},{4,6},{6,4},{8,10},{10,8},{12,14},{14,12},{16,18},{18,... | collective-permute-start | bytes 786440 | tf_op jit(solution)/shard_map/ppermute | solution.py:555
  42.6 1.3 %collective-permute-start.8 = (f32[16,8,256]{2,1,0:T(8,128)S(1)}, f32[16,8,256]{2,1,0:T(8,128)S(1)}, u32[]{:S(2)}, u32[]{:S(2)}) collective-permute-start(f32[16,8,256]{2,1,0:T(8,128)S(1)} %collective-permute-done.7.refs_5_.refs_3_), channel_id=1, source_target_pairs={{0,2},{2,0},{4,6},{6,4},{8,10},{10,8},{12,14},{14,12},{16,18},{18,... | collective-permute-start | bytes 393224 | tf_op jit(solution)/shard_map/ppermute | solution.py:555
  49.0 12.2 %collective-permute-start.16 = (f32[8,8,256]{2,1,0:T(8,128)S(1)}, f32[8,8,256]{2,1,0:T(8,128)S(1)}, u32[]{:S(2)}, u32[]{:S(2)}) collective-permute-start(f32[8,8,256]{2,1,0:T(8,128)S(1)} %get-tuple-element.77), channel_id=1, source_target_pairs={{2,5},{3,4},{4,3},{5,2},{6,9},{7,8},{8,7},{9,6},{10,13},{11,12},{1... | collective-permute-start | bytes 196616 | tf_op jit(solution)/shard_map/ppermute | solution.py:563
  49.7 14.6 %collective-permute-start.14 = (f32[16,8,256]{2,1,0:T(8,128)S(1)}, f32[16,8,256]{2,1,0:T(8,128)S(1)}, u32[]{:S(2)}, u32[]{:S(2)}) collective-permute-start(f32[16,8,256]{2,1,0:T(8,128)S(1)} %get-tuple-element.76), channel_id=1, source_target_pairs={{0,1},{1,0},{2,3},{3,2},{4,5},{5,4},{6,7},{7,6},{8,9},{9,8},{10,11... | collective-permute-start | bytes 393224 | tf_op jit(solution)/shard_map/ppermute | solution.py:561
  51.8 13.9 %collective-permute-start.11 = (f32[8,32,256]{2,1,0:T(8,128)S(1)}, f32[8,32,256]{2,1,0:T(8,128)S(1)}, u32[]{:S(2)}, u32[]{:S(2)}) collective-permute-start(f32[8,32,256]{2,1,0:T(8,128)S(1)} %get-tuple-element.70.refs_2_.p2), channel_id=1, source_target_pairs={{2,4},{4,2},{6,8},{8,6},{10,12},{12,10},{14,16},{16,14},{18,20},{2... | collective-permute-start | bytes 786440 | tf_op jit(solution)/shard_map/ppermute | solution.py:558
  52.5 13.2 %collective-permute-start.10 = (f32[8,32,256]{2,1,0:T(8,128)S(1)}, f32[8,32,256]{2,1,0:T(8,128)S(1)}, u32[]{:S(2)}, u32[]{:S(2)}) collective-permute-start(f32[8,32,256]{2,1,0:T(8,128)S(1)} %get-tuple-element.70.refs_2_.p2), channel_id=1, source_target_pairs={{0,2},{2,0},{4,6},{6,4},{8,10},{10,8},{12,14},{14,12},{16,18},{18,... | collective-permute-start | bytes 786440 | tf_op jit(solution)/shard_map/ppermute | solution.py:555
  60.6 8.1 %collective-permute-start.20 = (f32[8,32,256]{2,1,0:T(8,128)S(1)}, f32[8,32,256]{2,1,0:T(8,128)S(1)}, u32[]{:S(2)}, u32[]{:S(2)}) collective-permute-start(f32[8,32,256]{2,1,0:T(8,128)S(1)} %get-tuple-element.80.refs_0_.q2), channel_id=1, source_target_pairs={{2,4},{4,2},{6,8},{8,6},{10,12},{12,10},{14,16},{16,14},{18,20},{2... | collective-permute-start | bytes 786440 | tf_op jit(solution)/shard_map/ppermute | solution.py:558
  61.2 7.4 %collective-permute-start.19 = (f32[8,32,256]{2,1,0:T(8,128)S(1)}, f32[8,32,256]{2,1,0:T(8,128)S(1)}, u32[]{:S(2)}, u32[]{:S(2)}) collective-permute-start(f32[8,32,256]{2,1,0:T(8,128)S(1)} %get-tuple-element.80.refs_0_.q2), channel_id=1, source_target_pairs={{0,2},{2,0},{4,6},{6,4},{8,10},{10,8},{12,14},{14,12},{16,18},{18,... | collective-permute-start | bytes 786440 | tf_op jit(solution)/shard_map/ppermute | solution.py:555
  64.3 1.3 %collective-permute-start.15 = (f32[16,8,256]{2,1,0:T(8,128)S(1)}, f32[16,8,256]{2,1,0:T(8,128)S(1)}, u32[]{:S(2)}, u32[]{:S(2)}) collective-permute-start(f32[16,8,256]{2,1,0:T(8,128)S(1)} %collective-permute-done.14.refs_5_.refs_3_), channel_id=1, source_target_pairs={{0,2},{2,0},{4,6},{6,4},{8,10},{10,8},{12,14},{14,12},{16,18},{18,... | collective-permute-start | bytes 393224 | tf_op jit(solution)/shard_map/ppermute | solution.py:555
  70.9 11.7 %collective-permute-start.23 = (f32[8,8,256]{2,1,0:T(8,128)S(1)}, f32[8,8,256]{2,1,0:T(8,128)S(1)}, u32[]{:S(2)}, u32[]{:S(2)}) collective-permute-start(f32[8,8,256]{2,1,0:T(8,128)S(1)} %get-tuple-element.86), channel_id=1, source_target_pairs={{2,5},{3,4},{4,3},{5,2},{6,9},{7,8},{8,7},{9,6},{10,13},{11,12},{1... | collective-permute-start | bytes 196616 | tf_op jit(solution)/shard_map/ppermute | solution.py:563
  71.6 13.7 %collective-permute-start.21 = (f32[16,8,256]{2,1,0:T(8,128)S(1)}, f32[16,8,256]{2,1,0:T(8,128)S(1)}, u32[]{:S(2)}, u32[]{:S(2)}) collective-permute-start(f32[16,8,256]{2,1,0:T(8,128)S(1)} %get-tuple-element.85), channel_id=1, source_target_pairs={{0,1},{1,0},{2,3},{3,2},{4,5},{5,4},{6,7},{7,6},{8,9},{9,8},{10,11... | collective-permute-start | bytes 393224 | tf_op jit(solution)/shard_map/ppermute | solution.py:561
  72.8 14.5 %collective-permute-start.18 = (f32[8,32,256]{2,1,0:T(8,128)S(1)}, f32[8,32,256]{2,1,0:T(8,128)S(1)}, u32[]{:S(2)}, u32[]{:S(2)}) collective-permute-start(f32[8,32,256]{2,1,0:T(8,128)S(1)} %get-tuple-element.79.refs_2_.p2), channel_id=1, source_target_pairs={{2,4},{4,2},{6,8},{8,6},{10,12},{12,10},{14,16},{16,14},{18,20},{2... | collective-permute-start | bytes 786440 | tf_op jit(solution)/shard_map/ppermute | solution.py:558
  73.5 13.9 %collective-permute-start.17 = (f32[8,32,256]{2,1,0:T(8,128)S(1)}, f32[8,32,256]{2,1,0:T(8,128)S(1)}, u32[]{:S(2)}, u32[]{:S(2)}) collective-permute-start(f32[8,32,256]{2,1,0:T(8,128)S(1)} %get-tuple-element.79.refs_2_.p2), channel_id=1, source_target_pairs={{0,2},{2,0},{4,6},{6,4},{8,10},{10,8},{12,14},{14,12},{16,18},{18,... | collective-permute-start | bytes 786440 | tf_op jit(solution)/shard_map/ppermute | solution.py:555
  81.8 3.5 %copy-start.11 = (s32[1,1,128]{2,1,0:T(1,128)S(1)}, s32[1,1,128]{2,1,0:T(1,128)}, u32[]{:S(2)}) copy-start(s32[1,1,128]{2,1,0:T(1,128)} %param.14) | copy-start | bytes 1540
  81.8 9.0 %collective-permute-start.25 = (f32[8,32,256]{2,1,0:T(8,128)S(1)}, f32[8,32,256]{2,1,0:T(8,128)S(1)}, u32[]{:S(2)}, u32[]{:S(2)}) collective-permute-start(f32[8,32,256]{2,1,0:T(8,128)S(1)} %get-tuple-element.89.refs_0_.q2), channel_id=1, source_target_pairs={{2,4},{4,2},{6,8},{8,6},{10,12},{12,10},{14,16},{16,14},{18,20},{2... | collective-permute-start | bytes 786440 | tf_op jit(solution)/shard_map/ppermute | solution.py:558
  82.6 8.2 %collective-permute-start.24 = (f32[8,32,256]{2,1,0:T(8,128)S(1)}, f32[8,32,256]{2,1,0:T(8,128)S(1)}, u32[]{:S(2)}, u32[]{:S(2)}) collective-permute-start(f32[8,32,256]{2,1,0:T(8,128)S(1)} %get-tuple-element.89.refs_0_.q2), channel_id=1, source_target_pairs={{0,2},{2,0},{4,6},{6,4},{8,10},{10,8},{12,14},{14,12},{16,18},{18,... | collective-permute-start | bytes 786440 | tf_op jit(solution)/shard_map/ppermute | solution.py:555
  85.3 2.1 %collective-permute-start.22 = (f32[16,8,256]{2,1,0:T(8,128)S(1)}, f32[16,8,256]{2,1,0:T(8,128)S(1)}, u32[]{:S(2)}, u32[]{:S(2)}) collective-permute-start(f32[16,8,256]{2,1,0:T(8,128)S(1)} %collective-permute-done.21.refs_5_.refs_3_), channel_id=1, source_target_pairs={{0,2},{2,0},{4,6},{6,4},{8,10},{10,8},{12,14},{14,12},{16,18},{18,... | collective-permute-start | bytes 393224 | tf_op jit(solution)/shard_map/ppermute | solution.py:555
  90.9 3.0 %copy-start.7 = (f32[8,32,256]{2,1,0:T(8,128)S(1)}, f32[8,32,256]{2,1,0:T(8,128)}, u32[]{:S(2)}) copy-start(f32[8,32,256]{2,1,0:T(8,128)} %get-tuple-element.52.p2) | copy-start | bytes 786436
  96.9 16.1 %all-to-all-start = ((f32[32,1,128]{2,1,0:T(1,128)}), f32[32,1,128]{2,1,0:T(1,128)S(1)}, u32[]{:S(2)}, u32[]{:S(2)}) async-start(f32[32,1,128]{2,1,0:T(1,128)} %get-tuple-element.103), calls=%async_computation | async-start | bytes 32768 | tf_op jit(solution)/shard_map/all_to_all | solution.py:611
  (8 other events, 6.8 us)

commit v3 on v2

--- a/solution.py
+++ b/solution.py
@@ -13,7 +13,6 @@
 F32 = jnp.float32
 
 VMEM = pl.BlockSpec(memory_space=pltpu.VMEM)
-SMEM = pl.BlockSpec(memory_space=pltpu.SMEM)
 
 
 def struct(*shape):
@@ -129,7 +128,13 @@
     refs = list(refs)
     scalars = parity()
     if not tangent:
-        source, wave = refs[:2]
+        sems, source, wave = refs.pop(), refs.pop(-2), refs.pop()
+        small = [
+            pltpu.make_async_copy(refs[0], source, sems.at[0]),
+            pltpu.make_async_copy(refs[1], wave, sems.at[1]),
+        ]
+        for copy in small:
+            copy.start()
         refs = refs[2:]
     if not blank:
         own, near, far = refs[:3]
@@ -200,6 +205,8 @@
         next1[...] = drive1[...]
 
     if not tangent:
+        for copy in small:
+            copy.wait()
         src_x = source[0] - lax.axis_index("gx") * size_x
         src_y = source[1] - lax.axis_index("gy") * size_y
         src_z = source[2]
@@ -262,11 +269,16 @@
     out = pl.pallas_call(
         functools.partial(step_pair_kernel, count, False, False, at),
         out_shape=outs,
-        in_specs=[SMEM, SMEM] + [VMEM] * len(args),
+        in_specs=[pl.BlockSpec(memory_space=pl.ANY)] * 2 + [VMEM] * len(args),
         out_specs=[VMEM] * len(outs),
-        scratch_shapes=[wide_shape(shape)],
+        scratch_shapes=[
+            wide_shape(shape),
+            pltpu.SMEM(source.shape, jnp.int32),
+            pltpu.SMEM(wave.shape, F32),
+            pltpu.SemaphoreType.DMA((2,)),
+        ],
         compiler_params=params(),
-        cost_estimate=cost(9_000_000, 4_000_000),
+        cost_estimate=cost(900_000_000, 400_000_000),
         name="pressure_steps",
     )(source, wave, *args)
     return out[0], out[1], out[2], out[3], list(out[4:])
@@ -289,7 +301,7 @@
         out_specs=[VMEM] * len(outs),
         scratch_shapes=[] if blank else [wide_shape(shape)],
         compiler_params=params(),
-        cost_estimate=cost(9_000_000, 4_000_000),
+        cost_estimate=cost(900_000_000, 400_000_000),
         name="tangent_steps",
     )(*args)
     return out[0], out[1], list(out[2 : 2 + count]), list(out[2 + count :])
@@ -303,9 +315,8 @@
     near_face = pl.ds((size_x - 4) * (1 - par_x), 4)
     moves = []
     for target, face in ((far, far_face), (near, near_face)):
-        moves.append((p_now, target.at[0:size_x]))
         for k, field in enumerate((p_prev, speed, perturb)):
-            start = size_x + 4 * k
+            start = 4 * k
             moves.append((field.at[face], target.at[start : start + 4]))
     for which in range(count):
         high = 1 - par_y if which == 0 else par_y
@@ -324,7 +335,7 @@
 
 
 def pack(shape, count, p_now, p_prev, speed, perturb):
-    outs = [struct(shape[0] + 12, shape[1], shape[2])] * 2
+    outs = [struct(12, shape[1], shape[2])] * 2
     outs += [struct(4 * shape[0], 8, shape[2])] * count
     outs += [struct(8, 8, shape[2])] * count
     out = pl.pallas_call(
@@ -332,15 +343,15 @@
         out_shape=outs,
         in_specs=[pl.BlockSpec(memory_space=pl.ANY)] * 4,
         out_specs=[VMEM] * len(outs),
-        scratch_shapes=[pltpu.SemaphoreType.DMA((8 + 6 * count,))],
-        compiler_params=params(),
+        scratch_shapes=[pltpu.SemaphoreType.DMA((6 + 6 * count,))],
+        compiler_params=pltpu.CompilerParams(vmem_limit_bytes=58 * 1024 * 1024),
         cost_estimate=cost(10_000, 3_000_000),
         name="pack",
     )(p_now, p_prev, speed, perturb)
     return out[0], out[1], list(out[2 : 2 + count]), list(out[2 + count :])
 
 
-def gather_ring_kernel(count, p_prev, speed, perturb, near, far, *refs):
+def gather_ring_kernel(count, p_prev, speed, perturb, near, far, _, *refs):
     strips, refs = refs[:count], refs[count:]
     near_strips, refs = refs[:count], refs[count:]
     corners, targets = refs[:count], refs[count:]
@@ -351,7 +362,7 @@
     far_at = (size_x + 4) * par_x
     for k, (own, target) in enumerate(zip((p_prev, speed, perturb), targets)):
         put(target, slice(4, 4 + size_x), inner, own[...])
-        face = slice(size_x + 4 * k, size_x + 4 * k + 4)
+        face = slice(4 * k, 4 * k + 4)
         put(target, pl.ds(near_at, 4), inner, near[face])
         put(target, pl.ds(far_at, 4), inner, far[face])
         part = (2, 3, 1)[k]
@@ -374,8 +385,8 @@
             pl.when(par_y == side)(functools.partial(fill, 1))
 
 
-def gather_ring(shape, count, fields, near, far, strips, near_strips, corners):
-    args = [*fields, near, far, *strips, *near_strips, *corners]
+def gather_ring(shape, count, fields, near, far, p_far, strips, near_strips, corners):
+    args = [*fields, near, far, p_far, *strips, *near_strips, *corners]
     return pl.pallas_call(
         functools.partial(gather_ring_kernel, count),
         out_shape=[ring_struct(shape)] * 3,
@@ -389,7 +400,11 @@
 
 def receive_kernel(rounds, cells, p1, p2, q1, q2, *refs):
     size_x, size_y, size_z = p2.shape
-    if rounds:
+    if rounds == 0:
+        observed, refs = refs[0], refs[1:]
+        refs[2][...] = observed[...]
+        synth, born = refs[:2]
+    elif rounds > 0:
         earlier, observed = refs[: 2 * rounds], refs[2 * rounds]
         synth, born, spread = refs[2 * rounds + 1 :]
     else:
@@ -429,7 +444,7 @@
         target[steps - 1 : steps, :] = at(second)
 
 
-    if rounds:
+    if rounds > 0:
         for k in range(rounds):
             synth[2 * k : 2 * k + 2, :] = earlier[2 * k][...]
             born[2 * k : 2 * k + 2, :] = earlier[2 * k + 1][...]
@@ -443,10 +458,13 @@
 
 def receive(cells, p1, p2, q1, q2, earlier=(), observed=None, total=0):
     count = cells.shape[1]
-    rounds = len(earlier) // 2
-    outs = [struct(2 * rounds + 2, count)] * 2
+    rounds = len(earlier) // 2 if total else (-1 if observed is None else 0)
+    outs = [struct(2 * max(rounds, 0) + 2, count)] * 2
     args = [cells, p1, p2, q1, q2]
-    if rounds:
+    if rounds == 0:
+        outs.append(struct(*observed.shape))
+        args.append(observed)
+    elif rounds > 0:
         outs.append(struct(total, 1, LANES))
         args += [*earlier, observed]
     return pl.pallas_call(
@@ -495,7 +513,13 @@
     )(sums, residual, born, speed, smooth)
 
 
-def smooth_kernel(perturb, smooth):
+def smooth_kernel(perturb, p_in, q_in, smooth, p_out, q_out, sems):
+    copies = [
+        pltpu.make_async_copy(p_in, p_out, sems.at[0]),
+        pltpu.make_async_copy(q_in, q_out, sems.at[1]),
+    ]
+    for copy in copies:
+        copy.start()
     size_x, size_y, _ = smooth.shape
     lane = lax.broadcasted_iota(jnp.int32, (size_y, LANES), 1)
 
@@ -523,18 +547,21 @@
         return carry
 
     lax.fori_loop(0, size_x, layer_step, 0)
-
-
-def smoothed(shape, perturb):
+    for copy in copies:
+        copy.wait()
+
+
+def smoothed(shape, perturb, p_now, q_now):
     return pl.pallas_call(
         smooth_kernel,
-        out_shape=struct(*shape),
-        in_specs=[VMEM],
-        out_specs=VMEM,
+        out_shape=[struct(*shape)] * 3,
+        in_specs=[VMEM] * 3,
+        out_specs=[VMEM] + [pl.BlockSpec(memory_space=pl.ANY)] * 2,
+        scratch_shapes=[pltpu.SemaphoreType.DMA((2,))],
         compiler_params=params(),
-        cost_estimate=cost(1_000_000, 1_200_000),
+        cost_estimate=cost(1_000_000, 2_200_000),
         name="smooth",
-    )(perturb)
+    )(perturb, p_now, q_now)
 
 
 def on_device(
@@ -564,6 +591,7 @@
         ]
         return got, [swap_near(value) for value in got], got_corners
 
+    p_far, p_near = swap_far(pressure_now), swap_near(pressure_now)
     far_send, near_send, strips, corners = pack(
         shape, count, pressure_now, pressure_prev, courant, perturbation
     )
@@ -575,16 +603,16 @@
         (pressure_prev, courant, perturbation),
         near,
         far,
+        p_far,
         strips,
         near_strips,
         corners,
     )
-    smooth = smoothed(shape, perturb)
     cells = rec_cells.reshape(1, -1)
     p_cur, q_cur, q_prev = pressure_now, None, None
-    p_far, p_near = far, near
     q_far = q_near = None
     earlier = []
+    traces = observed.reshape(steps, -1)
     for step in range(0, steps, 2):
         around = (strips, near_strips, corners)
         p_pieces = (p_cur, p_near, p_far) + around
@@ -602,13 +630,17 @@
             strips, near_strips, corners = swap_strips(strips, corners)
             q_far, q_near = swap_far(q_cur), swap_near(q_cur)
         if not last:
-            earlier += receive(cells, p_prev, p_cur, q_prev, q_cur)
+            got = list(receive(cells, p_prev, p_cur, q_prev, q_cur, (), traces))
+            if step == 0:
+                held = got.pop()
+            traces = None
+            earlier += got
     total = count_x * count_y
-    observed_traces = observed.reshape(steps, -1)
     residual, born, spread = receive(
-        cells, p_prev, p_cur, q_prev, q_cur, earlier, observed_traces, total
+        cells, p_prev, p_cur, q_prev, q_cur, earlier, held, total
     )
     sums = lax.all_to_all(spread, AXES, 0, 0)
+    smooth, p_cur, q_cur = smoothed(shape, perturb, p_cur, q_cur)
     predicted, updated_model = finish(sums, residual, born, courant, smooth)
     predicted = predicted.reshape(observed.shape)
     return (p_cur, q_cur, predicted, updated_model)

time: 115 us -> 106 us (0.922)
  local copies, waits for them, and re-layouts: 6.09 us -> 1.33 us
  starting transfers between devices: 66.2 us -> 63.4 us
  Pallas kernels: 26.7 us -> 25.2 us
    unnamed x26 -> x16, local copies, waits for them, and re-layouts: 6.09 us -> 1.33 us
    pallas_call x4, Pallas kernels: 12 us -> 9.36 us  [pressure_steps(): pl.pallas_call(functools.partial(step_pair_kernel, count, False, False, a...]
    ppermute x4, starting transfers between devices: 7.99 us -> 6.53 us  [swap_strips(): lax.ppermute(value, 'gy', pairs)]
    all_to_all x1, starting transfers between devices: 9.02 us -> 7.65 us  [on_device(): sums = lax.all_to_all(spread, AXES, 0, 0)]
    pallas_call x1, Pallas kernels: 1.27 us -> 2.42 us  [pack(): pl.pallas_call(functools.partial(pack_kernel, count), out_shape=outs, in_...]
    ppermute x7 -> x8, starting transfers between devices: 4.81 us -> 5.52 us  [swap_far(): return lax.ppermute(value, 'gx', far_x)]
    ppermute x11 -> x12, waiting for transfers between devices: 2.9 us -> 3.47 us  [swap_near(): return lax.ppermute(value, 'gx', near_x)]
    ppermute x11 -> x12, starting transfers between devices: 41.6 us -> 41.1 us  [swap_near(): return lax.ppermute(value, 'gx', near_x)]
  transfers between devices with their start and end apart: 27 -> 29, of which waited for: 5 -> 5; matrix products, arithmetic and copies ran while one was open for 0% -> 0% of each run, Pallas kernels for 11% -> 10%
where the time goes in v3:
time: 106 us; the launch traced here: 105 us
  starting transfers between devices  63.4 us (60%)
  Pallas kernels  25.2 us (24%)
  waiting for transfers between devices  14.2 us (13%)
  local copies, waits for them, and re-layouts  1.33 us (1%)
  between operations  1.17 us (1%)
    ppermute x12, starting transfers between devices, swap_near(): return lax.ppermute(value, 'gx', near_x)  41.1 us
    pallas_call x4, Pallas kernels, pressure_steps(): pl.pallas_call(functools.partial(step_pair_kernel, count, False, False, a...  9.36 us
    pallas_call x4, Pallas kernels, tangent_steps(): pl.pallas_call(functools.partial(step_pair_kernel, count, True, blank, 0)...  8.09 us
    all_to_all x1, starting transfers between devices, on_device(): sums = lax.all_to_all(spread, AXES, 0, 0)  7.65 us
    ppermute x4, starting transfers between devices, swap_strips(): lax.ppermute(value, 'gy', pairs)  6.53 us
    all_to_all x1, waiting for transfers between devices, on_device(): sums = lax.all_to_all(spread, AXES, 0, 0)  6.25 us
    ppermute x8, starting transfers between devices, swap_far(): return lax.ppermute(value, 'gx', far_x)  5.52 us
    ppermute x4, waiting for transfers between devices, swap_strips(): lax.ppermute(value, 'gy', pairs)  4.47 us
  transfers between devices with their start and end apart: 29, of which 5 were waited for; matrix products, arithmetic and copies ran while one was open for 0% of the time, Pallas kernels for 10%

profile of v3, /device:TPU:0, one launch (start us, length us, event | category | flops | bytes accessed | tf_op | source)
XLA Modules:
  0.0 105.3 jit_solution(15930159261260861689)
XLA Ops:
  0.7 2.4 %pack.1 = (f32[12,32,256]{2,1,0:T(8,128)}, f32[12,32,256]{2,1,0:T(8,128)}, f32[32,8,256]{2,1,0:T(8,128)}, f32[8,8,256]{2,1,0:T(8,128)}) custom-call(f32[8,32,256]{2,1,0:T(8,128)} %refs_2_.1, f32[8,32,256]{2,1,0:T(8,128)} %p_prev.3, f32[8,32,256]{2,1,0:T(8,128)} %speed.5, f32[8,32,256]{2,1,0:T(8,128)} %perturb.3), custom_call_target="tpu_custom_call" | custom-call | flops 10000 | bytes 3000000 | tf_op jit(solution)/shard_map/pack/pallas_call | solution.py:341
  3.1 3.0 %collective-permute-start.3 = (f32[32,8,256]{2,1,0:T(8,128)}, f32[32,8,256]{2,1,0:T(8,128)S(1)}, u32[]{:S(2)}, u32[]{:S(2)}) collective-permute-start(f32[32,8,256]{2,1,0:T(8,128)} %get-tuple-element.62), channel_id=1, source_target_pairs={{0,1},{1,0},{2,3},{3,2},{4,5},{5,4},{6,7},{7,6},{8,9},{9,8},{10,11... | collective-permute-start | bytes 786440 | tf_op jit(solution)/shard_map/ppermute | solution.py:588
  7.5 0.7 collective-permute-start.2
  8.2 4.5 %collective-permute-done.3.refs_0_.refs_5_ = f32[32,8,256]{2,1,0:T(8,128)S(1)} collective-permute-done((f32[32,8,256]{2,1,0:T(8,128)}, f32[32,8,256]{2,1,0:T(8,128)S(1)}, u32[]{:S(2)}, u32[]{:S(2)}) %collective-permute-start.3) | collective-permute-done | bytes 262176 | tf_op jit(solution)/shard_map/ppermute | solution.py:588
  12.6 2.7 %collective-permute-start.4 = (f32[32,8,256]{2,1,0:T(8,128)S(1)}, f32[32,8,256]{2,1,0:T(8,128)S(1)}, u32[]{:S(2)}, u32[]{:S(2)}) collective-permute-start(f32[32,8,256]{2,1,0:T(8,128)S(1)} %collective-permute-done.3.refs_0_.refs_5_), channel_id=1, source_target_pairs={{0,2},{2,0},{4,6},{6,4},{8,10},{10,8},{12,14},{14,12},{16,18},{18,... | collective-permute-start | bytes 786440 | tf_op jit(solution)/shard_map/ppermute | solution.py:582
  15.3 1.2 %collective-permute-start.6 = (f32[8,32,256]{2,1,0:T(8,128)S(1)}, f32[8,32,256]{2,1,0:T(8,128)S(1)}, u32[]{:S(2)}, u32[]{:S(2)}) collective-permute-start(f32[8,32,256]{2,1,0:T(8,128)S(1)} %copy-done.3), channel_id=1, source_target_pairs={{0,2},{2,0},{4,6},{6,4},{8,10},{10,8},{12,14},{14,12},{16,18},{18,... | collective-permute-start | bytes 786440 | tf_op jit(solution)/shard_map/ppermute | solution.py:582
  16.7 0.9 collective-permute-done.6.refs_3_
  18.3 2.3 %pressure_steps.4 = (f32[16,2,48,128]{3,2,1,0:T(8,128)S(1)}, f32[8,32,256]{2,1,0:T(8,128)S(1)}, f32[16,2,48,128]{3,2,1,0:T(8,128)S(1)}, f32[8,2,32,128]{3,2,1,0:T(8,128)S(1)}, f32[8,8,256]{2,1,0:T(8,128)S(1)}) custom-call(s32[3]{0:T(128)S(1)} %copy-done.4, f32[8]{0:T(128)S(1)} %copy-done.5, f32[8,32,256]{2,1,0:T(8,128)S(1)} %copy-done.3, ...), custom_call_target="tpu_custom_call" | custom-call | flops 900000000 | bytes 400000000 | tf_op jit(solution)/shard_map/pressure_steps/pallas_call | solution.py:269
  20.6 0.7 collective-permute-start.8
  21.3 12.2 %collective-permute-start.7 = (f32[8,32,256]{2,1,0:T(8,128)S(1)}, f32[8,32,256]{2,1,0:T(8,128)S(1)}, u32[]{:S(2)}, u32[]{:S(2)}) collective-permute-start(f32[8,32,256]{2,1,0:T(8,128)S(1)} %get-tuple-element.67.refs_2_.p2), channel_id=1, source_target_pairs={{0,2},{2,0},{4,6},{6,4},{8,10},{10,8},{12,14},{14,12},{16,18},{18,... | collective-permute-start | bytes 786440 | tf_op jit(solution)/shard_map/ppermute | solution.py:582
  36.1 5.0 %collective-permute-start.14 = (f32[8,32,256]{2,1,0:T(8,128)S(1)}, f32[8,32,256]{2,1,0:T(8,128)S(1)}, u32[]{:S(2)}, u32[]{:S(2)}) collective-permute-start(f32[8,32,256]{2,1,0:T(8,128)S(1)} %get-tuple-element.75.refs_0_.q2), channel_id=1, source_target_pairs={{0,2},{2,0},{4,6},{6,4},{8,10},{10,8},{12,14},{14,12},{16,18},{18,... | collective-permute-start | bytes 786440 | tf_op jit(solution)/shard_map/ppermute | solution.py:582
  41.1 1.3 %collective-permute-done.10.refs_6_.refs_4_ = f32[16,8,256]{2,1,0:T(8,128)S(1)} collective-permute-done((f32[16,8,256]{2,1,0:T(8,128)S(1)}, f32[16,8,256]{2,1,0:T(8,128)S(1)}, u32[]{:S(2)}, u32[]{:S(2)}) %collective-permute-start.10) | collective-permute-done | bytes 131104 | tf_op jit(solution)/shard_map/ppermute | solution.py:582
  42.4 2.3 %pressure_steps.5 = (f32[16,2,48,128]{3,2,1,0:T(8,128)S(1)}, f32[8,32,256]{2,1,0:T(8,128)S(1)}, f32[16,2,48,128]{3,2,1,0:T(8,128)S(1)}, f32[8,2,32,128]{3,2,1,0:T(8,128)S(1)}, f32[8,8,256]{2,1,0:T(8,128)S(1)}) custom-call(s32[3]{0:T(128)S(1)} %copy-done.4, f32[8]{0:T(128)S(1)} %copy-done.5, f32[8,32,256]{2,1,0:T(8,128)S(1)} %get-tuple-element.67.refs_2_.p2, ...), custom_call_target="tpu_custom_call" | custom-call | flops 900000000 | bytes 400000000 | tf_op jit(solution)/shard_map/pressure_steps/pallas_call | solution.py:269
  44.7 2.3 %tangent_steps.5 = (f32[16,2,48,128]{3,2,1,0:T(8,128)S(1)}, f32[8,32,256]{2,1,0:T(8,128)S(1)}, f32[16,8,256]{2,1,0:T(8,128)S(1)}, f32[8,8,256]{2,1,0:T(8,128)S(1)}) custom-call(f32[8,32,256]{2,1,0:T(8,128)S(1)} %get-tuple-element.75.refs_0_.q2, f32[8,32,256]{2,1,0:T(8,128)S(1)} %collective-permute-done.14.refs_1_, ...), custom_call_target="tpu_custom_call" | custom-call | flops 900000000 | bytes 400000000 | tf_op jit(solution)/shard_map/tangent_steps/pallas_call | solution.py:297
  47.0 1.5 %collective-permute-start.16 = (f32[16,8,256]{2,1,0:T(8,128)S(1)}, f32[16,8,256]{2,1,0:T(8,128)S(1)}, u32[]{:S(2)}, u32[]{:S(2)}) collective-permute-start(f32[16,8,256]{2,1,0:T(8,128)S(1)} %get-tuple-element.80), channel_id=1, source_target_pairs={{0,1},{1,0},{2,3},{3,2},{4,5},{5,4},{6,7},{7,6},{8,9},{9,8},{10,11... | collective-permute-start | bytes 393224 | tf_op jit(solution)/shard_map/ppermute | solution.py:588
  49.1 2.7 %collective-permute-start.12 = (f32[8,32,256]{2,1,0:T(8,128)S(1)}, f32[8,32,256]{2,1,0:T(8,128)S(1)}, u32[]{:S(2)}, u32[]{:S(2)}) collective-permute-start(f32[8,32,256]{2,1,0:T(8,128)S(1)} %get-tuple-element.74.refs_2_.p2), channel_id=1, source_target_pairs={{0,2},{2,0},{4,6},{6,4},{8,10},{10,8},{12,14},{14,12},{16,18},{18,... | collective-permute-start | bytes 786440 | tf_op jit(solution)/shard_map/ppermute | solution.py:582
  52.5 0.7 collective-permute-start.22
  53.2 6.0 %collective-permute-start.21 = (f32[8,32,256]{2,1,0:T(8,128)S(1)}, f32[8,32,256]{2,1,0:T(8,128)S(1)}, u32[]{:S(2)}, u32[]{:S(2)}) collective-permute-start(f32[8,32,256]{2,1,0:T(8,128)S(1)} %get-tuple-element.84.refs_0_.q2), channel_id=1, source_target_pairs={{0,2},{2,0},{4,6},{6,4},{8,10},{10,8},{12,14},{14,12},{16,18},{18,... | collective-permute-start | bytes 786440 | tf_op jit(solution)/shard_map/ppermute | solution.py:582
  59.3 1.3 %collective-permute-done.17.refs_6_.refs_4_ = f32[16,8,256]{2,1,0:T(8,128)S(1)} collective-permute-done((f32[16,8,256]{2,1,0:T(8,128)S(1)}, f32[16,8,256]{2,1,0:T(8,128)S(1)}, u32[]{:S(2)}, u32[]{:S(2)}) %collective-permute-start.17) | collective-permute-done | bytes 131104 | tf_op jit(solution)/shard_map/ppermute | solution.py:582
  60.6 2.5 %pressure_steps.6 = (f32[16,2,48,128]{3,2,1,0:T(8,128)S(1)}, f32[8,32,256]{2,1,0:T(8,128)S(1)}, f32[16,2,48,128]{3,2,1,0:T(8,128)S(1)}, f32[8,2,32,128]{3,2,1,0:T(8,128)S(1)}, f32[8,8,256]{2,1,0:T(8,128)S(1)}) custom-call(s32[3]{0:T(128)S(1)} %copy-done.4, f32[8]{0:T(128)S(1)} %copy-done.5, f32[8,32,256]{2,1,0:T(8,128)S(1)} %get-tuple-element.74.refs_2_.p2, ...), custom_call_target="tpu_custom_call" | custom-call | flops 900000000 | bytes 400000000 | tf_op jit(solution)/shard_map/pressure_steps/pallas_call | solution.py:269
  63.1 2.3 %tangent_steps.6 = (f32[16,2,48,128]{3,2,1,0:T(8,128)S(1)}, f32[8,32,256]{2,1,0:T(8,128)S(1)}, f32[16,8,256]{2,1,0:T(8,128)S(1)}, f32[8,8,256]{2,1,0:T(8,128)S(1)}) custom-call(f32[8,32,256]{2,1,0:T(8,128)S(1)} %get-tuple-element.84.refs_0_.q2, f32[8,32,256]{2,1,0:T(8,128)S(1)} %collective-permute-done.21.refs_1_, ...), custom_call_target="tpu_custom_call" | custom-call | flops 900000000 | bytes 400000000 | tf_op jit(solution)/shard_map/tangent_steps/pallas_call | solution.py:297
  65.3 1.4 %collective-permute-start.23 = (f32[16,8,256]{2,1,0:T(8,128)S(1)}, f32[16,8,256]{2,1,0:T(8,128)S(1)}, u32[]{:S(2)}, u32[]{:S(2)}) collective-permute-start(f32[16,8,256]{2,1,0:T(8,128)S(1)} %get-tuple-element.89), channel_id=1, source_target_pairs={{0,1},{1,0},{2,3},{3,2},{4,5},{5,4},{6,7},{7,6},{8,9},{9,8},{10,11... | collective-permute-start | bytes 393224 | tf_op jit(solution)/shard_map/ppermute | solution.py:588
  66.8 0.8 collective-permute-start.20
  67.6 6.1 %collective-permute-start.19 = (f32[8,32,256]{2,1,0:T(8,128)S(1)}, f32[8,32,256]{2,1,0:T(8,128)S(1)}, u32[]{:S(2)}, u32[]{:S(2)}) collective-permute-start(f32[8,32,256]{2,1,0:T(8,128)S(1)} %get-tuple-element.83.refs_2_.p2), channel_id=1, source_target_pairs={{0,2},{2,0},{4,6},{6,4},{8,10},{10,8},{12,14},{14,12},{16,18},{18,... | collective-permute-start | bytes 786440 | tf_op jit(solution)/shard_map/ppermute | solution.py:582
  75.1 5.1 %collective-permute-start.26 = (f32[8,32,256]{2,1,0:T(8,128)S(1)}, f32[8,32,256]{2,1,0:T(8,128)S(1)}, u32[]{:S(2)}, u32[]{:S(2)}) collective-permute-start(f32[8,32,256]{2,1,0:T(8,128)S(1)} %get-tuple-element.93.refs_0_.q2), channel_id=1, source_target_pairs={{0,2},{2,0},{4,6},{6,4},{8,10},{10,8},{12,14},{14,12},{16,18},{18,... | collective-permute-start | bytes 786440 | tf_op jit(solution)/shard_map/ppermute | solution.py:582
  82.9 2.3 %pressure_steps.7 = (f32[16,2,48,128]{3,2,1,0:T(8,128)S(1)}, f32[8,32,256]{2,1,0:T(8,128)S(1)}, f32[16,2,48,128]{3,2,1,0:T(8,128)S(1)}, f32[8,2,32,128]{3,2,1,0:T(8,128)S(1)}, f32[8,8,256]{2,1,0:T(8,128)S(1)}) custom-call(s32[3]{0:T(128)S(1)} %copy-done.4, f32[8]{0:T(128)S(1)} %copy-done.5, f32[8,32,256]{2,1,0:T(8,128)S(1)} %get-tuple-element.83.refs_2_.p2, ...), custom_call_target="tpu_custom_call" | custom-call | flops 900000000 | bytes 400000000 | tf_op jit(solution)/shard_map/pressure_steps/pallas_call | solution.py:269
  85.2 2.9 %tangent_steps.7 = (f32[16,2,48,128]{3,2,1,0:T(8,128)S(1)}, f32[8,32,256]{2,1,0:T(8,128)S(1)}, f32[16,8,256]{2,1,0:T(8,128)}, f32[8,8,256]{2,1,0:T(8,128)}) custom-call(f32[8,32,256]{2,1,0:T(8,128)S(1)} %get-tuple-element.93.refs_0_.q2, f32[8,32,256]{2,1,0:T(8,128)S(1)} %collective-permute-done.26.refs_1_, ...), custom_call_target="tpu_custom_call" | custom-call | flops 900000000 | bytes 400000000 | tf_op jit(solution)/shard_map/tangent_steps/pallas_call | solution.py:297
  88.1 1.4 %receive.7 = (f32[8,128]{1,0:T(8,128)S(1)}, f32[8,128]{1,0:T(8,128)S(1)}, f32[32,1,128]{2,1,0:T(1,128)}) custom-call(s32[1,128]{1,0:T(1,128)S(1)} %bitcast.6, f32[16,2,48,128]{3,2,1,0:T(8,128)S(1)} %get-tuple-element.101.p1, f32[8,32,256]{2,1,0:T(8,128)S(1)} %get-tuple-element.92.p_in.p2, f32[16,2,48,128]{3,2,1,0:T(8,128)S(1)} %get-tuple-element.102.q1, ...), custom_call_target="tpu_custom_call" | custom-call | flops 20000000 | bytes 2500000 | tf_op jit(solution)/shard_map/receive/pallas_call | solution.py:470
  89.5 7.6 %all-to-all-start = ((f32[32,1,128]{2,1,0:T(1,128)}), f32[32,1,128]{2,1,0:T(1,128)S(1)}, u32[]{:S(2)}, u32[]{:S(2)}) async-start(f32[32,1,128]{2,1,0:T(1,128)} %get-tuple-element.110), calls=%async_computation | async-start | bytes 32768 | tf_op jit(solution)/shard_map/all_to_all | solution.py:642
  97.1 0.9 smooth.1
  98.0 6.2 %all-to-all-done.sums = f32[32,1,128]{2,1,0:T(1,128)S(1)} async-done(((f32[32,1,128]{2,1,0:T(1,128)}), f32[32,1,128]{2,1,0:T(1,128)S(1)}, u32[]{:S(2)}, u32[]{:S(2)}) %all-to-all-start) | async-done | bytes 16416 | tf_op jit(solution)/shard_map/all_to_all | solution.py:642
  104.3 0.9 finish.1
  (58 shorter events, 10.3 us)
Async XLA Ops:
  0.6 15.8 %copy-start = (f32[8,32,256]{2,1,0:T(8,128)S(1)}, f32[8,32,256]{2,1,0:T(8,128)}, u32[]{:S(2)}) copy-start(f32[8,32,256]{2,1,0:T(8,128)} %speed.5) | copy-start | bytes 786436
  0.7 15.8 %copy-start.2 = (f32[8,32,256]{2,1,0:T(8,128)S(1)}, f32[8,32,256]{2,1,0:T(8,128)}, u32[]{:S(2)}) copy-start(f32[8,32,256]{2,1,0:T(8,128)} %perturb.3) | copy-start | bytes 786436
  0.7 15.8 %copy-start.1 = (f32[8,32,256]{2,1,0:T(8,128)S(1)}, f32[8,32,256]{2,1,0:T(8,128)}, u32[]{:S(2)}) copy-start(f32[8,32,256]{2,1,0:T(8,128)} %p_prev.3) | copy-start | bytes 786436
  3.1 9.5 %collective-permute-start.3 = (f32[32,8,256]{2,1,0:T(8,128)}, f32[32,8,256]{2,1,0:T(8,128)S(1)}, u32[]{:S(2)}, u32[]{:S(2)}) collective-permute-start(f32[32,8,256]{2,1,0:T(8,128)} %get-tuple-element.62), channel_id=1, source_target_pairs={{0,1},{1,0},{2,3},{3,2},{4,5},{5,4},{6,7},{7,6},{8,9},{9,8},{10,11... | collective-permute-start | bytes 786440 | tf_op jit(solution)/shard_map/ppermute | solution.py:588
  6.1 10.3 %collective-permute-start = (f32[12,32,256]{2,1,0:T(8,128)}, f32[12,32,256]{2,1,0:T(8,128)S(1)}, u32[]{:S(2)}, u32[]{:S(2)}) collective-permute-start(f32[12,32,256]{2,1,0:T(8,128)} %get-tuple-element.60), channel_id=1, source_target_pairs={{0,2},{2,0},{4,6},{6,4},{8,10},{10,8},{12,14},{14,12},{16,18},{18,... | collective-permute-start | bytes 1179656 | tf_op jit(solution)/shard_map/ppermute | solution.py:582
  6.1 10.3 %collective-permute-start.1 = (f32[12,32,256]{2,1,0:T(8,128)}, f32[12,32,256]{2,1,0:T(8,128)S(1)}, u32[]{:S(2)}, u32[]{:S(2)}) collective-permute-start(f32[12,32,256]{2,1,0:T(8,128)} %get-tuple-element.61), channel_id=1, source_target_pairs={{2,4},{4,2},{6,8},{8,6},{10,12},{12,10},{14,16},{16,14},{18,20},{2... | collective-permute-start | bytes 1179656 | tf_op jit(solution)/shard_map/ppermute | solution.py:585
  6.8 8.5 %collective-permute-start.5 = (f32[8,8,256]{2,1,0:T(8,128)}, f32[8,8,256]{2,1,0:T(8,128)S(1)}, u32[]{:S(2)}, u32[]{:S(2)}) collective-permute-start(f32[8,8,256]{2,1,0:T(8,128)} %get-tuple-element.63), channel_id=1, source_target_pairs={{2,5},{3,4},{4,3},{5,2},{6,9},{7,8},{8,7},{9,6},{10,13},{11,12},{1... | collective-permute-start | bytes 196616 | tf_op jit(solution)/shard_map/ppermute | solution.py:590
  7.5 9.0 %collective-permute-start.2 = (f32[8,32,256]{2,1,0:T(8,128)S(1)}, f32[8,32,256]{2,1,0:T(8,128)S(1)}, u32[]{:S(2)}, u32[]{:S(2)}) collective-permute-start(f32[8,32,256]{2,1,0:T(8,128)S(1)} %copy-done.3), channel_id=1, source_target_pairs={{2,4},{4,2},{6,8},{8,6},{10,12},{12,10},{14,16},{16,14},{18,20},{2... | collective-permute-start | bytes 786440 | tf_op jit(solution)/shard_map/ppermute | solution.py:585
  12.6 3.8 %collective-permute-start.4 = (f32[32,8,256]{2,1,0:T(8,128)S(1)}, f32[32,8,256]{2,1,0:T(8,128)S(1)}, u32[]{:S(2)}, u32[]{:S(2)}) collective-permute-start(f32[32,8,256]{2,1,0:T(8,128)S(1)} %collective-permute-done.3.refs_0_.refs_5_), channel_id=1, source_target_pairs={{0,2},{2,0},{4,6},{6,4},{8,10},{10,8},{12,14},{14,12},{16,18},{18,... | collective-permute-start | bytes 786440 | tf_op jit(solution)/shard_map/ppermute | solution.py:582
  15.3 2.3 %collective-permute-start.6 = (f32[8,32,256]{2,1,0:T(8,128)S(1)}, f32[8,32,256]{2,1,0:T(8,128)S(1)}, u32[]{:S(2)}, u32[]{:S(2)}) collective-permute-start(f32[8,32,256]{2,1,0:T(8,128)S(1)} %copy-done.3), channel_id=1, source_target_pairs={{0,2},{2,0},{4,6},{6,4},{8,10},{10,8},{12,14},{14,12},{16,18},{18,... | collective-permute-start | bytes 786440 | tf_op jit(solution)/shard_map/ppermute | solution.py:582
  20.6 20.5 %collective-permute-start.8 = (f32[8,32,256]{2,1,0:T(8,128)S(1)}, f32[8,32,256]{2,1,0:T(8,128)S(1)}, u32[]{:S(2)}, u32[]{:S(2)}) collective-permute-start(f32[8,32,256]{2,1,0:T(8,128)S(1)} %get-tuple-element.67.refs_2_.p2), channel_id=1, source_target_pairs={{2,4},{4,2},{6,8},{8,6},{10,12},{12,10},{14,16},{16,14},{18,20},{2... | collective-permute-start | bytes 786440 | tf_op jit(solution)/shard_map/ppermute | solution.py:585
  21.3 19.9 %collective-permute-start.7 = (f32[8,32,256]{2,1,0:T(8,128)S(1)}, f32[8,32,256]{2,1,0:T(8,128)S(1)}, u32[]{:S(2)}, u32[]{:S(2)}) collective-permute-start(f32[8,32,256]{2,1,0:T(8,128)S(1)} %get-tuple-element.67.refs_2_.p2), channel_id=1, source_target_pairs={{0,2},{2,0},{4,6},{6,4},{8,10},{10,8},{12,14},{14,12},{16,18},{18,... | collective-permute-start | bytes 786440 | tf_op jit(solution)/shard_map/ppermute | solution.py:582
  34.1 6.9 %collective-permute-start.9 = (f32[16,8,256]{2,1,0:T(8,128)S(1)}, f32[16,8,256]{2,1,0:T(8,128)S(1)}, u32[]{:S(2)}, u32[]{:S(2)}) collective-permute-start(f32[16,8,256]{2,1,0:T(8,128)S(1)} %get-tuple-element.71), channel_id=1, source_target_pairs={{0,1},{1,0},{2,3},{3,2},{4,5},{5,4},{6,7},{7,6},{8,9},{9,8},{10,11... | collective-permute-start | bytes 393224 | tf_op jit(solution)/shard_map/ppermute | solution.py:588
  34.7 1.3 %collective-permute-start.11 = (f32[8,8,256]{2,1,0:T(8,128)S(1)}, f32[8,8,256]{2,1,0:T(8,128)S(1)}, u32[]{:S(2)}, u32[]{:S(2)}) collective-permute-start(f32[8,8,256]{2,1,0:T(8,128)S(1)} %get-tuple-element.72), channel_id=1, source_target_pairs={{2,5},{3,4},{4,3},{5,2},{6,9},{7,8},{8,7},{9,6},{10,13},{11,12},{1... | collective-permute-start | bytes 196616 | tf_op jit(solution)/shard_map/ppermute | solution.py:590
  35.4 9.3 %collective-permute-start.15 = (f32[8,32,256]{2,1,0:T(8,128)S(1)}, f32[8,32,256]{2,1,0:T(8,128)S(1)}, u32[]{:S(2)}, u32[]{:S(2)}) collective-permute-start(f32[8,32,256]{2,1,0:T(8,128)S(1)} %get-tuple-element.75.refs_0_.q2), channel_id=1, source_target_pairs={{2,4},{4,2},{6,8},{8,6},{10,12},{12,10},{14,16},{16,14},{18,20},{2... | collective-permute-start | bytes 786440 | tf_op jit(solution)/shard_map/ppermute | solution.py:585
  36.1 8.6 %collective-permute-start.14 = (f32[8,32,256]{2,1,0:T(8,128)S(1)}, f32[8,32,256]{2,1,0:T(8,128)S(1)}, u32[]{:S(2)}, u32[]{:S(2)}) collective-permute-start(f32[8,32,256]{2,1,0:T(8,128)S(1)} %get-tuple-element.75.refs_0_.q2), channel_id=1, source_target_pairs={{0,2},{2,0},{4,6},{6,4},{8,10},{10,8},{12,14},{14,12},{16,18},{18,... | collective-permute-start | bytes 786440 | tf_op jit(solution)/shard_map/ppermute | solution.py:582
  41.0 1.3 %collective-permute-start.10 = (f32[16,8,256]{2,1,0:T(8,128)S(1)}, f32[16,8,256]{2,1,0:T(8,128)S(1)}, u32[]{:S(2)}, u32[]{:S(2)}) collective-permute-start(f32[16,8,256]{2,1,0:T(8,128)S(1)} %collective-permute-done.9.refs_5_.refs_3_), channel_id=1, source_target_pairs={{0,2},{2,0},{4,6},{6,4},{8,10},{10,8},{12,14},{14,12},{16,18},{18,... | collective-permute-start | bytes 393224 | tf_op jit(solution)/shard_map/ppermute | solution.py:582
  47.0 12.2 %collective-permute-start.16 = (f32[16,8,256]{2,1,0:T(8,128)S(1)}, f32[16,8,256]{2,1,0:T(8,128)S(1)}, u32[]{:S(2)}, u32[]{:S(2)}) collective-permute-start(f32[16,8,256]{2,1,0:T(8,128)S(1)} %get-tuple-element.80), channel_id=1, source_target_pairs={{0,1},{1,0},{2,3},{3,2},{4,5},{5,4},{6,7},{7,6},{8,9},{9,8},{10,11... | collective-permute-start | bytes 393224 | tf_op jit(solution)/shard_map/ppermute | solution.py:588
  48.5 12.1 %collective-permute-start.13 = (f32[8,32,256]{2,1,0:T(8,128)S(1)}, f32[8,32,256]{2,1,0:T(8,128)S(1)}, u32[]{:S(2)}, u32[]{:S(2)}) collective-permute-start(f32[8,32,256]{2,1,0:T(8,128)S(1)} %get-tuple-element.74.refs_2_.p2), channel_id=1, source_target_pairs={{2,4},{4,2},{6,8},{8,6},{10,12},{12,10},{14,16},{16,14},{18,20},{2... | collective-permute-start | bytes 786440 | tf_op jit(solution)/shard_map/ppermute | solution.py:585
  49.1 11.4 %collective-permute-start.12 = (f32[8,32,256]{2,1,0:T(8,128)S(1)}, f32[8,32,256]{2,1,0:T(8,128)S(1)}, u32[]{:S(2)}, u32[]{:S(2)}) collective-permute-start(f32[8,32,256]{2,1,0:T(8,128)S(1)} %get-tuple-element.74.refs_2_.p2), channel_id=1, source_target_pairs={{0,2},{2,0},{4,6},{6,4},{8,10},{10,8},{12,14},{14,12},{16,18},{18,... | collective-permute-start | bytes 786440 | tf_op jit(solution)/shard_map/ppermute | solution.py:582
  51.8 1.3 %collective-permute-start.18 = (f32[8,8,256]{2,1,0:T(8,128)S(1)}, f32[8,8,256]{2,1,0:T(8,128)S(1)}, u32[]{:S(2)}, u32[]{:S(2)}) collective-permute-start(f32[8,8,256]{2,1,0:T(8,128)S(1)} %get-tuple-element.81), channel_id=1, source_target_pairs={{2,5},{3,4},{4,3},{5,2},{6,9},{7,8},{8,7},{9,6},{10,13},{11,12},{1... | collective-permute-start | bytes 196616 | tf_op jit(solution)/shard_map/ppermute | solution.py:590
  52.5 10.5 %collective-permute-start.22 = (f32[8,32,256]{2,1,0:T(8,128)S(1)}, f32[8,32,256]{2,1,0:T(8,128)S(1)}, u32[]{:S(2)}, u32[]{:S(2)}) collective-permute-start(f32[8,32,256]{2,1,0:T(8,128)S(1)} %get-tuple-element.84.refs_0_.q2), channel_id=1, source_target_pairs={{2,4},{4,2},{6,8},{8,6},{10,12},{12,10},{14,16},{16,14},{18,20},{2... | collective-permute-start | bytes 786440 | tf_op jit(solution)/shard_map/ppermute | solution.py:585
  53.2 9.9 %collective-permute-start.21 = (f32[8,32,256]{2,1,0:T(8,128)S(1)}, f32[8,32,256]{2,1,0:T(8,128)S(1)}, u32[]{:S(2)}, u32[]{:S(2)}) collective-permute-start(f32[8,32,256]{2,1,0:T(8,128)S(1)} %get-tuple-element.84.refs_0_.q2), channel_id=1, source_target_pairs={{0,2},{2,0},{4,6},{6,4},{8,10},{10,8},{12,14},{14,12},{16,18},{18,... | collective-permute-start | bytes 786440 | tf_op jit(solution)/shard_map/ppermute | solution.py:582
  59.2 1.3 %collective-permute-start.17 = (f32[16,8,256]{2,1,0:T(8,128)S(1)}, f32[16,8,256]{2,1,0:T(8,128)S(1)}, u32[]{:S(2)}, u32[]{:S(2)}) collective-permute-start(f32[16,8,256]{2,1,0:T(8,128)S(1)} %collective-permute-done.16.refs_5_.refs_3_), channel_id=1, source_target_pairs={{0,2},{2,0},{4,6},{6,4},{8,10},{10,8},{12,14},{14,12},{16,18},{18,... | collective-permute-start | bytes 393224 | tf_op jit(solution)/shard_map/ppermute | solution.py:582
  65.3 14.9 %collective-permute-start.23 = (f32[16,8,256]{2,1,0:T(8,128)S(1)}, f32[16,8,256]{2,1,0:T(8,128)S(1)}, u32[]{:S(2)}, u32[]{:S(2)}) collective-permute-start(f32[16,8,256]{2,1,0:T(8,128)S(1)} %get-tuple-element.89), channel_id=1, source_target_pairs={{0,1},{1,0},{2,3},{3,2},{4,5},{5,4},{6,7},{7,6},{8,9},{9,8},{10,11... | collective-permute-start | bytes 393224 | tf_op jit(solution)/shard_map/ppermute | solution.py:588
  66.8 16.1 %collective-permute-start.20 = (f32[8,32,256]{2,1,0:T(8,128)S(1)}, f32[8,32,256]{2,1,0:T(8,128)S(1)}, u32[]{:S(2)}, u32[]{:S(2)}) collective-permute-start(f32[8,32,256]{2,1,0:T(8,128)S(1)} %get-tuple-element.83.refs_2_.p2), channel_id=1, source_target_pairs={{2,4},{4,2},{6,8},{8,6},{10,12},{12,10},{14,16},{16,14},{18,20},{2... | collective-permute-start | bytes 786440 | tf_op jit(solution)/shard_map/ppermute | solution.py:585
  67.6 15.3 %collective-permute-start.19 = (f32[8,32,256]{2,1,0:T(8,128)S(1)}, f32[8,32,256]{2,1,0:T(8,128)S(1)}, u32[]{:S(2)}, u32[]{:S(2)}) collective-permute-start(f32[8,32,256]{2,1,0:T(8,128)S(1)} %get-tuple-element.83.refs_2_.p2), channel_id=1, source_target_pairs={{0,2},{2,0},{4,6},{6,4},{8,10},{10,8},{12,14},{14,12},{16,18},{18,... | collective-permute-start | bytes 786440 | tf_op jit(solution)/shard_map/ppermute | solution.py:582
  73.7 1.3 %collective-permute-start.25 = (f32[8,8,256]{2,1,0:T(8,128)S(1)}, f32[8,8,256]{2,1,0:T(8,128)S(1)}, u32[]{:S(2)}, u32[]{:S(2)}) collective-permute-start(f32[8,8,256]{2,1,0:T(8,128)S(1)} %get-tuple-element.90), channel_id=1, source_target_pairs={{2,5},{3,4},{4,3},{5,2},{6,9},{7,8},{8,7},{9,6},{10,13},{11,12},{1... | collective-permute-start | bytes 196616 | tf_op jit(solution)/shard_map/ppermute | solution.py:590
  74.4 10.8 %collective-permute-start.27 = (f32[8,32,256]{2,1,0:T(8,128)S(1)}, f32[8,32,256]{2,1,0:T(8,128)S(1)}, u32[]{:S(2)}, u32[]{:S(2)}) collective-permute-start(f32[8,32,256]{2,1,0:T(8,128)S(1)} %get-tuple-element.93.refs_0_.q2), channel_id=1, source_target_pairs={{2,4},{4,2},{6,8},{8,6},{10,12},{12,10},{14,16},{16,14},{18,20},{2... | collective-permute-start | bytes 786440 | tf_op jit(solution)/shard_map/ppermute | solution.py:585
  75.1 10.1 %collective-permute-start.26 = (f32[8,32,256]{2,1,0:T(8,128)S(1)}, f32[8,32,256]{2,1,0:T(8,128)S(1)}, u32[]{:S(2)}, u32[]{:S(2)}) collective-permute-start(f32[8,32,256]{2,1,0:T(8,128)S(1)} %get-tuple-element.93.refs_0_.q2), channel_id=1, source_target_pairs={{0,2},{2,0},{4,6},{6,4},{8,10},{10,8},{12,14},{14,12},{16,18},{18,... | collective-permute-start | bytes 786440 | tf_op jit(solution)/shard_map/ppermute | solution.py:582
  80.2 2.6 %collective-permute-start.24 = (f32[16,8,256]{2,1,0:T(8,128)S(1)}, f32[16,8,256]{2,1,0:T(8,128)S(1)}, u32[]{:S(2)}, u32[]{:S(2)}) collective-permute-start(f32[16,8,256]{2,1,0:T(8,128)S(1)} %collective-permute-done.23.refs_5_.refs_3_), channel_id=1, source_target_pairs={{0,2},{2,0},{4,6},{6,4},{8,10},{10,8},{12,14},{14,12},{16,18},{18,... | collective-permute-start | bytes 393224 | tf_op jit(solution)/shard_map/ppermute | solution.py:582
  89.5 14.8 %all-to-all-start = ((f32[32,1,128]{2,1,0:T(1,128)}), f32[32,1,128]{2,1,0:T(1,128)S(1)}, u32[]{:S(2)}, u32[]{:S(2)}) async-start(f32[32,1,128]{2,1,0:T(1,128)} %get-tuple-element.110), calls=%async_computation | async-start | bytes 32768 | tf_op jit(solution)/shard_map/all_to_all | solution.py:642
  (5 other events, 22.3 us)

commit v4 on v3

--- a/solution.py
+++ b/solution.py
@@ -136,7 +136,10 @@
         for copy in small:
             copy.start()
         refs = refs[2:]
-    if not blank:
+    if tangent and not blank:
+        wide, prev = refs[:2]
+        refs = refs[2:]
+    elif not blank:
         own, near, far = refs[:3]
         refs = refs[3:]
         strips, refs = refs[:count], refs[count:]
@@ -166,10 +169,9 @@
         return lax.broadcasted_iota(jnp.int32, (rows, LANES), 1)
 
     if not blank:
-        wide = refs.pop(0)
-        place_wide(
-            wide, scalars, own, near, far, strips, near_strips, corners, 1 if tangent else 0
-        )
+        if not tangent:
+            wide = refs.pop(0)
+            place_wide(wide, scalars, own, near, far, strips, near_strips, corners, 0)
 
         def advance(layer, start, rows):
             laps = laplace(wide, layer + 4, start + 8, rows, lanes(rows))
@@ -250,6 +252,11 @@
             corner_out[which][0:4] = partner_strips[which][facing]
             strip = strip_out[which][pl.ds(size_x + (size_x - 4) * par_x, 4)]
             corner_out[which][4:8] = strip
+
+
+def place_kernel(count, own, near, far, *refs):
+    strips, near_strips, corners = (refs[k * count : (k + 1) * count] for k in range(3))
+    place_wide(refs[-1], parity(), own, near, far, strips, near_strips, corners, 1)
 
 
 def wide_shape(shape):
@@ -291,15 +298,24 @@
     outs += [struct(8, 8, shape[2])] * count
     args = []
     if not blank:
-        own, near, far, strips, near_strips, corners = pieces
-        args = [own, near, far, *strips, *near_strips, *corners, prev]
+        own, near, far, strips, near_strips, corners, done = pieces
+        args = [own, near, far, *strips, *near_strips, *corners, done]
+        wide = pl.pallas_call(
+            functools.partial(place_kernel, count),
+            out_shape=struct(shape[0] + 16, 2, shape[1] + 32, LANES),
+            in_specs=[VMEM] * len(args),
+            out_specs=VMEM,
+            compiler_params=params(),
+            cost_estimate=cost(10_000, 3_000_000),
+            name="place",
+        )(*args)
+        args = [wide, prev]
     args += [speed, drive1, drive2, *partner_strips]
     out = pl.pallas_call(
         functools.partial(step_pair_kernel, count, True, blank, 0),
         out_shape=outs,
         in_specs=[VMEM] * len(args),
         out_specs=[VMEM] * len(outs),
-        scratch_shapes=[] if blank else [wide_shape(shape)],
         compiler_params=params(),
         cost_estimate=cost(900_000_000, 400_000_000),
         name="tangent_steps",
@@ -351,7 +367,7 @@
     return out[0], out[1], list(out[2 : 2 + count]), list(out[2 + count :])
 
 
-def gather_ring_kernel(count, p_prev, speed, perturb, near, far, _, *refs):
+def gather_ring_kernel(count, p_prev, speed, perturb, near, far, *refs):
     strips, refs = refs[:count], refs[count:]
     near_strips, refs = refs[:count], refs[count:]
     corners, targets = refs[:count], refs[count:]
@@ -385,8 +401,8 @@
             pl.when(par_y == side)(functools.partial(fill, 1))
 
 
-def gather_ring(shape, count, fields, near, far, p_far, strips, near_strips, corners):
-    args = [*fields, near, far, p_far, *strips, *near_strips, *corners]
+def gather_ring(shape, count, fields, near, far, strips, near_strips, corners):
+    args = [*fields, near, far, *strips, *near_strips, *corners]
     return pl.pallas_call(
         functools.partial(gather_ring_kernel, count),
         out_shape=[ring_struct(shape)] * 3,
@@ -603,7 +619,6 @@
         (pressure_prev, courant, perturbation),
         near,
         far,
-        p_far,
         strips,
         near_strips,
         corners,
@@ -616,7 +631,7 @@
     for step in range(0, steps, 2):
         around = (strips, near_strips, corners)
         p_pieces = (p_cur, p_near, p_far) + around
-        q_pieces = None if q_cur is None else (q_cur, q_near, q_far) + around
+        q_pieces = None if q_cur is None else (q_cur, q_near, q_far) + around + (earlier[-1],)
         p_prev, p_cur, drive1, drive2, p_strips = pressure_steps(
             shape, count, step, source_pos, wavelet, p_pieces, p_prev, speed, perturb
         )

time: 106 us -> 104 us (0.981)
  starting transfers between devices: 63.4 us -> 60 us
  local copies, waits for them, and re-layouts: 1.33 us -> 2.88 us
    ppermute x12, starting transfers between devices: 41.1 us -> 38.9 us  [swap_near(): return lax.ppermute(value, 'gx', near_x)]
    unnamed x16 -> x18, local copies, waits for them, and re-layouts: 1.33 us -> 2.88 us
  transfers between devices with their start and end apart: 29 -> 29, of which waited for: 5 -> 6; matrix products, arithmetic and copies ran while one was open for 0% -> 0% of each run, Pallas kernels for 10% -> 13%
where the time goes in v4:
time: 104 us; the launch traced here: 103 us
  starting transfers between devices  60 us (58%)
  Pallas kernels  25 us (24%)
  waiting for transfers between devices  14 us (13%)
  local copies, waits for them, and re-layouts  2.88 us (3%)
  between operations  1.19 us (1%)
    ppermute x12, starting transfers between devices, swap_near(): return lax.ppermute(value, 'gx', near_x)  38.9 us
    pallas_call x4, Pallas kernels, pressure_steps(): pl.pallas_call(functools.partial(step_pair_kernel, count, False, False, a...  9.37 us
    pallas_call x4, Pallas kernels, tangent_steps(): pl.pallas_call(functools.partial(step_pair_kernel, count, True, blank, 0)...  7.67 us
    all_to_all x1, starting transfers between devices, on_device(): sums = lax.all_to_all(spread, AXES, 0, 0)  7.46 us
    all_to_all x1, waiting for transfers between devices, on_device(): sums = lax.all_to_all(spread, AXES, 0, 0)  6.25 us
    ppermute x4, starting transfers between devices, swap_strips(): lax.ppermute(value, 'gy', pairs)  5.6 us
    ppermute x8, starting transfers between devices, swap_far(): return lax.ppermute(value, 'gx', far_x)  5.39 us
    ppermute x4, waiting for transfers between devices, swap_strips(): lax.ppermute(value, 'gy', pairs)  5.17 us
  transfers between devices with their start and end apart: 29, of which 6 were waited for; matrix products, arithmetic and copies ran while one was open for 0% of the time, Pallas kernels for 13%

profile of v4, /device:TPU:0, one launch (start us, length us, event | category | flops | bytes accessed | tf_op | source)
XLA Modules:
  0.0 103.1 jit_solution(1471705902987709629)
XLA Ops:
  0.7 2.4 %pack.1 = (f32[12,32,256]{2,1,0:T(8,128)}, f32[12,32,256]{2,1,0:T(8,128)}, f32[32,8,256]{2,1,0:T(8,128)}, f32[8,8,256]{2,1,0:T(8,128)}) custom-call(f32[8,32,256]{2,1,0:T(8,128)} %refs_2_.1, f32[8,32,256]{2,1,0:T(8,128)} %p_prev.3, f32[8,32,256]{2,1,0:T(8,128)} %speed.5, f32[8,32,256]{2,1,0:T(8,128)} %perturb.3), custom_call_target="tpu_custom_call" | custom-call | flops 10000 | bytes 3000000 | tf_op jit(solution)/shard_map/pack/pallas_call | solution.py:357
  3.1 3.0 %collective-permute-start.2 = (f32[32,8,256]{2,1,0:T(8,128)}, f32[32,8,256]{2,1,0:T(8,128)S(1)}, u32[]{:S(2)}, u32[]{:S(2)}) collective-permute-start(f32[32,8,256]{2,1,0:T(8,128)} %get-tuple-element.62), channel_id=1, source_target_pairs={{0,1},{1,0},{2,3},{3,2},{4,5},{5,4},{6,7},{7,6},{8,9},{9,8},{10,11... | collective-permute-start | bytes 786440 | tf_op jit(solution)/shard_map/ppermute | solution.py:604
  6.1 0.7 collective-permute-start.1
  7.4 5.2 %collective-permute-done.2.refs_0_.refs_5_ = f32[32,8,256]{2,1,0:T(8,128)S(1)} collective-permute-done((f32[32,8,256]{2,1,0:T(8,128)}, f32[32,8,256]{2,1,0:T(8,128)S(1)}, u32[]{:S(2)}, u32[]{:S(2)}) %collective-permute-start.2) | collective-permute-done | bytes 262176 | tf_op jit(solution)/shard_map/ppermute | solution.py:604
  14.4 0.9 copy-done
  15.4 0.9 copy-done.2
  16.3 0.9 copy-done.3
  17.5 2.3 %pressure_steps.4 = (f32[16,2,48,128]{3,2,1,0:T(8,128)S(1)}, f32[8,32,256]{2,1,0:T(8,128)S(1)}, f32[16,2,48,128]{3,2,1,0:T(8,128)S(1)}, f32[8,2,32,128]{3,2,1,0:T(8,128)S(1)}, f32[8,8,256]{2,1,0:T(8,128)S(1)}) custom-call(s32[3]{0:T(128)S(1)} %copy-done.5, f32[8]{0:T(128)S(1)} %copy-done.6, f32[8,32,256]{2,1,0:T(8,128)S(1)} %copy-done.4, ...), custom_call_target="tpu_custom_call" | custom-call | flops 900000000 | bytes 400000000 | tf_op jit(solution)/shard_map/pressure_steps/pallas_call | solution.py:276
  19.8 0.7 collective-permute-start.8
  20.5 9.5 %collective-permute-start.7 = (f32[8,32,256]{2,1,0:T(8,128)S(1)}, f32[8,32,256]{2,1,0:T(8,128)S(1)}, u32[]{:S(2)}, u32[]{:S(2)}) collective-permute-start(f32[8,32,256]{2,1,0:T(8,128)S(1)} %get-tuple-element.67.refs_2_.p2), channel_id=1, source_target_pairs={{0,2},{2,0},{4,6},{6,4},{8,10},{10,8},{12,14},{14,12},{16,18},{18,... | collective-permute-start | bytes 786440 | tf_op jit(solution)/shard_map/ppermute | solution.py:598
  31.9 0.7 collective-permute-start.15
  32.6 7.7 %collective-permute-start.14 = (f32[8,32,256]{2,1,0:T(8,128)S(1)}, f32[8,32,256]{2,1,0:T(8,128)S(1)}, u32[]{:S(2)}, u32[]{:S(2)}) collective-permute-start(f32[8,32,256]{2,1,0:T(8,128)S(1)} %get-tuple-element.75.q2.own), channel_id=1, source_target_pairs={{0,2},{2,0},{4,6},{6,4},{8,10},{10,8},{12,14},{14,12},{16,18},{18,... | collective-permute-start | bytes 786440 | tf_op jit(solution)/shard_map/ppermute | solution.py:598
  41.7 2.3 %pressure_steps.5 = (f32[16,2,48,128]{3,2,1,0:T(8,128)S(1)}, f32[8,32,256]{2,1,0:T(8,128)S(1)}, f32[16,2,48,128]{3,2,1,0:T(8,128)S(1)}, f32[8,2,32,128]{3,2,1,0:T(8,128)S(1)}, f32[8,8,256]{2,1,0:T(8,128)S(1)}) custom-call(s32[3]{0:T(128)S(1)} %copy-done.5, f32[8]{0:T(128)S(1)} %copy-done.6, f32[8,32,256]{2,1,0:T(8,128)S(1)} %get-tuple-element.67.refs_2_.p2, ...), custom_call_target="tpu_custom_call" | custom-call | flops 900000000 | bytes 400000000 | tf_op jit(solution)/shard_map/pressure_steps/pallas_call | solution.py:276
  44.0 0.7 collective-permute-start.13
  44.7 3.8 %collective-permute-start.12 = (f32[8,32,256]{2,1,0:T(8,128)S(1)}, f32[8,32,256]{2,1,0:T(8,128)S(1)}, u32[]{:S(2)}, u32[]{:S(2)}) collective-permute-start(f32[8,32,256]{2,1,0:T(8,128)S(1)} %get-tuple-element.74.refs_2_.p2), channel_id=1, source_target_pairs={{0,2},{2,0},{4,6},{6,4},{8,10},{10,8},{12,14},{14,12},{16,18},{18,... | collective-permute-start | bytes 786440 | tf_op jit(solution)/shard_map/ppermute | solution.py:598
  48.6 2.1 %tangent_steps.5 = (f32[16,2,48,128]{3,2,1,0:T(8,128)S(1)}, f32[8,32,256]{2,1,0:T(8,128)S(1)}, f32[16,8,256]{2,1,0:T(8,128)S(1)}, f32[8,8,256]{2,1,0:T(8,128)S(1)}) custom-call(f32[24,2,64,128]{3,2,1,0:T(8,128)S(1)} %place.3.refs_0_, f32[16,2,48,128]{3,2,1,0:T(8,128)S(1)} %get-tuple-element.76.q1.refs_1_, ...), custom_call_target="tpu_custom_call" | custom-call | flops 900000000 | bytes 400000000 | tf_op jit(solution)/shard_map/tangent_steps/pallas_call | solution.py:314
  50.7 1.4 %collective-permute-start.16 = (f32[16,8,256]{2,1,0:T(8,128)S(1)}, f32[16,8,256]{2,1,0:T(8,128)S(1)}, u32[]{:S(2)}, u32[]{:S(2)}) collective-permute-start(f32[16,8,256]{2,1,0:T(8,128)S(1)} %get-tuple-element.81), channel_id=1, source_target_pairs={{0,1},{1,0},{2,3},{3,2},{4,5},{5,4},{6,7},{7,6},{8,9},{9,8},{10,11... | collective-permute-start | bytes 393224 | tf_op jit(solution)/shard_map/ppermute | solution.py:604
  52.8 0.7 collective-permute-start.22
  53.5 5.6 %collective-permute-start.21 = (f32[8,32,256]{2,1,0:T(8,128)S(1)}, f32[8,32,256]{2,1,0:T(8,128)S(1)}, u32[]{:S(2)}, u32[]{:S(2)}) collective-permute-start(f32[8,32,256]{2,1,0:T(8,128)S(1)} %get-tuple-element.85.q2.own), channel_id=1, source_target_pairs={{0,2},{2,0},{4,6},{6,4},{8,10},{10,8},{12,14},{14,12},{16,18},{18,... | collective-permute-start | bytes 786440 | tf_op jit(solution)/shard_map/ppermute | solution.py:598
  60.4 2.5 %pressure_steps.6 = (f32[16,2,48,128]{3,2,1,0:T(8,128)S(1)}, f32[8,32,256]{2,1,0:T(8,128)S(1)}, f32[16,2,48,128]{3,2,1,0:T(8,128)S(1)}, f32[8,2,32,128]{3,2,1,0:T(8,128)S(1)}, f32[8,8,256]{2,1,0:T(8,128)S(1)}) custom-call(s32[3]{0:T(128)S(1)} %copy-done.5, f32[8]{0:T(128)S(1)} %copy-done.6, f32[8,32,256]{2,1,0:T(8,128)S(1)} %get-tuple-element.74.refs_2_.p2, ...), custom_call_target="tpu_custom_call" | custom-call | flops 900000000 | bytes 400000000 | tf_op jit(solution)/shard_map/pressure_steps/pallas_call | solution.py:276
  63.0 2.1 %tangent_steps.6 = (f32[16,2,48,128]{3,2,1,0:T(8,128)S(1)}, f32[8,32,256]{2,1,0:T(8,128)S(1)}, f32[16,8,256]{2,1,0:T(8,128)S(1)}, f32[8,8,256]{2,1,0:T(8,128)S(1)}) custom-call(f32[24,2,64,128]{3,2,1,0:T(8,128)S(1)} %place.4.refs_0_, f32[16,2,48,128]{3,2,1,0:T(8,128)S(1)} %get-tuple-element.86.q1.refs_1_, ...), custom_call_target="tpu_custom_call" | custom-call | flops 900000000 | bytes 400000000 | tf_op jit(solution)/shard_map/tangent_steps/pallas_call | solution.py:314
  66.5 6.5 %collective-permute-start.19 = (f32[8,32,256]{2,1,0:T(8,128)S(1)}, f32[8,32,256]{2,1,0:T(8,128)S(1)}, u32[]{:S(2)}, u32[]{:S(2)}) collective-permute-start(f32[8,32,256]{2,1,0:T(8,128)S(1)} %get-tuple-element.84.refs_2_.p2), channel_id=1, source_target_pairs={{0,2},{2,0},{4,6},{6,4},{8,10},{10,8},{12,14},{14,12},{16,18},{18,... | collective-permute-start | bytes 786440 | tf_op jit(solution)/shard_map/ppermute | solution.py:598
  73.6 0.7 collective-permute-start.27
  74.3 5.1 %collective-permute-start.26 = (f32[8,32,256]{2,1,0:T(8,128)S(1)}, f32[8,32,256]{2,1,0:T(8,128)S(1)}, u32[]{:S(2)}, u32[]{:S(2)}) collective-permute-start(f32[8,32,256]{2,1,0:T(8,128)S(1)} %get-tuple-element.95.q2.own), channel_id=1, source_target_pairs={{0,2},{2,0},{4,6},{6,4},{8,10},{10,8},{12,14},{14,12},{16,18},{18,... | collective-permute-start | bytes 786440 | tf_op jit(solution)/shard_map/ppermute | solution.py:598
  80.1 0.7 collective-permute-done.24.refs_6_.refs_1_
  80.8 2.3 %pressure_steps.7 = (f32[16,2,48,128]{3,2,1,0:T(8,128)S(1)}, f32[8,32,256]{2,1,0:T(8,128)S(1)}, f32[16,2,48,128]{3,2,1,0:T(8,128)S(1)}, f32[8,2,32,128]{3,2,1,0:T(8,128)S(1)}, f32[8,8,256]{2,1,0:T(8,128)S(1)}) custom-call(s32[3]{0:T(128)S(1)} %copy-done.5, f32[8]{0:T(128)S(1)} %copy-done.6, f32[8,32,256]{2,1,0:T(8,128)S(1)} %get-tuple-element.84.refs_2_.p2, ...), custom_call_target="tpu_custom_call" | custom-call | flops 900000000 | bytes 400000000 | tf_op jit(solution)/shard_map/pressure_steps/pallas_call | solution.py:276
  83.2 2.8 %tangent_steps.7 = (f32[16,2,48,128]{3,2,1,0:T(8,128)S(1)}, f32[8,32,256]{2,1,0:T(8,128)S(1)}, f32[16,8,256]{2,1,0:T(8,128)}, f32[8,8,256]{2,1,0:T(8,128)}) custom-call(f32[24,2,64,128]{3,2,1,0:T(8,128)S(1)} %place.5.refs_0_, f32[16,2,48,128]{3,2,1,0:T(8,128)S(1)} %get-tuple-element.96.q1.refs_1_, ...), custom_call_target="tpu_custom_call" | custom-call | flops 900000000 | bytes 400000000 | tf_op jit(solution)/shard_map/tangent_steps/pallas_call | solution.py:314
  86.0 1.4 %receive.7 = (f32[8,128]{1,0:T(8,128)S(1)}, f32[8,128]{1,0:T(8,128)S(1)}, f32[32,1,128]{2,1,0:T(1,128)}) custom-call(s32[1,128]{1,0:T(1,128)S(1)} %bitcast.6, f32[16,2,48,128]{3,2,1,0:T(8,128)S(1)} %get-tuple-element.104.p1, f32[8,32,256]{2,1,0:T(8,128)S(1)} %get-tuple-element.94.p_in.p2, f32[16,2,48,128]{3,2,1,0:T(8,128)S(1)} %get-tuple-element.105.q1, ...), custom_call_target="tpu_custom_call" | custom-call | flops 20000000 | bytes 2500000 | tf_op jit(solution)/shard_map/receive/pallas_call | solution.py:486
  87.4 7.5 %all-to-all-start = ((f32[32,1,128]{2,1,0:T(1,128)}), f32[32,1,128]{2,1,0:T(1,128)S(1)}, u32[]{:S(2)}, u32[]{:S(2)}) async-start(f32[32,1,128]{2,1,0:T(1,128)} %get-tuple-element.110), calls=%async_computation | async-start | bytes 32768 | tf_op jit(solution)/shard_map/all_to_all | solution.py:657
  94.9 0.9 smooth.1
  95.7 6.2 %all-to-all-done.sums = f32[32,1,128]{2,1,0:T(1,128)S(1)} async-done(((f32[32,1,128]{2,1,0:T(1,128)}), f32[32,1,128]{2,1,0:T(1,128)S(1)}, u32[]{:S(2)}, u32[]{:S(2)}) %all-to-all-start) | async-done | bytes 16416 | tf_op jit(solution)/shard_map/all_to_all | solution.py:657
  102.0 0.9 finish.1
  (63 shorter events, 10.9 us)
Async XLA Ops:
  0.6 16.9 %copy-start.4 = (f32[8,32,256]{2,1,0:T(8,128)S(1)}, f32[8,32,256]{2,1,0:T(8,128)}, u32[]{:S(2)}) copy-start(f32[8,32,256]{2,1,0:T(8,128)} %refs_2_.1) | copy-start | bytes 786436
  0.6 16.9 %copy-start.6 = (f32[8]{0:T(128)S(1)}, f32[8]{0:T(128)}, u32[]{:S(2)}) copy-start(f32[8]{0:T(128)} %refs_1_.7) | copy-start | bytes 100
  0.7 16.9 %copy-start.5 = (s32[3]{0:T(128)S(1)}, s32[3]{0:T(128)}, u32[]{:S(2)}) copy-start(s32[3]{0:T(128)} %refs_0_.7) | copy-start | bytes 40
  3.1 9.5 %collective-permute-start.2 = (f32[32,8,256]{2,1,0:T(8,128)}, f32[32,8,256]{2,1,0:T(8,128)S(1)}, u32[]{:S(2)}, u32[]{:S(2)}) collective-permute-start(f32[32,8,256]{2,1,0:T(8,128)} %get-tuple-element.62), channel_id=1, source_target_pairs={{0,1},{1,0},{2,3},{3,2},{4,5},{5,4},{6,7},{7,6},{8,9},{9,8},{10,11... | collective-permute-start | bytes 786440 | tf_op jit(solution)/shard_map/ppermute | solution.py:604
  6.1 7.7 %collective-permute-start = (f32[12,32,256]{2,1,0:T(8,128)}, f32[12,32,256]{2,1,0:T(8,128)S(1)}, u32[]{:S(2)}, u32[]{:S(2)}) collective-permute-start(f32[12,32,256]{2,1,0:T(8,128)} %get-tuple-element.60), channel_id=1, source_target_pairs={{0,2},{2,0},{4,6},{6,4},{8,10},{10,8},{12,14},{14,12},{16,18},{18,... | collective-permute-start | bytes 1179656 | tf_op jit(solution)/shard_map/ppermute | solution.py:598
  6.1 7.7 %collective-permute-start.1 = (f32[12,32,256]{2,1,0:T(8,128)}, f32[12,32,256]{2,1,0:T(8,128)S(1)}, u32[]{:S(2)}, u32[]{:S(2)}) collective-permute-start(f32[12,32,256]{2,1,0:T(8,128)} %get-tuple-element.61), channel_id=1, source_target_pairs={{2,4},{4,2},{6,8},{8,6},{10,12},{12,10},{14,16},{16,14},{18,20},{2... | collective-permute-start | bytes 1179656 | tf_op jit(solution)/shard_map/ppermute | solution.py:601
  6.7 6.3 %collective-permute-start.4 = (f32[8,8,256]{2,1,0:T(8,128)}, f32[8,8,256]{2,1,0:T(8,128)S(1)}, u32[]{:S(2)}, u32[]{:S(2)}) collective-permute-start(f32[8,8,256]{2,1,0:T(8,128)} %get-tuple-element.63), channel_id=1, source_target_pairs={{2,5},{3,4},{4,3},{5,2},{6,9},{7,8},{8,7},{9,6},{10,13},{11,12},{1... | collective-permute-start | bytes 196616 | tf_op jit(solution)/shard_map/ppermute | solution.py:606
  12.6 1.9 %collective-permute-start.3 = (f32[32,8,256]{2,1,0:T(8,128)S(1)}, f32[32,8,256]{2,1,0:T(8,128)S(1)}, u32[]{:S(2)}, u32[]{:S(2)}) collective-permute-start(f32[32,8,256]{2,1,0:T(8,128)S(1)} %collective-permute-done.2.refs_0_.refs_5_), channel_id=1, source_target_pairs={{0,2},{2,0},{4,6},{6,4},{8,10},{10,8},{12,14},{14,12},{16,18},{18,... | collective-permute-start | bytes 786440 | tf_op jit(solution)/shard_map/ppermute | solution.py:598
  12.6 4.9 %collective-permute-start.5 = (f32[8,32,256]{2,1,0:T(8,128)}, f32[8,32,256]{2,1,0:T(8,128)S(1)}, u32[]{:S(2)}, u32[]{:S(2)}) collective-permute-start(f32[8,32,256]{2,1,0:T(8,128)} %refs_2_.1), channel_id=1, source_target_pairs={{0,2},{2,0},{4,6},{6,4},{8,10},{10,8},{12,14},{14,12},{16,18},{18,... | collective-permute-start | bytes 786440 | tf_op jit(solution)/shard_map/ppermute | solution.py:598
  13.1 4.4 %collective-permute-start.6 = (f32[8,32,256]{2,1,0:T(8,128)}, f32[8,32,256]{2,1,0:T(8,128)S(1)}, u32[]{:S(2)}, u32[]{:S(2)}) collective-permute-start(f32[8,32,256]{2,1,0:T(8,128)} %refs_2_.1), channel_id=1, source_target_pairs={{2,4},{4,2},{6,8},{8,6},{10,12},{12,10},{14,16},{16,14},{18,20},{2... | collective-permute-start | bytes 786440 | tf_op jit(solution)/shard_map/ppermute | solution.py:601
  19.8 21.3 %collective-permute-start.8 = (f32[8,32,256]{2,1,0:T(8,128)S(1)}, f32[8,32,256]{2,1,0:T(8,128)S(1)}, u32[]{:S(2)}, u32[]{:S(2)}) collective-permute-start(f32[8,32,256]{2,1,0:T(8,128)S(1)} %get-tuple-element.67.refs_2_.p2), channel_id=1, source_target_pairs={{2,4},{4,2},{6,8},{8,6},{10,12},{12,10},{14,16},{16,14},{18,20},{2... | collective-permute-start | bytes 786440 | tf_op jit(solution)/shard_map/ppermute | solution.py:601
  20.5 20.6 %collective-permute-start.7 = (f32[8,32,256]{2,1,0:T(8,128)S(1)}, f32[8,32,256]{2,1,0:T(8,128)S(1)}, u32[]{:S(2)}, u32[]{:S(2)}) collective-permute-start(f32[8,32,256]{2,1,0:T(8,128)S(1)} %get-tuple-element.67.refs_2_.p2), channel_id=1, source_target_pairs={{0,2},{2,0},{4,6},{6,4},{8,10},{10,8},{12,14},{14,12},{16,18},{18,... | collective-permute-start | bytes 786440 | tf_op jit(solution)/shard_map/ppermute | solution.py:598
  30.6 9.7 %collective-permute-start.9 = (f32[16,8,256]{2,1,0:T(8,128)S(1)}, f32[16,8,256]{2,1,0:T(8,128)S(1)}, u32[]{:S(2)}, u32[]{:S(2)}) collective-permute-start(f32[16,8,256]{2,1,0:T(8,128)S(1)} %get-tuple-element.71), channel_id=1, source_target_pairs={{0,1},{1,0},{2,3},{3,2},{4,5},{5,4},{6,7},{7,6},{8,9},{9,8},{10,11... | collective-permute-start | bytes 393224 | tf_op jit(solution)/shard_map/ppermute | solution.py:604
  31.2 1.3 %collective-permute-start.11 = (f32[8,8,256]{2,1,0:T(8,128)S(1)}, f32[8,8,256]{2,1,0:T(8,128)S(1)}, u32[]{:S(2)}, u32[]{:S(2)}) collective-permute-start(f32[8,8,256]{2,1,0:T(8,128)S(1)} %get-tuple-element.72), channel_id=1, source_target_pairs={{2,5},{3,4},{4,3},{5,2},{6,9},{7,8},{8,7},{9,6},{10,13},{11,12},{1... | collective-permute-start | bytes 196616 | tf_op jit(solution)/shard_map/ppermute | solution.py:606
  31.9 16.6 %collective-permute-start.15 = (f32[8,32,256]{2,1,0:T(8,128)S(1)}, f32[8,32,256]{2,1,0:T(8,128)S(1)}, u32[]{:S(2)}, u32[]{:S(2)}) collective-permute-start(f32[8,32,256]{2,1,0:T(8,128)S(1)} %get-tuple-element.75.q2.own), channel_id=1, source_target_pairs={{2,4},{4,2},{6,8},{8,6},{10,12},{12,10},{14,16},{16,14},{18,20},{2... | collective-permute-start | bytes 786440 | tf_op jit(solution)/shard_map/ppermute | solution.py:601
  32.6 15.9 %collective-permute-start.14 = (f32[8,32,256]{2,1,0:T(8,128)S(1)}, f32[8,32,256]{2,1,0:T(8,128)S(1)}, u32[]{:S(2)}, u32[]{:S(2)}) collective-permute-start(f32[8,32,256]{2,1,0:T(8,128)S(1)} %get-tuple-element.75.q2.own), channel_id=1, source_target_pairs={{0,2},{2,0},{4,6},{6,4},{8,10},{10,8},{12,14},{14,12},{16,18},{18,... | collective-permute-start | bytes 786440 | tf_op jit(solution)/shard_map/ppermute | solution.py:598
  40.3 1.3 %collective-permute-start.10 = (f32[16,8,256]{2,1,0:T(8,128)S(1)}, f32[16,8,256]{2,1,0:T(8,128)S(1)}, u32[]{:S(2)}, u32[]{:S(2)}) collective-permute-start(f32[16,8,256]{2,1,0:T(8,128)S(1)} %collective-permute-done.9.refs_5_.refs_0_), channel_id=1, source_target_pairs={{0,2},{2,0},{4,6},{6,4},{8,10},{10,8},{12,14},{14,12},{16,18},{18,... | collective-permute-start | bytes 393224 | tf_op jit(solution)/shard_map/ppermute | solution.py:598
  44.0 15.8 %collective-permute-start.13 = (f32[8,32,256]{2,1,0:T(8,128)S(1)}, f32[8,32,256]{2,1,0:T(8,128)S(1)}, u32[]{:S(2)}, u32[]{:S(2)}) collective-permute-start(f32[8,32,256]{2,1,0:T(8,128)S(1)} %get-tuple-element.74.refs_2_.p2), channel_id=1, source_target_pairs={{2,4},{4,2},{6,8},{8,6},{10,12},{12,10},{14,16},{16,14},{18,20},{2... | collective-permute-start | bytes 786440 | tf_op jit(solution)/shard_map/ppermute | solution.py:601
  44.7 15.2 %collective-permute-start.12 = (f32[8,32,256]{2,1,0:T(8,128)S(1)}, f32[8,32,256]{2,1,0:T(8,128)S(1)}, u32[]{:S(2)}, u32[]{:S(2)}) collective-permute-start(f32[8,32,256]{2,1,0:T(8,128)S(1)} %get-tuple-element.74.refs_2_.p2), channel_id=1, source_target_pairs={{0,2},{2,0},{4,6},{6,4},{8,10},{10,8},{12,14},{14,12},{16,18},{18,... | collective-permute-start | bytes 786440 | tf_op jit(solution)/shard_map/ppermute | solution.py:598
  50.7 8.3 %collective-permute-start.16 = (f32[16,8,256]{2,1,0:T(8,128)S(1)}, f32[16,8,256]{2,1,0:T(8,128)S(1)}, u32[]{:S(2)}, u32[]{:S(2)}) collective-permute-start(f32[16,8,256]{2,1,0:T(8,128)S(1)} %get-tuple-element.81), channel_id=1, source_target_pairs={{0,1},{1,0},{2,3},{3,2},{4,5},{5,4},{6,7},{7,6},{8,9},{9,8},{10,11... | collective-permute-start | bytes 393224 | tf_op jit(solution)/shard_map/ppermute | solution.py:604
  52.1 1.3 %collective-permute-start.18 = (f32[8,8,256]{2,1,0:T(8,128)S(1)}, f32[8,8,256]{2,1,0:T(8,128)S(1)}, u32[]{:S(2)}, u32[]{:S(2)}) collective-permute-start(f32[8,8,256]{2,1,0:T(8,128)S(1)} %get-tuple-element.82), channel_id=1, source_target_pairs={{2,5},{3,4},{4,3},{5,2},{6,9},{7,8},{8,7},{9,6},{10,13},{11,12},{1... | collective-permute-start | bytes 196616 | tf_op jit(solution)/shard_map/ppermute | solution.py:606
  52.8 10.2 %collective-permute-start.22 = (f32[8,32,256]{2,1,0:T(8,128)S(1)}, f32[8,32,256]{2,1,0:T(8,128)S(1)}, u32[]{:S(2)}, u32[]{:S(2)}) collective-permute-start(f32[8,32,256]{2,1,0:T(8,128)S(1)} %get-tuple-element.85.q2.own), channel_id=1, source_target_pairs={{2,4},{4,2},{6,8},{8,6},{10,12},{12,10},{14,16},{16,14},{18,20},{2... | collective-permute-start | bytes 786440 | tf_op jit(solution)/shard_map/ppermute | solution.py:601
  53.5 9.5 %collective-permute-start.21 = (f32[8,32,256]{2,1,0:T(8,128)S(1)}, f32[8,32,256]{2,1,0:T(8,128)S(1)}, u32[]{:S(2)}, u32[]{:S(2)}) collective-permute-start(f32[8,32,256]{2,1,0:T(8,128)S(1)} %get-tuple-element.85.q2.own), channel_id=1, source_target_pairs={{0,2},{2,0},{4,6},{6,4},{8,10},{10,8},{12,14},{14,12},{16,18},{18,... | collective-permute-start | bytes 786440 | tf_op jit(solution)/shard_map/ppermute | solution.py:598
  59.1 1.3 %collective-permute-start.17 = (f32[16,8,256]{2,1,0:T(8,128)S(1)}, f32[16,8,256]{2,1,0:T(8,128)S(1)}, u32[]{:S(2)}, u32[]{:S(2)}) collective-permute-start(f32[16,8,256]{2,1,0:T(8,128)S(1)} %collective-permute-done.16.refs_5_.refs_0_), channel_id=1, source_target_pairs={{0,2},{2,0},{4,6},{6,4},{8,10},{10,8},{12,14},{14,12},{16,18},{18,... | collective-permute-start | bytes 393224 | tf_op jit(solution)/shard_map/ppermute | solution.py:598
  65.2 14.3 %collective-permute-start.23 = (f32[16,8,256]{2,1,0:T(8,128)S(1)}, f32[16,8,256]{2,1,0:T(8,128)S(1)}, u32[]{:S(2)}, u32[]{:S(2)}) collective-permute-start(f32[16,8,256]{2,1,0:T(8,128)S(1)} %get-tuple-element.91), channel_id=1, source_target_pairs={{0,1},{1,0},{2,3},{3,2},{4,5},{5,4},{6,7},{7,6},{8,9},{9,8},{10,11... | collective-permute-start | bytes 393224 | tf_op jit(solution)/shard_map/ppermute | solution.py:604
  65.8 15.0 %collective-permute-start.20 = (f32[8,32,256]{2,1,0:T(8,128)S(1)}, f32[8,32,256]{2,1,0:T(8,128)S(1)}, u32[]{:S(2)}, u32[]{:S(2)}) collective-permute-start(f32[8,32,256]{2,1,0:T(8,128)S(1)} %get-tuple-element.84.refs_2_.p2), channel_id=1, source_target_pairs={{2,4},{4,2},{6,8},{8,6},{10,12},{12,10},{14,16},{16,14},{18,20},{2... | collective-permute-start | bytes 786440 | tf_op jit(solution)/shard_map/ppermute | solution.py:601
  66.5 14.3 %collective-permute-start.19 = (f32[8,32,256]{2,1,0:T(8,128)S(1)}, f32[8,32,256]{2,1,0:T(8,128)S(1)}, u32[]{:S(2)}, u32[]{:S(2)}) collective-permute-start(f32[8,32,256]{2,1,0:T(8,128)S(1)} %get-tuple-element.84.refs_2_.p2), channel_id=1, source_target_pairs={{0,2},{2,0},{4,6},{6,4},{8,10},{10,8},{12,14},{14,12},{16,18},{18,... | collective-permute-start | bytes 786440 | tf_op jit(solution)/shard_map/ppermute | solution.py:598
  72.9 1.3 %collective-permute-start.25 = (f32[8,8,256]{2,1,0:T(8,128)S(1)}, f32[8,8,256]{2,1,0:T(8,128)S(1)}, u32[]{:S(2)}, u32[]{:S(2)}) collective-permute-start(f32[8,8,256]{2,1,0:T(8,128)S(1)} %get-tuple-element.92), channel_id=1, source_target_pairs={{2,5},{3,4},{4,3},{5,2},{6,9},{7,8},{8,7},{9,6},{10,13},{11,12},{1... | collective-permute-start | bytes 196616 | tf_op jit(solution)/shard_map/ppermute | solution.py:606
  73.6 9.5 %collective-permute-start.27 = (f32[8,32,256]{2,1,0:T(8,128)S(1)}, f32[8,32,256]{2,1,0:T(8,128)S(1)}, u32[]{:S(2)}, u32[]{:S(2)}) collective-permute-start(f32[8,32,256]{2,1,0:T(8,128)S(1)} %get-tuple-element.95.q2.own), channel_id=1, source_target_pairs={{2,4},{4,2},{6,8},{8,6},{10,12},{12,10},{14,16},{16,14},{18,20},{2... | collective-permute-start | bytes 786440 | tf_op jit(solution)/shard_map/ppermute | solution.py:601
  74.3 8.8 %collective-permute-start.26 = (f32[8,32,256]{2,1,0:T(8,128)S(1)}, f32[8,32,256]{2,1,0:T(8,128)S(1)}, u32[]{:S(2)}, u32[]{:S(2)}) collective-permute-start(f32[8,32,256]{2,1,0:T(8,128)S(1)} %get-tuple-element.95.q2.own), channel_id=1, source_target_pairs={{0,2},{2,0},{4,6},{6,4},{8,10},{10,8},{12,14},{14,12},{16,18},{18,... | collective-permute-start | bytes 786440 | tf_op jit(solution)/shard_map/ppermute | solution.py:598
  79.4 1.3 %collective-permute-start.24 = (f32[16,8,256]{2,1,0:T(8,128)S(1)}, f32[16,8,256]{2,1,0:T(8,128)S(1)}, u32[]{:S(2)}, u32[]{:S(2)}) collective-permute-start(f32[16,8,256]{2,1,0:T(8,128)S(1)} %collective-permute-done.23.refs_5_.refs_0_), channel_id=1, source_target_pairs={{0,2},{2,0},{4,6},{6,4},{8,10},{10,8},{12,14},{14,12},{16,18},{18,... | collective-permute-start | bytes 393224 | tf_op jit(solution)/shard_map/ppermute | solution.py:598
  87.4 14.6 %all-to-all-start = ((f32[32,1,128]{2,1,0:T(1,128)}), f32[32,1,128]{2,1,0:T(1,128)S(1)}, u32[]{:S(2)}, u32[]{:S(2)}) async-start(f32[32,1,128]{2,1,0:T(1,128)} %get-tuple-element.110), calls=%async_computation | async-start | bytes 32768 | tf_op jit(solution)/shard_map/all_to_all | solution.py:657
  (6 other events, 39.8 us)

commit v5 on v4

--- a/solution.py
+++ b/solution.py
@@ -124,7 +124,7 @@
     return [jnp.where(even, high, low), jnp.where(even, low, high)]
 
 
-def step_pair_kernel(count, tangent, blank, at, *refs):
+def step_pair_kernel(count, sends, tangent, blank, at, *refs):
     refs = list(refs)
     scalars = parity()
     if not tangent:
@@ -150,7 +150,7 @@
     if tangent:
         drive1, drive2 = refs[:2]
         refs = refs[2:]
-        partner_strips, refs = refs[:count], refs[count:]
+        partner_strips, refs = refs[:sends], refs[sends:]
     else:
         perturb = refs.pop(0)
     next1, next2 = refs[:2]
@@ -158,9 +158,9 @@
     if not tangent:
         drive1, drive2 = refs[:2]
         refs = refs[2:]
-    strip_out, refs = refs[:count], refs[count:]
+    strip_out, refs = refs[:sends], refs[sends:]
     if tangent:
-        corner_out, refs = refs[:count], refs[count:]
+        corner_out, refs = refs[:sends], refs[sends:]
     size_x, size_y, _ = next2.shape
     par_x = scalars[0]
     inner = slice(8, 8 + size_y)
@@ -241,8 +241,8 @@
             row = next2[src_x, pl.ds(src_y, 1), :]
             next2[src_x, pl.ds(src_y, 1), :] = row + jnp.where(hit, wave[at + 1], 0.0)
 
-    made = send_strips(scalars, next2[...], size_x, size_y)
-    for which in range(count):
+    made = send_strips(scalars, next2[...], size_x, size_y) if sends else []
+    for which in range(sends):
         if not tangent:
             strip_out[which][...] = made[which]
         else:
@@ -267,14 +267,14 @@
     return struct(shape[0] + 8, 2, shape[1] + 16, LANES)
 
 
-def pressure_steps(shape, count, at, source, wave, pieces, prev, speed, perturb):
+def pressure_steps(shape, count, sends, at, source, wave, pieces, prev, speed, perturb):
     own, near, far, strips, near_strips, corners = pieces
     outs = [ring_struct(shape), struct(*shape), ring_struct(shape)]
     outs += [struct(shape[0], 2, shape[1], LANES)]
-    outs += [struct(shape[0], 8, shape[2])] * count
+    outs += [struct(shape[0], 8, shape[2])] * sends
     args = [own, near, far, *strips, *near_strips, *corners, prev, speed, perturb]
     out = pl.pallas_call(
-        functools.partial(step_pair_kernel, count, False, False, at),
+        functools.partial(step_pair_kernel, count, sends, False, False, at),
         out_shape=outs,
         in_specs=[pl.BlockSpec(memory_space=pl.ANY)] * 2 + [VMEM] * len(args),
         out_specs=[VMEM] * len(outs),
@@ -291,11 +291,11 @@
     return out[0], out[1], out[2], out[3], list(out[4:])
 
 
-def tangent_steps(shape, count, pieces, prev, speed, drive1, drive2, partner_strips):
+def tangent_steps(shape, count, sends, pieces, prev, speed, drive1, drive2, partner_strips):
     blank = pieces is None
     outs = [ring_struct(shape), struct(*shape)]
-    outs += [struct(2 * shape[0], 8, shape[2])] * count
-    outs += [struct(8, 8, shape[2])] * count
+    outs += [struct(2 * shape[0], 8, shape[2])] * sends
+    outs += [struct(8, 8, shape[2])] * sends
     args = []
     if not blank:
         own, near, far, strips, near_strips, corners, done = pieces
@@ -312,7 +312,7 @@
         args = [wide, prev]
     args += [speed, drive1, drive2, *partner_strips]
     out = pl.pallas_call(
-        functools.partial(step_pair_kernel, count, True, blank, 0),
+        functools.partial(step_pair_kernel, count, sends, True, blank, 0),
         out_shape=outs,
         in_specs=[VMEM] * len(args),
         out_specs=[VMEM] * len(outs),
@@ -320,7 +320,7 @@
         cost_estimate=cost(900_000_000, 400_000_000),
         name="tangent_steps",
     )(*args)
-    return out[0], out[1], list(out[2 : 2 + count]), list(out[2 + count :])
+    return out[0], out[1], list(out[2 : 2 + sends]), list(out[2 + sends :])
 
 
 def pack_kernel(count, p_now, p_prev, speed, perturb, far, near, *rest):
@@ -629,17 +629,18 @@
     earlier = []
     traces = observed.reshape(steps, -1)
     for step in range(0, steps, 2):
+        last = step + 2 >= steps
+        sends = 0 if last else count
         around = (strips, near_strips, corners)
         p_pieces = (p_cur, p_near, p_far) + around
         q_pieces = None if q_cur is None else (q_cur, q_near, q_far) + around + (earlier[-1],)
         p_prev, p_cur, drive1, drive2, p_strips = pressure_steps(
-            shape, count, step, source_pos, wavelet, p_pieces, p_prev, speed, perturb
+            shape, count, sends, step, source_pos, wavelet, p_pieces, p_prev, speed, perturb
         )
-        last = step + 2 >= steps
         if not last:
             p_far, p_near = swap_far(p_cur), swap_near(p_cur)
         q_prev, q_cur, strips, corners = tangent_steps(
-            shape, count, q_pieces, q_prev, speed, drive1, drive2, p_strips
+            shape, count, sends, q_pieces, q_prev, speed, drive1, drive2, p_strips
         )
         if not last:
             strips, near_strips, corners = swap_strips(strips, corners)

time: 104 us -> 103 us (level)
  no operation moved by 1% of the time
where the time goes in v5:
time: 103 us; the launch traced here: 102 us
  starting transfers between devices  60 us (58%)
  Pallas kernels  24.4 us (24%)
  waiting for transfers between devices  14 us (14%)
  local copies, waits for them, and re-layouts  2.88 us (3%)
  between operations  1.2 us (1%)
    ppermute x12, starting transfers between devices, swap_near(): return lax.ppermute(value, 'gx', near_x)  38.9 us
    pallas_call x4, Pallas kernels, pressure_steps(): pl.pallas_call(functools.partial(step_pair_kernel, count, sends, False, F...  9.37 us
    all_to_all x1, starting transfers between devices, on_device(): sums = lax.all_to_all(spread, AXES, 0, 0)  7.46 us
    pallas_call x4, Pallas kernels, tangent_steps(): pl.pallas_call(functools.partial(step_pair_kernel, count, sends, True, bl...  7.02 us
    all_to_all x1, waiting for transfers between devices, on_device(): sums = lax.all_to_all(spread, AXES, 0, 0)  6.25 us
    ppermute x4, starting transfers between devices, swap_strips(): lax.ppermute(value, 'gy', pairs)  5.61 us
    ppermute x8, starting transfers between devices, swap_far(): return lax.ppermute(value, 'gx', far_x)  5.39 us
    ppermute x4, waiting for transfers between devices, swap_strips(): lax.ppermute(value, 'gy', pairs)  5.17 us
  transfers between devices with their start and end apart: 29, of which 6 were waited for; matrix products, arithmetic and copies ran while one was open for 0% of the time, Pallas kernels for 13%

profile of v5, /device:TPU:0, one launch (start us, length us, event | category | flops | bytes accessed | tf_op | source)
XLA Modules:
  0.0 102.4 jit_solution(9478467812776198627)
XLA Ops:
  0.7 2.4 %pack.1 = (f32[12,32,256]{2,1,0:T(8,128)}, f32[12,32,256]{2,1,0:T(8,128)}, f32[32,8,256]{2,1,0:T(8,128)}, f32[8,8,256]{2,1,0:T(8,128)}) custom-call(f32[8,32,256]{2,1,0:T(8,128)} %refs_2_.1, f32[8,32,256]{2,1,0:T(8,128)} %p_prev.3, f32[8,32,256]{2,1,0:T(8,128)} %speed.5, f32[8,32,256]{2,1,0:T(8,128)} %perturb.3), custom_call_target="tpu_custom_call" | custom-call | flops 10000 | bytes 3000000 | tf_op jit(solution)/shard_map/pack/pallas_call | solution.py:357
  3.1 3.0 %collective-permute-start.2 = (f32[32,8,256]{2,1,0:T(8,128)}, f32[32,8,256]{2,1,0:T(8,128)S(1)}, u32[]{:S(2)}, u32[]{:S(2)}) collective-permute-start(f32[32,8,256]{2,1,0:T(8,128)} %get-tuple-element.61), channel_id=1, source_target_pairs={{0,1},{1,0},{2,3},{3,2},{4,5},{5,4},{6,7},{7,6},{8,9},{9,8},{10,11... | collective-permute-start | bytes 786440 | tf_op jit(solution)/shard_map/ppermute | solution.py:604
  6.1 0.7 collective-permute-start.1
  7.4 5.2 %collective-permute-done.2.refs_0_.refs_5_ = f32[32,8,256]{2,1,0:T(8,128)S(1)} collective-permute-done((f32[32,8,256]{2,1,0:T(8,128)}, f32[32,8,256]{2,1,0:T(8,128)S(1)}, u32[]{:S(2)}, u32[]{:S(2)}) %collective-permute-start.2) | collective-permute-done | bytes 262176 | tf_op jit(solution)/shard_map/ppermute | solution.py:604
  14.4 0.9 copy-done
  15.4 0.9 copy-done.2
  16.3 0.9 copy-done.3
  17.5 2.3 %pressure_steps.4 = (f32[16,2,48,128]{3,2,1,0:T(8,128)S(1)}, f32[8,32,256]{2,1,0:T(8,128)S(1)}, f32[16,2,48,128]{3,2,1,0:T(8,128)S(1)}, f32[8,2,32,128]{3,2,1,0:T(8,128)S(1)}, f32[8,8,256]{2,1,0:T(8,128)S(1)}) custom-call(s32[3]{0:T(128)S(1)} %copy-done.5, f32[8]{0:T(128)S(1)} %copy-done.6, f32[8,32,256]{2,1,0:T(8,128)S(1)} %copy-done.4, ...), custom_call_target="tpu_custom_call" | custom-call | flops 900000000 | bytes 400000000 | tf_op jit(solution)/shard_map/pressure_steps/pallas_call | solution.py:276
  19.8 0.7 collective-permute-start.8
  20.5 9.5 %collective-permute-start.7 = (f32[8,32,256]{2,1,0:T(8,128)S(1)}, f32[8,32,256]{2,1,0:T(8,128)S(1)}, u32[]{:S(2)}, u32[]{:S(2)}) collective-permute-start(f32[8,32,256]{2,1,0:T(8,128)S(1)} %get-tuple-element.66.refs_2_.p2), channel_id=1, source_target_pairs={{0,2},{2,0},{4,6},{6,4},{8,10},{10,8},{12,14},{14,12},{16,18},{18,... | collective-permute-start | bytes 786440 | tf_op jit(solution)/shard_map/ppermute | solution.py:598
  31.9 0.7 collective-permute-start.15
  32.6 7.7 %collective-permute-start.14 = (f32[8,32,256]{2,1,0:T(8,128)S(1)}, f32[8,32,256]{2,1,0:T(8,128)S(1)}, u32[]{:S(2)}, u32[]{:S(2)}) collective-permute-start(f32[8,32,256]{2,1,0:T(8,128)S(1)} %get-tuple-element.74.q2.own), channel_id=1, source_target_pairs={{0,2},{2,0},{4,6},{6,4},{8,10},{10,8},{12,14},{14,12},{16,18},{18,... | collective-permute-start | bytes 786440 | tf_op jit(solution)/shard_map/ppermute | solution.py:598
  41.7 2.3 %pressure_steps.5 = (f32[16,2,48,128]{3,2,1,0:T(8,128)S(1)}, f32[8,32,256]{2,1,0:T(8,128)S(1)}, f32[16,2,48,128]{3,2,1,0:T(8,128)S(1)}, f32[8,2,32,128]{3,2,1,0:T(8,128)S(1)}, f32[8,8,256]{2,1,0:T(8,128)S(1)}) custom-call(s32[3]{0:T(128)S(1)} %copy-done.5, f32[8]{0:T(128)S(1)} %copy-done.6, f32[8,32,256]{2,1,0:T(8,128)S(1)} %get-tuple-element.66.refs_2_.p2, ...), custom_call_target="tpu_custom_call" | custom-call | flops 900000000 | bytes 400000000 | tf_op jit(solution)/shard_map/pressure_steps/pallas_call | solution.py:276
  44.0 0.7 collective-permute-start.13
  44.7 3.8 %collective-permute-start.12 = (f32[8,32,256]{2,1,0:T(8,128)S(1)}, f32[8,32,256]{2,1,0:T(8,128)S(1)}, u32[]{:S(2)}, u32[]{:S(2)}) collective-permute-start(f32[8,32,256]{2,1,0:T(8,128)S(1)} %get-tuple-element.73.refs_2_.p2), channel_id=1, source_target_pairs={{0,2},{2,0},{4,6},{6,4},{8,10},{10,8},{12,14},{14,12},{16,18},{18,... | collective-permute-start | bytes 786440 | tf_op jit(solution)/shard_map/ppermute | solution.py:598
  48.6 2.1 %tangent_steps.5 = (f32[16,2,48,128]{3,2,1,0:T(8,128)S(1)}, f32[8,32,256]{2,1,0:T(8,128)S(1)}, f32[16,8,256]{2,1,0:T(8,128)S(1)}, f32[8,8,256]{2,1,0:T(8,128)S(1)}) custom-call(f32[24,2,64,128]{3,2,1,0:T(8,128)S(1)} %place.3.refs_0_, f32[16,2,48,128]{3,2,1,0:T(8,128)S(1)} %get-tuple-element.75.q1.refs_1_, ...), custom_call_target="tpu_custom_call" | custom-call | flops 900000000 | bytes 400000000 | tf_op jit(solution)/shard_map/tangent_steps/pallas_call | solution.py:314
  50.7 1.4 %collective-permute-start.16 = (f32[16,8,256]{2,1,0:T(8,128)S(1)}, f32[16,8,256]{2,1,0:T(8,128)S(1)}, u32[]{:S(2)}, u32[]{:S(2)}) collective-permute-start(f32[16,8,256]{2,1,0:T(8,128)S(1)} %get-tuple-element.80), channel_id=1, source_target_pairs={{0,1},{1,0},{2,3},{3,2},{4,5},{5,4},{6,7},{7,6},{8,9},{9,8},{10,11... | collective-permute-start | bytes 393224 | tf_op jit(solution)/shard_map/ppermute | solution.py:604
  52.8 0.7 collective-permute-start.22
  53.5 5.6 %collective-permute-start.21 = (f32[8,32,256]{2,1,0:T(8,128)S(1)}, f32[8,32,256]{2,1,0:T(8,128)S(1)}, u32[]{:S(2)}, u32[]{:S(2)}) collective-permute-start(f32[8,32,256]{2,1,0:T(8,128)S(1)} %get-tuple-element.84.q2.own), channel_id=1, source_target_pairs={{0,2},{2,0},{4,6},{6,4},{8,10},{10,8},{12,14},{14,12},{16,18},{18,... | collective-permute-start | bytes 786440 | tf_op jit(solution)/shard_map/ppermute | solution.py:598
  60.5 2.5 %pressure_steps.6 = (f32[16,2,48,128]{3,2,1,0:T(8,128)S(1)}, f32[8,32,256]{2,1,0:T(8,128)S(1)}, f32[16,2,48,128]{3,2,1,0:T(8,128)S(1)}, f32[8,2,32,128]{3,2,1,0:T(8,128)S(1)}, f32[8,8,256]{2,1,0:T(8,128)S(1)}) custom-call(s32[3]{0:T(128)S(1)} %copy-done.5, f32[8]{0:T(128)S(1)} %copy-done.6, f32[8,32,256]{2,1,0:T(8,128)S(1)} %get-tuple-element.73.refs_2_.p2, ...), custom_call_target="tpu_custom_call" | custom-call | flops 900000000 | bytes 400000000 | tf_op jit(solution)/shard_map/pressure_steps/pallas_call | solution.py:276
  63.1 2.1 %tangent_steps.6 = (f32[16,2,48,128]{3,2,1,0:T(8,128)S(1)}, f32[8,32,256]{2,1,0:T(8,128)S(1)}, f32[16,8,256]{2,1,0:T(8,128)S(1)}, f32[8,8,256]{2,1,0:T(8,128)S(1)}) custom-call(f32[24,2,64,128]{3,2,1,0:T(8,128)S(1)} %place.4.refs_0_, f32[16,2,48,128]{3,2,1,0:T(8,128)S(1)} %get-tuple-element.85.q1.refs_1_, ...), custom_call_target="tpu_custom_call" | custom-call | flops 900000000 | bytes 400000000 | tf_op jit(solution)/shard_map/tangent_steps/pallas_call | solution.py:314
  66.5 6.5 %collective-permute-start.19 = (f32[8,32,256]{2,1,0:T(8,128)S(1)}, f32[8,32,256]{2,1,0:T(8,128)S(1)}, u32[]{:S(2)}, u32[]{:S(2)}) collective-permute-start(f32[8,32,256]{2,1,0:T(8,128)S(1)} %get-tuple-element.83.refs_2_.p2), channel_id=1, source_target_pairs={{0,2},{2,0},{4,6},{6,4},{8,10},{10,8},{12,14},{14,12},{16,18},{18,... | collective-permute-start | bytes 786440 | tf_op jit(solution)/shard_map/ppermute | solution.py:598
  73.6 0.7 collective-permute-start.27
  74.3 5.1 %collective-permute-start.26 = (f32[8,32,256]{2,1,0:T(8,128)S(1)}, f32[8,32,256]{2,1,0:T(8,128)S(1)}, u32[]{:S(2)}, u32[]{:S(2)}) collective-permute-start(f32[8,32,256]{2,1,0:T(8,128)S(1)} %get-tuple-element.94.q2.own), channel_id=1, source_target_pairs={{0,2},{2,0},{4,6},{6,4},{8,10},{10,8},{12,14},{14,12},{16,18},{18,... | collective-permute-start | bytes 786440 | tf_op jit(solution)/shard_map/ppermute | solution.py:598
  80.1 0.7 collective-permute-done.24.refs_6_.refs_1_
  80.8 2.3 %pressure_steps.7 = (f32[16,2,48,128]{3,2,1,0:T(8,128)S(1)}, f32[8,32,256]{2,1,0:T(8,128)S(1)}, f32[16,2,48,128]{3,2,1,0:T(8,128)S(1)}, f32[8,2,32,128]{3,2,1,0:T(8,128)S(1)}) custom-call(s32[3]{0:T(128)S(1)} %copy-done.5, f32[8]{0:T(128)S(1)} %copy-done.6, f32[8,32,256]{2,1,0:T(8,128)S(1)} %get-tuple-element.83.refs_2_.p2, ...), custom_call_target="tpu_custom_call" | custom-call | flops 900000000 | bytes 400000000 | tf_op jit(solution)/shard_map/pressure_steps/pallas_call | solution.py:276
  83.2 2.1 %tangent_steps.7 = (f32[16,2,48,128]{3,2,1,0:T(8,128)S(1)}, f32[8,32,256]{2,1,0:T(8,128)S(1)}) custom-call(f32[24,2,64,128]{3,2,1,0:T(8,128)S(1)} %place.5.refs_0_, f32[16,2,48,128]{3,2,1,0:T(8,128)S(1)} %get-tuple-element.95.q1.refs_1_, f32[16,2,48,128]{3,2,1,0:T(8,128)S(1)} %get-tuple-element.65.refs_9_.refs_0_.refs_2_, ...), custom_call_target="tpu_custom_call" | custom-call | flops 900000000 | bytes 400000000 | tf_op jit(solution)/shard_map/tangent_steps/pallas_call | solution.py:314
  85.4 1.4 %receive.7 = (f32[8,128]{1,0:T(8,128)S(1)}, f32[8,128]{1,0:T(8,128)S(1)}, f32[32,1,128]{2,1,0:T(1,128)}) custom-call(s32[1,128]{1,0:T(1,128)S(1)} %bitcast.6, f32[16,2,48,128]{3,2,1,0:T(8,128)S(1)} %get-tuple-element.102.p1, f32[8,32,256]{2,1,0:T(8,128)S(1)} %get-tuple-element.93.p_in.p2, f32[16,2,48,128]{3,2,1,0:T(8,128)S(1)} %get-tuple-element.103.q1, ...), custom_call_target="tpu_custom_call" | custom-call | flops 20000000 | bytes 2500000 | tf_op jit(solution)/shard_map/receive/pallas_call | solution.py:486
  86.8 7.5 %all-to-all-start = ((f32[32,1,128]{2,1,0:T(1,128)}), f32[32,1,128]{2,1,0:T(1,128)S(1)}, u32[]{:S(2)}, u32[]{:S(2)}) async-start(f32[32,1,128]{2,1,0:T(1,128)} %get-tuple-element.108), calls=%async_computation | async-start | bytes 32768 | tf_op jit(solution)/shard_map/all_to_all | solution.py:658
  94.2 0.9 smooth.1
  95.1 6.2 %all-to-all-done.sums = f32[32,1,128]{2,1,0:T(1,128)S(1)} async-done(((f32[32,1,128]{2,1,0:T(1,128)}), f32[32,1,128]{2,1,0:T(1,128)S(1)}, u32[]{:S(2)}, u32[]{:S(2)}) %all-to-all-start) | async-done | bytes 16416 | tf_op jit(solution)/shard_map/all_to_all | solution.py:658
  101.4 0.9 finish.1
  (63 shorter events, 10.9 us)
Async XLA Ops:
  0.6 16.9 %copy-start.4 = (f32[8,32,256]{2,1,0:T(8,128)S(1)}, f32[8,32,256]{2,1,0:T(8,128)}, u32[]{:S(2)}) copy-start(f32[8,32,256]{2,1,0:T(8,128)} %refs_2_.1) | copy-start | bytes 786436
  0.6 16.9 %copy-start.6 = (f32[8]{0:T(128)S(1)}, f32[8]{0:T(128)}, u32[]{:S(2)}) copy-start(f32[8]{0:T(128)} %refs_1_.7) | copy-start | bytes 100
  0.7 16.9 %copy-start.5 = (s32[3]{0:T(128)S(1)}, s32[3]{0:T(128)}, u32[]{:S(2)}) copy-start(s32[3]{0:T(128)} %refs_0_.7) | copy-start | bytes 40
  3.1 9.5 %collective-permute-start.2 = (f32[32,8,256]{2,1,0:T(8,128)}, f32[32,8,256]{2,1,0:T(8,128)S(1)}, u32[]{:S(2)}, u32[]{:S(2)}) collective-permute-start(f32[32,8,256]{2,1,0:T(8,128)} %get-tuple-element.61), channel_id=1, source_target_pairs={{0,1},{1,0},{2,3},{3,2},{4,5},{5,4},{6,7},{7,6},{8,9},{9,8},{10,11... | collective-permute-start | bytes 786440 | tf_op jit(solution)/shard_map/ppermute | solution.py:604
  6.1 7.7 %collective-permute-start = (f32[12,32,256]{2,1,0:T(8,128)}, f32[12,32,256]{2,1,0:T(8,128)S(1)}, u32[]{:S(2)}, u32[]{:S(2)}) collective-permute-start(f32[12,32,256]{2,1,0:T(8,128)} %get-tuple-element.59), channel_id=1, source_target_pairs={{0,2},{2,0},{4,6},{6,4},{8,10},{10,8},{12,14},{14,12},{16,18},{18,... | collective-permute-start | bytes 1179656 | tf_op jit(solution)/shard_map/ppermute | solution.py:598
  6.1 7.7 %collective-permute-start.1 = (f32[12,32,256]{2,1,0:T(8,128)}, f32[12,32,256]{2,1,0:T(8,128)S(1)}, u32[]{:S(2)}, u32[]{:S(2)}) collective-permute-start(f32[12,32,256]{2,1,0:T(8,128)} %get-tuple-element.60), channel_id=1, source_target_pairs={{2,4},{4,2},{6,8},{8,6},{10,12},{12,10},{14,16},{16,14},{18,20},{2... | collective-permute-start | bytes 1179656 | tf_op jit(solution)/shard_map/ppermute | solution.py:601
  6.7 6.3 %collective-permute-start.4 = (f32[8,8,256]{2,1,0:T(8,128)}, f32[8,8,256]{2,1,0:T(8,128)S(1)}, u32[]{:S(2)}, u32[]{:S(2)}) collective-permute-start(f32[8,8,256]{2,1,0:T(8,128)} %get-tuple-element.62), channel_id=1, source_target_pairs={{2,5},{3,4},{4,3},{5,2},{6,9},{7,8},{8,7},{9,6},{10,13},{11,12},{1... | collective-permute-start | bytes 196616 | tf_op jit(solution)/shard_map/ppermute | solution.py:606
  12.6 1.9 %collective-permute-start.3 = (f32[32,8,256]{2,1,0:T(8,128)S(1)}, f32[32,8,256]{2,1,0:T(8,128)S(1)}, u32[]{:S(2)}, u32[]{:S(2)}) collective-permute-start(f32[32,8,256]{2,1,0:T(8,128)S(1)} %collective-permute-done.2.refs_0_.refs_5_), channel_id=1, source_target_pairs={{0,2},{2,0},{4,6},{6,4},{8,10},{10,8},{12,14},{14,12},{16,18},{18,... | collective-permute-start | bytes 786440 | tf_op jit(solution)/shard_map/ppermute | solution.py:598
  12.6 4.9 %collective-permute-start.5 = (f32[8,32,256]{2,1,0:T(8,128)}, f32[8,32,256]{2,1,0:T(8,128)S(1)}, u32[]{:S(2)}, u32[]{:S(2)}) collective-permute-start(f32[8,32,256]{2,1,0:T(8,128)} %refs_2_.1), channel_id=1, source_target_pairs={{0,2},{2,0},{4,6},{6,4},{8,10},{10,8},{12,14},{14,12},{16,18},{18,... | collective-permute-start | bytes 786440 | tf_op jit(solution)/shard_map/ppermute | solution.py:598
  13.1 4.4 %collective-permute-start.6 = (f32[8,32,256]{2,1,0:T(8,128)}, f32[8,32,256]{2,1,0:T(8,128)S(1)}, u32[]{:S(2)}, u32[]{:S(2)}) collective-permute-start(f32[8,32,256]{2,1,0:T(8,128)} %refs_2_.1), channel_id=1, source_target_pairs={{2,4},{4,2},{6,8},{8,6},{10,12},{12,10},{14,16},{16,14},{18,20},{2... | collective-permute-start | bytes 786440 | tf_op jit(solution)/shard_map/ppermute | solution.py:601
  19.8 21.3 %collective-permute-start.8 = (f32[8,32,256]{2,1,0:T(8,128)S(1)}, f32[8,32,256]{2,1,0:T(8,128)S(1)}, u32[]{:S(2)}, u32[]{:S(2)}) collective-permute-start(f32[8,32,256]{2,1,0:T(8,128)S(1)} %get-tuple-element.66.refs_2_.p2), channel_id=1, source_target_pairs={{2,4},{4,2},{6,8},{8,6},{10,12},{12,10},{14,16},{16,14},{18,20},{2... | collective-permute-start | bytes 786440 | tf_op jit(solution)/shard_map/ppermute | solution.py:601
  20.5 20.6 %collective-permute-start.7 = (f32[8,32,256]{2,1,0:T(8,128)S(1)}, f32[8,32,256]{2,1,0:T(8,128)S(1)}, u32[]{:S(2)}, u32[]{:S(2)}) collective-permute-start(f32[8,32,256]{2,1,0:T(8,128)S(1)} %get-tuple-element.66.refs_2_.p2), channel_id=1, source_target_pairs={{0,2},{2,0},{4,6},{6,4},{8,10},{10,8},{12,14},{14,12},{16,18},{18,... | collective-permute-start | bytes 786440 | tf_op jit(solution)/shard_map/ppermute | solution.py:598
  30.6 9.7 %collective-permute-start.9 = (f32[16,8,256]{2,1,0:T(8,128)S(1)}, f32[16,8,256]{2,1,0:T(8,128)S(1)}, u32[]{:S(2)}, u32[]{:S(2)}) collective-permute-start(f32[16,8,256]{2,1,0:T(8,128)S(1)} %get-tuple-element.70), channel_id=1, source_target_pairs={{0,1},{1,0},{2,3},{3,2},{4,5},{5,4},{6,7},{7,6},{8,9},{9,8},{10,11... | collective-permute-start | bytes 393224 | tf_op jit(solution)/shard_map/ppermute | solution.py:604
  31.2 1.3 %collective-permute-start.11 = (f32[8,8,256]{2,1,0:T(8,128)S(1)}, f32[8,8,256]{2,1,0:T(8,128)S(1)}, u32[]{:S(2)}, u32[]{:S(2)}) collective-permute-start(f32[8,8,256]{2,1,0:T(8,128)S(1)} %get-tuple-element.71), channel_id=1, source_target_pairs={{2,5},{3,4},{4,3},{5,2},{6,9},{7,8},{8,7},{9,6},{10,13},{11,12},{1... | collective-permute-start | bytes 196616 | tf_op jit(solution)/shard_map/ppermute | solution.py:606
  31.9 16.6 %collective-permute-start.15 = (f32[8,32,256]{2,1,0:T(8,128)S(1)}, f32[8,32,256]{2,1,0:T(8,128)S(1)}, u32[]{:S(2)}, u32[]{:S(2)}) collective-permute-start(f32[8,32,256]{2,1,0:T(8,128)S(1)} %get-tuple-element.74.q2.own), channel_id=1, source_target_pairs={{2,4},{4,2},{6,8},{8,6},{10,12},{12,10},{14,16},{16,14},{18,20},{2... | collective-permute-start | bytes 786440 | tf_op jit(solution)/shard_map/ppermute | solution.py:601
  32.6 15.9 %collective-permute-start.14 = (f32[8,32,256]{2,1,0:T(8,128)S(1)}, f32[8,32,256]{2,1,0:T(8,128)S(1)}, u32[]{:S(2)}, u32[]{:S(2)}) collective-permute-start(f32[8,32,256]{2,1,0:T(8,128)S(1)} %get-tuple-element.74.q2.own), channel_id=1, source_target_pairs={{0,2},{2,0},{4,6},{6,4},{8,10},{10,8},{12,14},{14,12},{16,18},{18,... | collective-permute-start | bytes 786440 | tf_op jit(solution)/shard_map/ppermute | solution.py:598
  40.3 1.3 %collective-permute-start.10 = (f32[16,8,256]{2,1,0:T(8,128)S(1)}, f32[16,8,256]{2,1,0:T(8,128)S(1)}, u32[]{:S(2)}, u32[]{:S(2)}) collective-permute-start(f32[16,8,256]{2,1,0:T(8,128)S(1)} %collective-permute-done.9.refs_5_.refs_0_), channel_id=1, source_target_pairs={{0,2},{2,0},{4,6},{6,4},{8,10},{10,8},{12,14},{14,12},{16,18},{18,... | collective-permute-start | bytes 393224 | tf_op jit(solution)/shard_map/ppermute | solution.py:598
  44.0 15.8 %collective-permute-start.13 = (f32[8,32,256]{2,1,0:T(8,128)S(1)}, f32[8,32,256]{2,1,0:T(8,128)S(1)}, u32[]{:S(2)}, u32[]{:S(2)}) collective-permute-start(f32[8,32,256]{2,1,0:T(8,128)S(1)} %get-tuple-element.73.refs_2_.p2), channel_id=1, source_target_pairs={{2,4},{4,2},{6,8},{8,6},{10,12},{12,10},{14,16},{16,14},{18,20},{2... | collective-permute-start | bytes 786440 | tf_op jit(solution)/shard_map/ppermute | solution.py:601
  44.7 15.2 %collective-permute-start.12 = (f32[8,32,256]{2,1,0:T(8,128)S(1)}, f32[8,32,256]{2,1,0:T(8,128)S(1)}, u32[]{:S(2)}, u32[]{:S(2)}) collective-permute-start(f32[8,32,256]{2,1,0:T(8,128)S(1)} %get-tuple-element.73.refs_2_.p2), channel_id=1, source_target_pairs={{0,2},{2,0},{4,6},{6,4},{8,10},{10,8},{12,14},{14,12},{16,18},{18,... | collective-permute-start | bytes 786440 | tf_op jit(solution)/shard_map/ppermute | solution.py:598
  50.7 8.4 %collective-permute-start.16 = (f32[16,8,256]{2,1,0:T(8,128)S(1)}, f32[16,8,256]{2,1,0:T(8,128)S(1)}, u32[]{:S(2)}, u32[]{:S(2)}) collective-permute-start(f32[16,8,256]{2,1,0:T(8,128)S(1)} %get-tuple-element.80), channel_id=1, source_target_pairs={{0,1},{1,0},{2,3},{3,2},{4,5},{5,4},{6,7},{7,6},{8,9},{9,8},{10,11... | collective-permute-start | bytes 393224 | tf_op jit(solution)/shard_map/ppermute | solution.py:604
  52.1 1.3 %collective-permute-start.18 = (f32[8,8,256]{2,1,0:T(8,128)S(1)}, f32[8,8,256]{2,1,0:T(8,128)S(1)}, u32[]{:S(2)}, u32[]{:S(2)}) collective-permute-start(f32[8,8,256]{2,1,0:T(8,128)S(1)} %get-tuple-element.81), channel_id=1, source_target_pairs={{2,5},{3,4},{4,3},{5,2},{6,9},{7,8},{8,7},{9,6},{10,13},{11,12},{1... | collective-permute-start | bytes 196616 | tf_op jit(solution)/shard_map/ppermute | solution.py:606
  52.8 10.2 %collective-permute-start.22 = (f32[8,32,256]{2,1,0:T(8,128)S(1)}, f32[8,32,256]{2,1,0:T(8,128)S(1)}, u32[]{:S(2)}, u32[]{:S(2)}) collective-permute-start(f32[8,32,256]{2,1,0:T(8,128)S(1)} %get-tuple-element.84.q2.own), channel_id=1, source_target_pairs={{2,4},{4,2},{6,8},{8,6},{10,12},{12,10},{14,16},{16,14},{18,20},{2... | collective-permute-start | bytes 786440 | tf_op jit(solution)/shard_map/ppermute | solution.py:601
  53.5 9.5 %collective-permute-start.21 = (f32[8,32,256]{2,1,0:T(8,128)S(1)}, f32[8,32,256]{2,1,0:T(8,128)S(1)}, u32[]{:S(2)}, u32[]{:S(2)}) collective-permute-start(f32[8,32,256]{2,1,0:T(8,128)S(1)} %get-tuple-element.84.q2.own), channel_id=1, source_target_pairs={{0,2},{2,0},{4,6},{6,4},{8,10},{10,8},{12,14},{14,12},{16,18},{18,... | collective-permute-start | bytes 786440 | tf_op jit(solution)/shard_map/ppermute | solution.py:598
  59.1 1.3 %collective-permute-start.17 = (f32[16,8,256]{2,1,0:T(8,128)S(1)}, f32[16,8,256]{2,1,0:T(8,128)S(1)}, u32[]{:S(2)}, u32[]{:S(2)}) collective-permute-start(f32[16,8,256]{2,1,0:T(8,128)S(1)} %collective-permute-done.16.refs_5_.refs_0_), channel_id=1, source_target_pairs={{0,2},{2,0},{4,6},{6,4},{8,10},{10,8},{12,14},{14,12},{16,18},{18,... | collective-permute-start | bytes 393224 | tf_op jit(solution)/shard_map/ppermute | solution.py:598
  65.2 14.3 %collective-permute-start.23 = (f32[16,8,256]{2,1,0:T(8,128)S(1)}, f32[16,8,256]{2,1,0:T(8,128)S(1)}, u32[]{:S(2)}, u32[]{:S(2)}) collective-permute-start(f32[16,8,256]{2,1,0:T(8,128)S(1)} %get-tuple-element.90), channel_id=1, source_target_pairs={{0,1},{1,0},{2,3},{3,2},{4,5},{5,4},{6,7},{7,6},{8,9},{9,8},{10,11... | collective-permute-start | bytes 393224 | tf_op jit(solution)/shard_map/ppermute | solution.py:604
  65.8 15.0 %collective-permute-start.20 = (f32[8,32,256]{2,1,0:T(8,128)S(1)}, f32[8,32,256]{2,1,0:T(8,128)S(1)}, u32[]{:S(2)}, u32[]{:S(2)}) collective-permute-start(f32[8,32,256]{2,1,0:T(8,128)S(1)} %get-tuple-element.83.refs_2_.p2), channel_id=1, source_target_pairs={{2,4},{4,2},{6,8},{8,6},{10,12},{12,10},{14,16},{16,14},{18,20},{2... | collective-permute-start | bytes 786440 | tf_op jit(solution)/shard_map/ppermute | solution.py:601
  66.5 14.3 %collective-permute-start.19 = (f32[8,32,256]{2,1,0:T(8,128)S(1)}, f32[8,32,256]{2,1,0:T(8,128)S(1)}, u32[]{:S(2)}, u32[]{:S(2)}) collective-permute-start(f32[8,32,256]{2,1,0:T(8,128)S(1)} %get-tuple-element.83.refs_2_.p2), channel_id=1, source_target_pairs={{0,2},{2,0},{4,6},{6,4},{8,10},{10,8},{12,14},{14,12},{16,18},{18,... | collective-permute-start | bytes 786440 | tf_op jit(solution)/shard_map/ppermute | solution.py:598
  72.9 1.3 %collective-permute-start.25 = (f32[8,8,256]{2,1,0:T(8,128)S(1)}, f32[8,8,256]{2,1,0:T(8,128)S(1)}, u32[]{:S(2)}, u32[]{:S(2)}) collective-permute-start(f32[8,8,256]{2,1,0:T(8,128)S(1)} %get-tuple-element.91), channel_id=1, source_target_pairs={{2,5},{3,4},{4,3},{5,2},{6,9},{7,8},{8,7},{9,6},{10,13},{11,12},{1... | collective-permute-start | bytes 196616 | tf_op jit(solution)/shard_map/ppermute | solution.py:606
  73.6 9.5 %collective-permute-start.27 = (f32[8,32,256]{2,1,0:T(8,128)S(1)}, f32[8,32,256]{2,1,0:T(8,128)S(1)}, u32[]{:S(2)}, u32[]{:S(2)}) collective-permute-start(f32[8,32,256]{2,1,0:T(8,128)S(1)} %get-tuple-element.94.q2.own), channel_id=1, source_target_pairs={{2,4},{4,2},{6,8},{8,6},{10,12},{12,10},{14,16},{16,14},{18,20},{2... | collective-permute-start | bytes 786440 | tf_op jit(solution)/shard_map/ppermute | solution.py:601
  74.3 8.8 %collective-permute-start.26 = (f32[8,32,256]{2,1,0:T(8,128)S(1)}, f32[8,32,256]{2,1,0:T(8,128)S(1)}, u32[]{:S(2)}, u32[]{:S(2)}) collective-permute-start(f32[8,32,256]{2,1,0:T(8,128)S(1)} %get-tuple-element.94.q2.own), channel_id=1, source_target_pairs={{0,2},{2,0},{4,6},{6,4},{8,10},{10,8},{12,14},{14,12},{16,18},{18,... | collective-permute-start | bytes 786440 | tf_op jit(solution)/shard_map/ppermute | solution.py:598
  79.4 1.3 %collective-permute-start.24 = (f32[16,8,256]{2,1,0:T(8,128)S(1)}, f32[16,8,256]{2,1,0:T(8,128)S(1)}, u32[]{:S(2)}, u32[]{:S(2)}) collective-permute-start(f32[16,8,256]{2,1,0:T(8,128)S(1)} %collective-permute-done.23.refs_5_.refs_0_), channel_id=1, source_target_pairs={{0,2},{2,0},{4,6},{6,4},{8,10},{10,8},{12,14},{14,12},{16,18},{18,... | collective-permute-start | bytes 393224 | tf_op jit(solution)/shard_map/ppermute | solution.py:598
  86.8 14.6 %all-to-all-start = ((f32[32,1,128]{2,1,0:T(1,128)}), f32[32,1,128]{2,1,0:T(1,128)S(1)}, u32[]{:S(2)}, u32[]{:S(2)}) async-start(f32[32,1,128]{2,1,0:T(1,128)} %get-tuple-element.108), calls=%async_computation | async-start | bytes 32768 | tf_op jit(solution)/shard_map/all_to_all | solution.py:658
  (6 other events, 39.8 us)

commit v6 on v5

--- a/solution.py
+++ b/solution.py
@@ -415,7 +415,7 @@
 
 
 def receive_kernel(rounds, cells, p1, p2, q1, q2, *refs):
-    size_x, size_y, size_z = p2.shape
+    size_x, size_y, size_z = q2.shape
     if rounds == 0:
         observed, refs = refs[0], refs[1:]
         refs[2][...] = observed[...]
@@ -452,6 +452,9 @@
         return total
 
     for one, two, target in ((p1, p2, synth), (q1, q2, born)):
+        if rounds > 0 and target is synth:
+            target[steps - 2 : steps, :] = one[...]
+            continue
         first = [
             one[4 : 4 + size_x, half, 8 : 8 + size_y, :].reshape(rows, LANES) for half in range(2)
         ]
@@ -645,6 +648,8 @@
         if not last:
             strips, near_strips, corners = swap_strips(strips, corners)
             q_far, q_near = swap_far(q_cur), swap_near(q_cur)
+        if last:
+            ready = receive(cells, p_prev, p_cur, p_prev, p_cur)[0]
         if not last:
             got = list(receive(cells, p_prev, p_cur, q_prev, q_cur, (), traces))
             if step == 0:
@@ -653,7 +658,7 @@
             earlier += got
     total = count_x * count_y
     residual, born, spread = receive(
-        cells, p_prev, p_cur, q_prev, q_cur, earlier, held, total
+        cells, ready, ready, q_prev, q_cur, earlier, held, total
     )
     sums = lax.all_to_all(spread, AXES, 0, 0)
     smooth, p_cur, q_cur = smoothed(shape, perturb, p_cur, q_cur)

time: 103 us -> 103 us (level)
  starting transfers between devices: 60 us -> 58.8 us
    all_to_all x1, starting transfers between devices: 7.46 us -> 6.26 us  [on_device(): sums = lax.all_to_all(spread, AXES, 0, 0)]
    pallas_call x4 -> x5, Pallas kernels: 3.36 us -> 4.37 us  [receive(): pl.pallas_call(functools.partial(receive_kernel, rounds), out_shape=outs,...]
  transfers between devices with their start and end apart: 29 -> 29, of which waited for: 6 -> 6; matrix products, arithmetic and copies ran while one was open for 0% -> 0% of each run, Pallas kernels for 13% -> 14%
where the time goes in v6:
time: 103 us; the launch traced here: 102 us
  starting transfers between devices  58.8 us (57%)
  Pallas kernels  25.3 us (25%)
  waiting for transfers between devices  14 us (14%)
  local copies, waits for them, and re-layouts  2.88 us (3%)
  between operations  1.19 us (1%)
    ppermute x12, starting transfers between devices, swap_near(): return lax.ppermute(value, 'gx', near_x)  38.9 us
    pallas_call x4, Pallas kernels, pressure_steps(): pl.pallas_call(functools.partial(step_pair_kernel, count, sends, False, F...  9.37 us
    pallas_call x4, Pallas kernels, tangent_steps(): pl.pallas_call(functools.partial(step_pair_kernel, count, sends, True, bl...  6.99 us
    all_to_all x1, starting transfers between devices, on_device(): sums = lax.all_to_all(spread, AXES, 0, 0)  6.26 us
    all_to_all x1, waiting for transfers between devices, on_device(): sums = lax.all_to_all(spread, AXES, 0, 0)  6.25 us
    ppermute x4, starting transfers between devices, swap_strips(): lax.ppermute(value, 'gy', pairs)  5.6 us
    ppermute x8, starting transfers between devices, swap_far(): return lax.ppermute(value, 'gx', far_x)  5.39 us
    ppermute x4, waiting for transfers between devices, swap_strips(): lax.ppermute(value, 'gy', pairs)  5.17 us
  transfers between devices with their start and end apart: 29, of which 6 were waited for; matrix products, arithmetic and copies ran while one was open for 0% of the time, Pallas kernels for 14%

profile of v6, /device:TPU:0, one launch (start us, length us, event | category | flops | bytes accessed | tf_op | source)
XLA Modules:
  0.0 102.2 jit_solution(14570237552475070760)
XLA Ops:
  0.7 2.4 %pack.1 = (f32[12,32,256]{2,1,0:T(8,128)}, f32[12,32,256]{2,1,0:T(8,128)}, f32[32,8,256]{2,1,0:T(8,128)}, f32[8,8,256]{2,1,0:T(8,128)}) custom-call(f32[8,32,256]{2,1,0:T(8,128)} %refs_2_.1, f32[8,32,256]{2,1,0:T(8,128)} %p_prev.3, f32[8,32,256]{2,1,0:T(8,128)} %speed.5, f32[8,32,256]{2,1,0:T(8,128)} %perturb.3), custom_call_target="tpu_custom_call" | custom-call | flops 10000 | bytes 3000000 | tf_op jit(solution)/shard_map/pack/pallas_call | solution.py:357
  3.1 3.0 %collective-permute-start.2 = (f32[32,8,256]{2,1,0:T(8,128)}, f32[32,8,256]{2,1,0:T(8,128)S(1)}, u32[]{:S(2)}, u32[]{:S(2)}) collective-permute-start(f32[32,8,256]{2,1,0:T(8,128)} %get-tuple-element.62), channel_id=1, source_target_pairs={{0,1},{1,0},{2,3},{3,2},{4,5},{5,4},{6,7},{7,6},{8,9},{9,8},{10,11... | collective-permute-start | bytes 786440 | tf_op jit(solution)/shard_map/ppermute | solution.py:607
  7.4 5.2 %collective-permute-done.2.refs_0_.refs_5_ = f32[32,8,256]{2,1,0:T(8,128)S(1)} collective-permute-done((f32[32,8,256]{2,1,0:T(8,128)}, f32[32,8,256]{2,1,0:T(8,128)S(1)}, u32[]{:S(2)}, u32[]{:S(2)}) %collective-permute-start.2) | collective-permute-done | bytes 262176 | tf_op jit(solution)/shard_map/ppermute | solution.py:607
  14.4 0.9 copy-done
  15.4 0.9 copy-done.2
  16.3 0.9 copy-done.3
  17.5 2.3 %pressure_steps.4 = (f32[16,2,48,128]{3,2,1,0:T(8,128)S(1)}, f32[8,32,256]{2,1,0:T(8,128)S(1)}, f32[16,2,48,128]{3,2,1,0:T(8,128)S(1)}, f32[8,2,32,128]{3,2,1,0:T(8,128)S(1)}, f32[8,8,256]{2,1,0:T(8,128)S(1)}) custom-call(s32[3]{0:T(128)S(1)} %copy-done.6, f32[8]{0:T(128)S(1)} %copy-done.7, f32[8,32,256]{2,1,0:T(8,128)S(1)} %copy-done.4, ...), custom_call_target="tpu_custom_call" | custom-call | flops 900000000 | bytes 400000000 | tf_op jit(solution)/shard_map/pressure_steps/pallas_call | solution.py:276
  19.8 0.7 collective-permute-start.8
  20.5 9.5 %collective-permute-start.7 = (f32[8,32,256]{2,1,0:T(8,128)S(1)}, f32[8,32,256]{2,1,0:T(8,128)S(1)}, u32[]{:S(2)}, u32[]{:S(2)}) collective-permute-start(f32[8,32,256]{2,1,0:T(8,128)S(1)} %get-tuple-element.67.refs_2_.p2), channel_id=1, source_target_pairs={{0,2},{2,0},{4,6},{6,4},{8,10},{10,8},{12,14},{14,12},{16,18},{18,... | collective-permute-start | bytes 786440 | tf_op jit(solution)/shard_map/ppermute | solution.py:601
  31.9 0.7 collective-permute-start.15
  32.6 7.7 %collective-permute-start.14 = (f32[8,32,256]{2,1,0:T(8,128)S(1)}, f32[8,32,256]{2,1,0:T(8,128)S(1)}, u32[]{:S(2)}, u32[]{:S(2)}) collective-permute-start(f32[8,32,256]{2,1,0:T(8,128)S(1)} %get-tuple-element.75.q2.own), channel_id=1, source_target_pairs={{0,2},{2,0},{4,6},{6,4},{8,10},{10,8},{12,14},{14,12},{16,18},{18,... | collective-permute-start | bytes 786440 | tf_op jit(solution)/shard_map/ppermute | solution.py:601
  41.7 2.3 %pressure_steps.5 = (f32[16,2,48,128]{3,2,1,0:T(8,128)S(1)}, f32[8,32,256]{2,1,0:T(8,128)S(1)}, f32[16,2,48,128]{3,2,1,0:T(8,128)S(1)}, f32[8,2,32,128]{3,2,1,0:T(8,128)S(1)}, f32[8,8,256]{2,1,0:T(8,128)S(1)}) custom-call(s32[3]{0:T(128)S(1)} %copy-done.6, f32[8]{0:T(128)S(1)} %copy-done.7, f32[8,32,256]{2,1,0:T(8,128)S(1)} %get-tuple-element.67.refs_2_.p2, ...), custom_call_target="tpu_custom_call" | custom-call | flops 900000000 | bytes 400000000 | tf_op jit(solution)/shard_map/pressure_steps/pallas_call | solution.py:276
  44.0 0.7 collective-permute-start.13
  44.7 3.8 %collective-permute-start.12 = (f32[8,32,256]{2,1,0:T(8,128)S(1)}, f32[8,32,256]{2,1,0:T(8,128)S(1)}, u32[]{:S(2)}, u32[]{:S(2)}) collective-permute-start(f32[8,32,256]{2,1,0:T(8,128)S(1)} %get-tuple-element.74.refs_2_.p2), channel_id=1, source_target_pairs={{0,2},{2,0},{4,6},{6,4},{8,10},{10,8},{12,14},{14,12},{16,18},{18,... | collective-permute-start | bytes 786440 | tf_op jit(solution)/shard_map/ppermute | solution.py:601
  48.6 2.1 %tangent_steps.5 = (f32[16,2,48,128]{3,2,1,0:T(8,128)S(1)}, f32[8,32,256]{2,1,0:T(8,128)S(1)}, f32[16,8,256]{2,1,0:T(8,128)S(1)}, f32[8,8,256]{2,1,0:T(8,128)S(1)}) custom-call(f32[24,2,64,128]{3,2,1,0:T(8,128)S(1)} %place.3.refs_0_, f32[16,2,48,128]{3,2,1,0:T(8,128)S(1)} %get-tuple-element.76.q1.refs_1_, ...), custom_call_target="tpu_custom_call" | custom-call | flops 900000000 | bytes 400000000 | tf_op jit(solution)/shard_map/tangent_steps/pallas_call | solution.py:314
  50.7 1.4 %collective-permute-start.16 = (f32[16,8,256]{2,1,0:T(8,128)S(1)}, f32[16,8,256]{2,1,0:T(8,128)S(1)}, u32[]{:S(2)}, u32[]{:S(2)}) collective-permute-start(f32[16,8,256]{2,1,0:T(8,128)S(1)} %get-tuple-element.81), channel_id=1, source_target_pairs={{0,1},{1,0},{2,3},{3,2},{4,5},{5,4},{6,7},{7,6},{8,9},{9,8},{10,11... | collective-permute-start | bytes 393224 | tf_op jit(solution)/shard_map/ppermute | solution.py:607
  52.8 0.7 collective-permute-start.22
  53.5 5.6 %collective-permute-start.21 = (f32[8,32,256]{2,1,0:T(8,128)S(1)}, f32[8,32,256]{2,1,0:T(8,128)S(1)}, u32[]{:S(2)}, u32[]{:S(2)}) collective-permute-start(f32[8,32,256]{2,1,0:T(8,128)S(1)} %get-tuple-element.85.q2.own), channel_id=1, source_target_pairs={{0,2},{2,0},{4,6},{6,4},{8,10},{10,8},{12,14},{14,12},{16,18},{18,... | collective-permute-start | bytes 786440 | tf_op jit(solution)/shard_map/ppermute | solution.py:601
  60.4 2.5 %pressure_steps.6 = (f32[16,2,48,128]{3,2,1,0:T(8,128)S(1)}, f32[8,32,256]{2,1,0:T(8,128)S(1)}, f32[16,2,48,128]{3,2,1,0:T(8,128)S(1)}, f32[8,2,32,128]{3,2,1,0:T(8,128)S(1)}, f32[8,8,256]{2,1,0:T(8,128)S(1)}) custom-call(s32[3]{0:T(128)S(1)} %copy-done.6, f32[8]{0:T(128)S(1)} %copy-done.7, f32[8,32,256]{2,1,0:T(8,128)S(1)} %get-tuple-element.74.refs_2_.p2, ...), custom_call_target="tpu_custom_call" | custom-call | flops 900000000 | bytes 400000000 | tf_op jit(solution)/shard_map/pressure_steps/pallas_call | solution.py:276
  63.0 2.1 %tangent_steps.6 = (f32[16,2,48,128]{3,2,1,0:T(8,128)S(1)}, f32[8,32,256]{2,1,0:T(8,128)S(1)}, f32[16,8,256]{2,1,0:T(8,128)S(1)}, f32[8,8,256]{2,1,0:T(8,128)S(1)}) custom-call(f32[24,2,64,128]{3,2,1,0:T(8,128)S(1)} %place.4.refs_0_, f32[16,2,48,128]{3,2,1,0:T(8,128)S(1)} %get-tuple-element.86.q1.refs_1_, ...), custom_call_target="tpu_custom_call" | custom-call | flops 900000000 | bytes 400000000 | tf_op jit(solution)/shard_map/tangent_steps/pallas_call | solution.py:314
  66.5 6.5 %collective-permute-start.19 = (f32[8,32,256]{2,1,0:T(8,128)S(1)}, f32[8,32,256]{2,1,0:T(8,128)S(1)}, u32[]{:S(2)}, u32[]{:S(2)}) collective-permute-start(f32[8,32,256]{2,1,0:T(8,128)S(1)} %get-tuple-element.84.refs_2_.p2), channel_id=1, source_target_pairs={{0,2},{2,0},{4,6},{6,4},{8,10},{10,8},{12,14},{14,12},{16,18},{18,... | collective-permute-start | bytes 786440 | tf_op jit(solution)/shard_map/ppermute | solution.py:601
  73.6 0.7 collective-permute-start.27
  74.3 5.1 %collective-permute-start.26 = (f32[8,32,256]{2,1,0:T(8,128)S(1)}, f32[8,32,256]{2,1,0:T(8,128)S(1)}, u32[]{:S(2)}, u32[]{:S(2)}) collective-permute-start(f32[8,32,256]{2,1,0:T(8,128)S(1)} %get-tuple-element.95.q2.own), channel_id=1, source_target_pairs={{0,2},{2,0},{4,6},{6,4},{8,10},{10,8},{12,14},{14,12},{16,18},{18,... | collective-permute-start | bytes 786440 | tf_op jit(solution)/shard_map/ppermute | solution.py:601
  80.1 0.7 collective-permute-done.24.refs_6_.refs_1_
  80.8 2.3 %pressure_steps.7 = (f32[16,2,48,128]{3,2,1,0:T(8,128)S(1)}, f32[8,32,256]{2,1,0:T(8,128)S(1)}, f32[16,2,48,128]{3,2,1,0:T(8,128)S(1)}, f32[8,2,32,128]{3,2,1,0:T(8,128)S(1)}) custom-call(s32[3]{0:T(128)S(1)} %copy-done.6, f32[8]{0:T(128)S(1)} %copy-done.7, f32[8,32,256]{2,1,0:T(8,128)S(1)} %get-tuple-element.84.refs_2_.p2, ...), custom_call_target="tpu_custom_call" | custom-call | flops 900000000 | bytes 400000000 | tf_op jit(solution)/shard_map/pressure_steps/pallas_call | solution.py:276
  83.1 1.2 %receive.8 = (f32[2,128]{1,0:T(2,128)S(1)}, f32[2,128]{1,0:T(2,128)}) custom-call(s32[1,128]{1,0:T(1,128)S(1)} %bitcast.6, f32[16,2,48,128]{3,2,1,0:T(8,128)S(1)} %get-tuple-element.103.p1.q1, f32[8,32,256]{2,1,0:T(8,128)S(1)} %get-tuple-element.94.p_in.p2.q2, f32[16,2,48,128]{3,2,1,0:T(8,128)S(1)} %get-tuple-element.103.p1.q1, ...), custom_call_target="tpu_custom_call" | custom-call | flops 20000000 | bytes 2500000 | tf_op jit(solution)/shard_map/receive/pallas_call | solution.py:489
  84.4 2.1 %tangent_steps.7 = (f32[16,2,48,128]{3,2,1,0:T(8,128)S(1)}, f32[8,32,256]{2,1,0:T(8,128)S(1)}) custom-call(f32[24,2,64,128]{3,2,1,0:T(8,128)S(1)} %place.5.refs_0_, f32[16,2,48,128]{3,2,1,0:T(8,128)S(1)} %get-tuple-element.96.q1.refs_1_, f32[16,2,48,128]{3,2,1,0:T(8,128)S(1)} %get-tuple-element.66.refs_9_.refs_0_.refs_2_, ...), custom_call_target="tpu_custom_call" | custom-call | flops 900000000 | bytes 400000000 | tf_op jit(solution)/shard_map/tangent_steps/pallas_call | solution.py:314
  86.5 1.2 %receive.9 = (f32[8,128]{1,0:T(8,128)S(1)}, f32[8,128]{1,0:T(8,128)S(1)}, f32[32,1,128]{2,1,0:T(1,128)}) custom-call(s32[1,128]{1,0:T(1,128)S(1)} %bitcast.7, f32[2,128]{1,0:T(2,128)S(1)} %get-tuple-element.104.p1.p2, f32[2,128]{1,0:T(2,128)S(1)} %get-tuple-element.104.p1.p2, f32[16,2,48,128]{3,2,1,0:T(8,128)S(1)} %get-tuple-element.105.q1, ...), custom_call_target="tpu_custom_call" | custom-call | flops 20000000 | bytes 2500000 | tf_op jit(solution)/shard_map/receive/pallas_call | solution.py:489
  87.7 6.3 %all-to-all-start = ((f32[32,1,128]{2,1,0:T(1,128)}), f32[32,1,128]{2,1,0:T(1,128)S(1)}, u32[]{:S(2)}, u32[]{:S(2)}) async-start(f32[32,1,128]{2,1,0:T(1,128)} %get-tuple-element.110), calls=%async_computation | async-start | bytes 32768 | tf_op jit(solution)/shard_map/all_to_all | solution.py:663
  94.0 0.9 smooth.1
  94.8 6.2 %all-to-all-done.sums = f32[32,1,128]{2,1,0:T(1,128)S(1)} async-done(((f32[32,1,128]{2,1,0:T(1,128)}), f32[32,1,128]{2,1,0:T(1,128)S(1)}, u32[]{:S(2)}, u32[]{:S(2)}) %all-to-all-start) | async-done | bytes 16416 | tf_op jit(solution)/shard_map/all_to_all | solution.py:663
  101.1 0.9 finish.1
  (64 shorter events, 11.6 us)
Async XLA Ops:
  0.6 16.9 %copy-start.4 = (f32[8,32,256]{2,1,0:T(8,128)S(1)}, f32[8,32,256]{2,1,0:T(8,128)}, u32[]{:S(2)}) copy-start(f32[8,32,256]{2,1,0:T(8,128)} %refs_2_.1) | copy-start | bytes 786436
  0.6 16.9 %copy-start.7 = (f32[8]{0:T(128)S(1)}, f32[8]{0:T(128)}, u32[]{:S(2)}) copy-start(f32[8]{0:T(128)} %refs_1_.7) | copy-start | bytes 100
  0.7 16.9 %copy-start.6 = (s32[3]{0:T(128)S(1)}, s32[3]{0:T(128)}, u32[]{:S(2)}) copy-start(s32[3]{0:T(128)} %refs_0_.7) | copy-start | bytes 40
  3.1 9.5 %collective-permute-start.2 = (f32[32,8,256]{2,1,0:T(8,128)}, f32[32,8,256]{2,1,0:T(8,128)S(1)}, u32[]{:S(2)}, u32[]{:S(2)}) collective-permute-start(f32[32,8,256]{2,1,0:T(8,128)} %get-tuple-element.62), channel_id=1, source_target_pairs={{0,1},{1,0},{2,3},{3,2},{4,5},{5,4},{6,7},{7,6},{8,9},{9,8},{10,11... | collective-permute-start | bytes 786440 | tf_op jit(solution)/shard_map/ppermute | solution.py:607
  6.1 7.7 %collective-permute-start = (f32[12,32,256]{2,1,0:T(8,128)}, f32[12,32,256]{2,1,0:T(8,128)S(1)}, u32[]{:S(2)}, u32[]{:S(2)}) collective-permute-start(f32[12,32,256]{2,1,0:T(8,128)} %get-tuple-element.60), channel_id=1, source_target_pairs={{0,2},{2,0},{4,6},{6,4},{8,10},{10,8},{12,14},{14,12},{16,18},{18,... | collective-permute-start | bytes 1179656 | tf_op jit(solution)/shard_map/ppermute | solution.py:601
  6.1 7.7 %collective-permute-start.1 = (f32[12,32,256]{2,1,0:T(8,128)}, f32[12,32,256]{2,1,0:T(8,128)S(1)}, u32[]{:S(2)}, u32[]{:S(2)}) collective-permute-start(f32[12,32,256]{2,1,0:T(8,128)} %get-tuple-element.61), channel_id=1, source_target_pairs={{2,4},{4,2},{6,8},{8,6},{10,12},{12,10},{14,16},{16,14},{18,20},{2... | collective-permute-start | bytes 1179656 | tf_op jit(solution)/shard_map/ppermute | solution.py:604
  6.7 6.3 %collective-permute-start.4 = (f32[8,8,256]{2,1,0:T(8,128)}, f32[8,8,256]{2,1,0:T(8,128)S(1)}, u32[]{:S(2)}, u32[]{:S(2)}) collective-permute-start(f32[8,8,256]{2,1,0:T(8,128)} %get-tuple-element.63), channel_id=1, source_target_pairs={{2,5},{3,4},{4,3},{5,2},{6,9},{7,8},{8,7},{9,6},{10,13},{11,12},{1... | collective-permute-start | bytes 196616 | tf_op jit(solution)/shard_map/ppermute | solution.py:609
  12.6 1.9 %collective-permute-start.3 = (f32[32,8,256]{2,1,0:T(8,128)S(1)}, f32[32,8,256]{2,1,0:T(8,128)S(1)}, u32[]{:S(2)}, u32[]{:S(2)}) collective-permute-start(f32[32,8,256]{2,1,0:T(8,128)S(1)} %collective-permute-done.2.refs_0_.refs_5_), channel_id=1, source_target_pairs={{0,2},{2,0},{4,6},{6,4},{8,10},{10,8},{12,14},{14,12},{16,18},{18,... | collective-permute-start | bytes 786440 | tf_op jit(solution)/shard_map/ppermute | solution.py:601
  12.6 4.9 %collective-permute-start.5 = (f32[8,32,256]{2,1,0:T(8,128)}, f32[8,32,256]{2,1,0:T(8,128)S(1)}, u32[]{:S(2)}, u32[]{:S(2)}) collective-permute-start(f32[8,32,256]{2,1,0:T(8,128)} %refs_2_.1), channel_id=1, source_target_pairs={{0,2},{2,0},{4,6},{6,4},{8,10},{10,8},{12,14},{14,12},{16,18},{18,... | collective-permute-start | bytes 786440 | tf_op jit(solution)/shard_map/ppermute | solution.py:601
  13.1 4.4 %collective-permute-start.6 = (f32[8,32,256]{2,1,0:T(8,128)}, f32[8,32,256]{2,1,0:T(8,128)S(1)}, u32[]{:S(2)}, u32[]{:S(2)}) collective-permute-start(f32[8,32,256]{2,1,0:T(8,128)} %refs_2_.1), channel_id=1, source_target_pairs={{2,4},{4,2},{6,8},{8,6},{10,12},{12,10},{14,16},{16,14},{18,20},{2... | collective-permute-start | bytes 786440 | tf_op jit(solution)/shard_map/ppermute | solution.py:604
  19.8 21.3 %collective-permute-start.8 = (f32[8,32,256]{2,1,0:T(8,128)S(1)}, f32[8,32,256]{2,1,0:T(8,128)S(1)}, u32[]{:S(2)}, u32[]{:S(2)}) collective-permute-start(f32[8,32,256]{2,1,0:T(8,128)S(1)} %get-tuple-element.67.refs_2_.p2), channel_id=1, source_target_pairs={{2,4},{4,2},{6,8},{8,6},{10,12},{12,10},{14,16},{16,14},{18,20},{2... | collective-permute-start | bytes 786440 | tf_op jit(solution)/shard_map/ppermute | solution.py:604
  20.5 20.6 %collective-permute-start.7 = (f32[8,32,256]{2,1,0:T(8,128)S(1)}, f32[8,32,256]{2,1,0:T(8,128)S(1)}, u32[]{:S(2)}, u32[]{:S(2)}) collective-permute-start(f32[8,32,256]{2,1,0:T(8,128)S(1)} %get-tuple-element.67.refs_2_.p2), channel_id=1, source_target_pairs={{0,2},{2,0},{4,6},{6,4},{8,10},{10,8},{12,14},{14,12},{16,18},{18,... | collective-permute-start | bytes 786440 | tf_op jit(solution)/shard_map/ppermute | solution.py:601
  30.6 9.7 %collective-permute-start.9 = (f32[16,8,256]{2,1,0:T(8,128)S(1)}, f32[16,8,256]{2,1,0:T(8,128)S(1)}, u32[]{:S(2)}, u32[]{:S(2)}) collective-permute-start(f32[16,8,256]{2,1,0:T(8,128)S(1)} %get-tuple-element.71), channel_id=1, source_target_pairs={{0,1},{1,0},{2,3},{3,2},{4,5},{5,4},{6,7},{7,6},{8,9},{9,8},{10,11... | collective-permute-start | bytes 393224 | tf_op jit(solution)/shard_map/ppermute | solution.py:607
  31.2 1.3 %collective-permute-start.11 = (f32[8,8,256]{2,1,0:T(8,128)S(1)}, f32[8,8,256]{2,1,0:T(8,128)S(1)}, u32[]{:S(2)}, u32[]{:S(2)}) collective-permute-start(f32[8,8,256]{2,1,0:T(8,128)S(1)} %get-tuple-element.72), channel_id=1, source_target_pairs={{2,5},{3,4},{4,3},{5,2},{6,9},{7,8},{8,7},{9,6},{10,13},{11,12},{1... | collective-permute-start | bytes 196616 | tf_op jit(solution)/shard_map/ppermute | solution.py:609
  31.9 16.6 %collective-permute-start.15 = (f32[8,32,256]{2,1,0:T(8,128)S(1)}, f32[8,32,256]{2,1,0:T(8,128)S(1)}, u32[]{:S(2)}, u32[]{:S(2)}) collective-permute-start(f32[8,32,256]{2,1,0:T(8,128)S(1)} %get-tuple-element.75.q2.own), channel_id=1, source_target_pairs={{2,4},{4,2},{6,8},{8,6},{10,12},{12,10},{14,16},{16,14},{18,20},{2... | collective-permute-start | bytes 786440 | tf_op jit(solution)/shard_map/ppermute | solution.py:604
  32.6 15.9 %collective-permute-start.14 = (f32[8,32,256]{2,1,0:T(8,128)S(1)}, f32[8,32,256]{2,1,0:T(8,128)S(1)}, u32[]{:S(2)}, u32[]{:S(2)}) collective-permute-start(f32[8,32,256]{2,1,0:T(8,128)S(1)} %get-tuple-element.75.q2.own), channel_id=1, source_target_pairs={{0,2},{2,0},{4,6},{6,4},{8,10},{10,8},{12,14},{14,12},{16,18},{18,... | collective-permute-start | bytes 786440 | tf_op jit(solution)/shard_map/ppermute | solution.py:601
  40.3 1.3 %collective-permute-start.10 = (f32[16,8,256]{2,1,0:T(8,128)S(1)}, f32[16,8,256]{2,1,0:T(8,128)S(1)}, u32[]{:S(2)}, u32[]{:S(2)}) collective-permute-start(f32[16,8,256]{2,1,0:T(8,128)S(1)} %collective-permute-done.9.refs_5_.refs_0_), channel_id=1, source_target_pairs={{0,2},{2,0},{4,6},{6,4},{8,10},{10,8},{12,14},{14,12},{16,18},{18,... | collective-permute-start | bytes 393224 | tf_op jit(solution)/shard_map/ppermute | solution.py:601
  44.0 15.8 %collective-permute-start.13 = (f32[8,32,256]{2,1,0:T(8,128)S(1)}, f32[8,32,256]{2,1,0:T(8,128)S(1)}, u32[]{:S(2)}, u32[]{:S(2)}) collective-permute-start(f32[8,32,256]{2,1,0:T(8,128)S(1)} %get-tuple-element.74.refs_2_.p2), channel_id=1, source_target_pairs={{2,4},{4,2},{6,8},{8,6},{10,12},{12,10},{14,16},{16,14},{18,20},{2... | collective-permute-start | bytes 786440 | tf_op jit(solution)/shard_map/ppermute | solution.py:604
  44.7 15.2 %collective-permute-start.12 = (f32[8,32,256]{2,1,0:T(8,128)S(1)}, f32[8,32,256]{2,1,0:T(8,128)S(1)}, u32[]{:S(2)}, u32[]{:S(2)}) collective-permute-start(f32[8,32,256]{2,1,0:T(8,128)S(1)} %get-tuple-element.74.refs_2_.p2), channel_id=1, source_target_pairs={{0,2},{2,0},{4,6},{6,4},{8,10},{10,8},{12,14},{14,12},{16,18},{18,... | collective-permute-start | bytes 786440 | tf_op jit(solution)/shard_map/ppermute | solution.py:601
  50.7 8.3 %collective-permute-start.16 = (f32[16,8,256]{2,1,0:T(8,128)S(1)}, f32[16,8,256]{2,1,0:T(8,128)S(1)}, u32[]{:S(2)}, u32[]{:S(2)}) collective-permute-start(f32[16,8,256]{2,1,0:T(8,128)S(1)} %get-tuple-element.81), channel_id=1, source_target_pairs={{0,1},{1,0},{2,3},{3,2},{4,5},{5,4},{6,7},{7,6},{8,9},{9,8},{10,11... | collective-permute-start | bytes 393224 | tf_op jit(solution)/shard_map/ppermute | solution.py:607
  52.1 1.3 %collective-permute-start.18 = (f32[8,8,256]{2,1,0:T(8,128)S(1)}, f32[8,8,256]{2,1,0:T(8,128)S(1)}, u32[]{:S(2)}, u32[]{:S(2)}) collective-permute-start(f32[8,8,256]{2,1,0:T(8,128)S(1)} %get-tuple-element.82), channel_id=1, source_target_pairs={{2,5},{3,4},{4,3},{5,2},{6,9},{7,8},{8,7},{9,6},{10,13},{11,12},{1... | collective-permute-start | bytes 196616 | tf_op jit(solution)/shard_map/ppermute | solution.py:609
  52.8 10.2 %collective-permute-start.22 = (f32[8,32,256]{2,1,0:T(8,128)S(1)}, f32[8,32,256]{2,1,0:T(8,128)S(1)}, u32[]{:S(2)}, u32[]{:S(2)}) collective-permute-start(f32[8,32,256]{2,1,0:T(8,128)S(1)} %get-tuple-element.85.q2.own), channel_id=1, source_target_pairs={{2,4},{4,2},{6,8},{8,6},{10,12},{12,10},{14,16},{16,14},{18,20},{2... | collective-permute-start | bytes 786440 | tf_op jit(solution)/shard_map/ppermute | solution.py:604
  53.5 9.5 %collective-permute-start.21 = (f32[8,32,256]{2,1,0:T(8,128)S(1)}, f32[8,32,256]{2,1,0:T(8,128)S(1)}, u32[]{:S(2)}, u32[]{:S(2)}) collective-permute-start(f32[8,32,256]{2,1,0:T(8,128)S(1)} %get-tuple-element.85.q2.own), channel_id=1, source_target_pairs={{0,2},{2,0},{4,6},{6,4},{8,10},{10,8},{12,14},{14,12},{16,18},{18,... | collective-permute-start | bytes 786440 | tf_op jit(solution)/shard_map/ppermute | solution.py:601
  59.1 1.3 %collective-permute-start.17 = (f32[16,8,256]{2,1,0:T(8,128)S(1)}, f32[16,8,256]{2,1,0:T(8,128)S(1)}, u32[]{:S(2)}, u32[]{:S(2)}) collective-permute-start(f32[16,8,256]{2,1,0:T(8,128)S(1)} %collective-permute-done.16.refs_5_.refs_0_), channel_id=1, source_target_pairs={{0,2},{2,0},{4,6},{6,4},{8,10},{10,8},{12,14},{14,12},{16,18},{18,... | collective-permute-start | bytes 393224 | tf_op jit(solution)/shard_map/ppermute | solution.py:601
  65.2 14.3 %collective-permute-start.23 = (f32[16,8,256]{2,1,0:T(8,128)S(1)}, f32[16,8,256]{2,1,0:T(8,128)S(1)}, u32[]{:S(2)}, u32[]{:S(2)}) collective-permute-start(f32[16,8,256]{2,1,0:T(8,128)S(1)} %get-tuple-element.91), channel_id=1, source_target_pairs={{0,1},{1,0},{2,3},{3,2},{4,5},{5,4},{6,7},{7,6},{8,9},{9,8},{10,11... | collective-permute-start | bytes 393224 | tf_op jit(solution)/shard_map/ppermute | solution.py:607
  65.8 15.0 %collective-permute-start.20 = (f32[8,32,256]{2,1,0:T(8,128)S(1)}, f32[8,32,256]{2,1,0:T(8,128)S(1)}, u32[]{:S(2)}, u32[]{:S(2)}) collective-permute-start(f32[8,32,256]{2,1,0:T(8,128)S(1)} %get-tuple-element.84.refs_2_.p2), channel_id=1, source_target_pairs={{2,4},{4,2},{6,8},{8,6},{10,12},{12,10},{14,16},{16,14},{18,20},{2... | collective-permute-start | bytes 786440 | tf_op jit(solution)/shard_map/ppermute | solution.py:604
  66.5 14.3 %collective-permute-start.19 = (f32[8,32,256]{2,1,0:T(8,128)S(1)}, f32[8,32,256]{2,1,0:T(8,128)S(1)}, u32[]{:S(2)}, u32[]{:S(2)}) collective-permute-start(f32[8,32,256]{2,1,0:T(8,128)S(1)} %get-tuple-element.84.refs_2_.p2), channel_id=1, source_target_pairs={{0,2},{2,0},{4,6},{6,4},{8,10},{10,8},{12,14},{14,12},{16,18},{18,... | collective-permute-start | bytes 786440 | tf_op jit(solution)/shard_map/ppermute | solution.py:601
  72.9 1.3 %collective-permute-start.25 = (f32[8,8,256]{2,1,0:T(8,128)S(1)}, f32[8,8,256]{2,1,0:T(8,128)S(1)}, u32[]{:S(2)}, u32[]{:S(2)}) collective-permute-start(f32[8,8,256]{2,1,0:T(8,128)S(1)} %get-tuple-element.92), channel_id=1, source_target_pairs={{2,5},{3,4},{4,3},{5,2},{6,9},{7,8},{8,7},{9,6},{10,13},{11,12},{1... | collective-permute-start | bytes 196616 | tf_op jit(solution)/shard_map/ppermute | solution.py:609
  73.6 10.7 %collective-permute-start.27 = (f32[8,32,256]{2,1,0:T(8,128)S(1)}, f32[8,32,256]{2,1,0:T(8,128)S(1)}, u32[]{:S(2)}, u32[]{:S(2)}) collective-permute-start(f32[8,32,256]{2,1,0:T(8,128)S(1)} %get-tuple-element.95.q2.own), channel_id=1, source_target_pairs={{2,4},{4,2},{6,8},{8,6},{10,12},{12,10},{14,16},{16,14},{18,20},{2... | collective-permute-start | bytes 786440 | tf_op jit(solution)/shard_map/ppermute | solution.py:604
  74.3 10.0 %collective-permute-start.26 = (f32[8,32,256]{2,1,0:T(8,128)S(1)}, f32[8,32,256]{2,1,0:T(8,128)S(1)}, u32[]{:S(2)}, u32[]{:S(2)}) collective-permute-start(f32[8,32,256]{2,1,0:T(8,128)S(1)} %get-tuple-element.95.q2.own), channel_id=1, source_target_pairs={{0,2},{2,0},{4,6},{6,4},{8,10},{10,8},{12,14},{14,12},{16,18},{18,... | collective-permute-start | bytes 786440 | tf_op jit(solution)/shard_map/ppermute | solution.py:601
  79.4 1.3 %collective-permute-start.24 = (f32[16,8,256]{2,1,0:T(8,128)S(1)}, f32[16,8,256]{2,1,0:T(8,128)S(1)}, u32[]{:S(2)}, u32[]{:S(2)}) collective-permute-start(f32[16,8,256]{2,1,0:T(8,128)S(1)} %collective-permute-done.23.refs_5_.refs_0_), channel_id=1, source_target_pairs={{0,2},{2,0},{4,6},{6,4},{8,10},{10,8},{12,14},{14,12},{16,18},{18,... | collective-permute-start | bytes 393224 | tf_op jit(solution)/shard_map/ppermute | solution.py:601
  87.7 13.4 %all-to-all-start = ((f32[32,1,128]{2,1,0:T(1,128)}), f32[32,1,128]{2,1,0:T(1,128)S(1)}, u32[]{:S(2)}, u32[]{:S(2)}) async-start(f32[32,1,128]{2,1,0:T(1,128)} %get-tuple-element.110), calls=%async_computation | async-start | bytes 32768 | tf_op jit(solution)/shard_map/all_to_all | solution.py:663
  (6 other events, 38.3 us)
